TPU v7x, 32 devices: a whole 2x2x4 slice. The times are simulated.
32 devices in a mesh: rep: 4 (over x, core), shard: 8 (over z, y).
Axes of the slice: x: 2, y: 2, z: 4, core: 2. Of those that a mesh axis runs over, the one named last changes fastest.
Arguments:
- tokens: bfloat16 [32768, 1024], P(('rep', 'shard')), may hold values from -6 to 6
- w_query: bfloat16 [1024, 1024], P('shard'), may hold values from -0.1875 to 0.1875
- w_key: bfloat16 [1024, 1024], P('shard'), may hold values from -0.1875 to 0.1875
- w_value: bfloat16 [1024, 1024], P('shard'), may hold values from -0.1875 to 0.1875
- b_query: bfloat16 [1024], P('shard'), may hold values from -3 to 3
- b_value: bfloat16 [1024], P('shard'), may hold values from -3 to 3
- w_out: bfloat16 [1024, 1024], P('shard'), may hold values from -3 to 3
- b_out: bfloat16 [1024], P('shard'), may hold values from -3 to 3
- gain_one: bfloat16 [1024], P('shard'), may hold values from 0.5 to 1.5
- shift_one: bfloat16 [1024], P('shard'), may hold values from -3 to 3
- w_inner: bfloat16 [1024, 4096], P('shard'), may hold values from -0.1875 to 0.1875
- b_inner: bfloat16 [4096], P('shard'), may hold values from -3 to 3
- w_outer: bfloat16 [4096, 1024], P('shard'), may hold values from -0.09375 to 0.09375
- b_outer: bfloat16 [1024], P('shard'), may hold values from -3 to 3
- gain_two: bfloat16 [1024], P('shard'), may hold values from 0.5 to 1.5
- shift_two: bfloat16 [1024], P('shard'), may hold values from -3 to 3
- cotangent: bfloat16 [32768, 1024], P(('rep', 'shard')), may hold values from -6 to 6
Outputs:
- output: bfloat16 [32768, 1024], P(('rep', 'shard'))
- d_tokens: bfloat16 [32768, 1024], P(('rep', 'shard'))
- grad_w_query: float32 [1024, 1024], P('shard')
- grad_w_key: float32 [1024, 1024], P('shard')
- grad_w_value: float32 [1024, 1024], P('shard')
- grad_b_query: float32 [1024], P('shard')
- grad_b_value: float32 [1024], P('shard')
- grad_w_out: float32 [1024, 1024], P('shard')
- grad_b_out: float32 [1024], P('shard')
- grad_gain_one: float32 [1024], P('shard')
- grad_shift_one: float32 [1024], P('shard')
- grad_w_inner: float32 [1024, 4096], P('shard')
- grad_b_inner: float32 [4096], P('shard')
- grad_w_outer: float32 [4096, 1024], P('shard')
- grad_b_outer: float32 [1024], P('shard')
- grad_gain_two: float32 [1024], P('shard')
- grad_shift_two: float32 [1024], P('shard')
All inputs are finite; a program needn't handle non-finite values.
Results may differ from a plain program's by a relative error of at most 0.017.
Values may be sent and summed in bfloat16 or wider, within the bound.
No kernel may reach another device: no remote copies, remote signals or barrier semaphores. Data moves between devices by JAX's collectives and lax.ppermute only.
A program may use at most 192 MiB of HBM per device.

v0:
```python
import functools

import jax
import jax.numpy as jnp
from jax import lax
from jax.experimental import pallas as pl
from jax.experimental.pallas import tpu as pltpu
from jax.sharding import PartitionSpec as P

D = 1024
H = 16
DH = 64
SEQ = 512
LANES = 128
GROUPS = 2
PAIRS = D // LANES // GROUPS
WIDE = D // GROUPS
AXES = ("cross", "core", "shard")
RING_MOST = 16
LOW = jnp.bfloat16
FULL = jnp.float32


def project(left, right):
    return jnp.dot(left, right, preferred_element_type=FULL)


def gram(left, right):
    return lax.dot_general(left, right, (((0,), (0,)), ((), ())), preferred_element_type=FULL)


def against(left, right):
    return lax.dot_general(left, right, (((1,), (1,)), ((), ())), preferred_element_type=FULL)


def normal(values):
    centre = values - jnp.mean(values, axis=-1, keepdims=True)
    spread = jnp.mean(centre * centre, axis=-1, keepdims=True)
    inverse = lax.rsqrt(spread + 1e-12)
    return centre * inverse, inverse


def normal_back(scaled, unit, inverse):
    mean = jnp.mean(scaled, axis=-1, keepdims=True)
    along = jnp.mean(scaled * unit, axis=-1, keepdims=True)
    return (scaled - mean - unit * along) * inverse


def head_mask(head):
    lane = lax.broadcasted_iota(jnp.int32, (SEQ, LANES), 1)
    return (lane // DH) == head


def attend_kernel(query_ref, key_ref, value_ref, *rest):
    out_ref, lse_ref = rest[-2:]
    query = query_ref[...] * LOW(0.125)
    key = key_ref[...]
    value_t = value_ref[...].T
    parts = []
    for head in range(LANES // DH):
        own = jnp.where(head_mask(head), query, jnp.zeros_like(query))
        scores = against(key, own)
        top = jnp.max(scores, axis=0, keepdims=True)
        expo = jnp.exp(scores - top)
        total = jnp.sum(expo, axis=0, keepdims=True)
        mixed = project(value_t[head * DH : (head + 1) * DH], expo.astype(LOW))
        parts.append(mixed * (1.0 / total))
        lse_ref[0, head : head + 1, :] = top + jnp.log(total)
    out_ref[...] = jnp.concatenate(parts, axis=0).T.astype(LOW)


def attend_back_kernel(query_ref, key_ref, value_ref, d_ref, lse_ref, out_ref, sum_ref):
    seq, pair = pl.program_id(0), pl.program_id(1)
    query = query_ref[...] * LOW(0.125)
    key = key_ref[...]
    value = value_ref[...]
    d_out = d_ref[...]
    key_t = key.T
    d_key = None
    d_value = None
    d_query = []
    for head in range(LANES // DH):
        mask = head_mask(head)
        own = jnp.where(mask, query, jnp.zeros_like(query))
        d_own = jnp.where(mask, d_out, jnp.zeros_like(d_out))
        probs = jnp.exp(against(key, own) - lse_ref[0, head : head + 1, :])
        d_probs = against(value, d_own)
        inner = jnp.sum(probs * d_probs, axis=0, keepdims=True)
        d_scores = (probs * (d_probs - inner)).astype(LOW)
        part_value = project(probs.astype(LOW), d_own)
        part_key = project(d_scores, own)
        d_value = part_value if d_value is None else d_value + part_value
        d_key = part_key if d_key is None else d_key + part_key
        d_query.append(project(key_t[head * DH : (head + 1) * DH], d_scores))
    d_query = jnp.concatenate(d_query, axis=0).T * 0.125
    for place, grad in enumerate((d_query, d_key, d_value)):
        start = pl.multiple_of(place * WIDE + pair * LANES, LANES)
        out_ref[:, pl.ds(start, LANES)] = grad.astype(LOW)
        total = jnp.sum(grad, axis=0, keepdims=True)
        before = sum_ref[0:1, pl.ds(start, LANES)]
        sum_ref[0:1, pl.ds(start, LANES)] = jnp.where(seq == 0, total, before + total)


def column_block(first):
    return pl.BlockSpec((SEQ, LANES), lambda seq, pair: (seq, first + pair))


LSE_BLOCK = pl.BlockSpec((1, LANES // DH, SEQ), lambda seq, pair: (seq * PAIRS + pair, 0, 0))


def triple():
    return [column_block(place * PAIRS) for place in range(3)]


def attend(qkv, group, before):
    count = qkv.shape[0]
    seqs = count // SEQ
    kept = [] if before is None else [before]
    return pl.pallas_call(
        attend_kernel,
        grid=(seqs, PAIRS),
        in_specs=triple() + [pl.BlockSpec(memory_space=pl.ANY)] * len(kept),
        out_specs=[column_block(group * PAIRS), LSE_BLOCK],
        out_shape=[
            jax.ShapeDtypeStruct((count, D), LOW),
            jax.ShapeDtypeStruct((seqs * PAIRS, LANES // DH, SEQ), FULL),
        ],
        input_output_aliases={3: 0} if kept else {},
        compiler_params=pltpu.CompilerParams(vmem_limit_bytes=32 * 2**20),
        name="attend",
    )(qkv, qkv, qkv, *kept)


def attend_back(qkv, d_attended, lse, group):
    count = qkv.shape[0]
    return pl.pallas_call(
        attend_back_kernel,
        grid=(count // SEQ, PAIRS),
        in_specs=triple() + [column_block(group * PAIRS), LSE_BLOCK],
        out_specs=[
            pl.BlockSpec((SEQ, 3 * WIDE), lambda seq, pair: (seq, 0)),
            pl.BlockSpec((8, 3 * WIDE), lambda seq, pair: (0, 0)),
        ],
        out_shape=[
            jax.ShapeDtypeStruct((count, 3 * WIDE), LOW),
            jax.ShapeDtypeStruct((8, 3 * WIDE), FULL),
        ],
        compiler_params=pltpu.CompilerParams(vmem_limit_bytes=40 * 2**20),
        name="attend_back",
    )(qkv, qkv, qkv, d_attended, lse)


ROWS = 256
COLUMNS = 512
EXTRA = 16
PARTS = 2
(QUERY, VALUE, OUT, GAIN_ONE, SHIFT_ONE, OUTER, GAIN_TWO, SHIFT_TWO) = range(8)


def line(ref, row):
    return ref[row : row + 1, :]


def kept(shape):
    return pl.BlockSpec(shape, lambda i: (0,) * len(shape), pipeline_mode=pl.Buffered(1))


def rows_of(width):
    return pl.BlockSpec((ROWS, width), lambda i: (i, 0))


def columns_of(height):
    return pl.BlockSpec((height, COLUMNS), lambda i: (0, i))


def add_line(ref, row, values):
    ref[row : row + 1, :] += jnp.sum(values, axis=0, keepdims=True)


def clear(ref):
    @pl.when(pl.program_id(0) == 0)
    def _():
        ref[...] = jnp.zeros_like(ref)


def pieces(rows, count=PARTS):
    step = rows // count
    return [slice(i * step, (i + 1) * step) for i in range(count)]


LIMIT = pltpu.CompilerParams(vmem_limit_bytes=48 * 2**20)


def out_kernel(attended_ref, w_ref, tokens_ref, vec_ref, unit_ref, inverse_ref, low_ref):
    for rows in pieces(ROWS):
        branch = project(attended_ref[rows, :], w_ref[...]) + line(vec_ref, OUT)
        unit, inverse = normal(tokens_ref[rows, :].astype(FULL) + branch)
        unit_ref[rows, :] = unit
        inverse_ref[rows, :] = jnp.broadcast_to(inverse, (inverse.shape[0], LANES))
        low_ref[rows, :] = (unit * line(vec_ref, GAIN_ONE) + line(vec_ref, SHIFT_ONE)).astype(LOW)


def out_norm(attended, w_out, tokens, vec):
    count = tokens.shape[0]
    return pl.pallas_call(
        out_kernel,
        grid=(count // ROWS,),
        in_specs=[rows_of(D), kept((D, D)), rows_of(D), kept((8, D))],
        out_specs=[rows_of(D), rows_of(LANES), rows_of(D)],
        out_shape=[
            jax.ShapeDtypeStruct((count, D), FULL),
            jax.ShapeDtypeStruct((count, LANES), FULL),
            jax.ShapeDtypeStruct((count, D), LOW),
        ],
        compiler_params=LIMIT,
        name="out_norm",
    )(attended, w_out, tokens, vec)


def inner_kernel(low_ref, w_ref, bias_ref, active_ref, slope_ref):
    for rows in pieces(low_ref.shape[0], 4):
        pre = project(low_ref[rows, :], w_ref[...]) + bias_ref[...]
        below = 0.5 * (1.0 + lax.erf(pre * (0.5**0.5)))
        active_ref[rows, :] = (pre * below).astype(LOW)
        slope_ref[rows, :] = (below + pre * jnp.exp(-0.5 * pre * pre) * 0.3989422804014327).astype(LOW)


def inner_gelu(low, w_inner, bias):
    count, hidden = low.shape[0], w_inner.shape[1]
    return pl.pallas_call(
        inner_kernel,
        grid=(hidden // COLUMNS,),
        in_specs=[kept((count, D)), columns_of(D), columns_of(1)],
        out_specs=[columns_of(count), columns_of(count)],
        out_shape=[jax.ShapeDtypeStruct((count, hidden), LOW)] * 2,
        compiler_params=LIMIT,
        name="inner_gelu",
    )(low, w_inner, bias)


def outer_kernel(active_ref, w_ref, unit_ref, vec_ref, cot_ref, out_ref, d_ref, d_low_ref, sum_ref):
    clear(sum_ref)
    for rows in pieces(ROWS):
        first = unit_ref[rows, :] * line(vec_ref, GAIN_ONE) + line(vec_ref, SHIFT_ONE)
        second = first + project(active_ref[rows, :], w_ref[...]) + line(vec_ref, OUTER)
        unit, inverse = normal(second)
        out_ref[rows, :] = (unit * line(vec_ref, GAIN_TWO) + line(vec_ref, SHIFT_TWO)).astype(LOW)
        cot = cot_ref[rows, :].astype(FULL)
        d_second = normal_back(cot * line(vec_ref, GAIN_TWO), unit, inverse)
        d_ref[rows, :] = d_second
        d_low_ref[rows, :] = d_second.astype(LOW)
        add_line(sum_ref, 0, cot * unit)
        add_line(sum_ref, 1, cot)
        add_line(sum_ref, 2, d_second)


def outer_norms(active, w_outer, unit, vec, cotangent):
    count, hidden = active.shape
    return pl.pallas_call(
        outer_kernel,
        grid=(count // ROWS,),
        in_specs=[rows_of(hidden), kept((hidden, D)), rows_of(D), kept((8, D)), rows_of(D)],
        out_specs=[rows_of(D), rows_of(D), rows_of(D), kept((8, D))],
        out_shape=[
            jax.ShapeDtypeStruct((count, D), LOW),
            jax.ShapeDtypeStruct((count, D), FULL),
            jax.ShapeDtypeStruct((count, D), LOW),
            jax.ShapeDtypeStruct((8, D), FULL),
        ],
        compiler_params=LIMIT,
        name="outer_norms",
    )(active, w_outer, unit, vec, cotangent)


def outer_back_kernel(d_ref, w_ref, slope_ref, out_ref, sum_ref):
    sum_ref[...] = jnp.zeros_like(sum_ref)
    for rows in pieces(d_ref.shape[0]):
        d_pre = against(d_ref[rows, :], w_ref[...]) * slope_ref[rows, :].astype(FULL)
        out_ref[rows, :] = d_pre.astype(LOW)
        add_line(sum_ref, 0, d_pre)


def outer_back(d_mid, w_outer, slope):
    count, hidden = slope.shape
    return pl.pallas_call(
        outer_back_kernel,
        grid=(hidden // COLUMNS,),
        in_specs=[kept((count, D)), pl.BlockSpec((COLUMNS, D), lambda i: (i, 0)), columns_of(count)],
        out_specs=[columns_of(count), columns_of(1)],
        out_shape=[
            jax.ShapeDtypeStruct((count, hidden), LOW),
            jax.ShapeDtypeStruct((1, hidden), FULL),
        ],
        compiler_params=LIMIT,
        name="outer_back",
    )(d_mid, w_outer, slope)


def inner_back_kernel(
    d_pre_ref, w_ref, d_ref, unit_ref, inverse_ref, vec_ref, w_out_ref, before_ref, *refs
):
    out_ref, low_ref, attended_ref, sum_ref, total_ref = refs[-5:]
    step = pl.program_id(0)
    part = against(d_pre_ref[...], w_ref[...])

    @pl.when(step == 0)
    def _():
        total_ref[...] = d_ref[...] + part

    @pl.when(step > 0)
    def _():
        total_ref[...] += part

    @pl.when(step == pl.num_programs(0) - 1)
    def _():
        sum_ref[...] = before_ref[...]
        for rows in pieces(total_ref.shape[0], 2):
            d_first = total_ref[rows, :]
            unit = unit_ref[rows, :]
            d_inner = normal_back(d_first * line(vec_ref, GAIN_ONE), unit, inverse_ref[rows, 0:1])
            low = d_inner.astype(LOW)
            out_ref[rows, :] = d_inner
            low_ref[rows, :] = low
            attended_ref[rows, :] = against(low, w_out_ref[...]).astype(LOW)
            add_line(sum_ref, 0, d_first * unit)
            add_line(sum_ref, 1, d_first)
            add_line(sum_ref, 2, d_inner)


def inner_back(part, d_pre, w_inner, d_second, unit, inverse, vec, w_out, sums, before):
    count, hidden = d_pre.shape
    rows = count // 2

    def own(width):
        return pl.BlockSpec((rows, width), lambda i: (part, 0), pipeline_mode=pl.Buffered(1))

    return pl.pallas_call(
        inner_back_kernel,
        grid=(hidden // COLUMNS,),
        in_specs=[
            pl.BlockSpec((rows, COLUMNS), lambda i: (part, i)),
            columns_of(D),
            own(D),
            own(D),
            own(LANES),
            kept((8, D)),
            kept((D, D)),
            kept((8, D)),
        ]
        + [pl.BlockSpec(memory_space=pl.ANY)] * len(before),
        out_specs=[own(D), own(D), own(D), kept((8, D))],
        out_shape=[
            jax.ShapeDtypeStruct((count, D), FULL),
            jax.ShapeDtypeStruct((count, D), LOW),
            jax.ShapeDtypeStruct((count, D), LOW),
            jax.ShapeDtypeStruct((8, D), FULL),
        ],
        input_output_aliases={8 + i: i for i in range(len(before))},
        scratch_shapes=[pltpu.VMEM((rows, D), FULL)],
        compiler_params=LIMIT,
        name="inner_back",
    )(d_pre, w_inner, d_second, unit, inverse, vec, w_out, sums, *before)


def tokens_kernel(base_ref, d_ref, w_ref, out_ref):
    out_ref[...] = (base_ref[...] + against(d_ref[...], w_ref[...])).astype(out_ref.dtype)


def tokens_back(base, d_group, w_group, kind):
    count, wide = d_group.shape
    rows = count // 2
    return pl.pallas_call(
        tokens_kernel,
        grid=(2,),
        in_specs=[
            pl.BlockSpec((rows, D), lambda i: (i, 0)),
            pl.BlockSpec((rows, wide), lambda i: (i, 0)),
            kept((D, wide)),
        ],
        out_specs=pl.BlockSpec((rows, D), lambda i: (i, 0)),
        out_shape=jax.ShapeDtypeStruct((count, D), kind),
        compiler_params=LIMIT,
        name="tokens_back",
    )(base, d_group, w_group)


def turn_kernel(ref, out_ref):
    out_ref[...] = ref[...].T


def turn(values):
    count, width = values.shape
    return pl.pallas_call(
        turn_kernel,
        grid=(count // ROWS,),
        in_specs=[rows_of(width)],
        out_specs=pl.BlockSpec((width, ROWS), lambda i: (0, i)),
        out_shape=jax.ShapeDtypeStruct((width, count), values.dtype),
        name="turn",
    )(values)


def product_kernel(left_ref, right_ref, out_ref):
    out_ref[...] = project(left_ref[...], right_ref[...]).astype(LOW)


def product_extra_kernel(size, left_ref, right_ref, small_ref, out_ref):
    found = project(left_ref[...], right_ref[...]).astype(LOW)
    body = found.shape[0] // size // 2
    for shard in range(size):
        extra = jnp.broadcast_to(small_ref[shard : shard + 1, :], (EXTRA, found.shape[1])).astype(LOW)
        for core in range(2):
            half = 2 * shard + core
            at = half * (body + EXTRA)
            out_ref[at : at + body, :] = found[half * body : (half + 1) * body]
            out_ref[at + body : at + body + EXTRA, :] = extra


def product(left, right, small=None, size=1):
    height, depth = left.shape
    rows = height if small is None else height + 2 * EXTRA * size
    return pl.pallas_call(
        product_kernel if small is None else functools.partial(product_extra_kernel, size),
        grid=(right.shape[1] // COLUMNS,),
        in_specs=[kept((height, depth)), columns_of(depth)] + ([] if small is None else [columns_of(size)]),
        out_specs=columns_of(rows),
        out_shape=jax.ShapeDtypeStruct((rows, right.shape[1]), LOW),
        compiler_params=LIMIT,
        name="product",
    )(left, right, *([] if small is None else [small]))


def assemble_kernel(moves, align, place_ref, *refs):
    out_ref, sems = refs[-2], refs[-1]
    copies = []
    for i, (which, start, rows) in enumerate(moves):
        place = pl.multiple_of(place_ref[i], align)
        source = refs[which].at[pl.ds(start, rows)]
        copies.append(pltpu.make_async_copy(source, out_ref.at[pl.ds(place, rows)], sems.at[i]))
    for copy in copies:
        copy.start()
    for copy in copies:
        copy.wait()


def assemble(arrays, moves, places, rows):
    align = min(move[2] for move in moves)
    return pl.pallas_call(
        functools.partial(assemble_kernel, moves, align),
        in_specs=[pl.BlockSpec(memory_space=pltpu.SMEM)] + [pl.BlockSpec(memory_space=pl.ANY)] * len(arrays),
        out_specs=pl.BlockSpec(memory_space=pltpu.VMEM),
        out_shape=jax.ShapeDtypeStruct((rows,) + arrays[0].shape[1:], arrays[0].dtype),
        scratch_shapes=[pltpu.SemaphoreType.DMA((len(moves),))],
        compiler_params=pltpu.CompilerParams(vmem_limit_bytes=24 * 2**20),
        name="assemble",
    )(jnp.stack(places).astype(jnp.int32), *arrays)


def pack_kernel(size, vectors, *refs):
    out_ref = refs[-1]
    for shard in range(size):
        at = 0
        for spans in vectors:
            lines = []
            for which, row, first, length in spans:
                lines += [(which, row, first + i) for i in range(0, length, LANES)]
            share = len(lines) // size
            for which, row, first in lines[shard * share : (shard + 1) * share]:
                out_ref[shard : shard + 1, at : at + LANES] = refs[which][row : row + 1, first : first + LANES]
                at += LANES


def pack(arrays, vectors, size):
    lengths = [sum(span[3] for span in spans) for spans in vectors]
    if any(length % (size * LANES) for length in lengths):
        whole = [
            jnp.concatenate([arrays[which][row, first : first + length] for which, row, first, length in spans])
            for spans in vectors
        ]
        return jnp.concatenate([vector.reshape(size, -1) for vector in whole], axis=1)
    return pl.pallas_call(
        functools.partial(pack_kernel, size, vectors),
        out_shape=jax.ShapeDtypeStruct((size, sum(lengths) // size), FULL),
        name="pack",
    )(*arrays)


def lay_kernel(*refs):
    row = jnp.concatenate([ref[...].astype(FULL) for ref in refs[:-1]], axis=1)
    refs[-1][...] = jnp.broadcast_to(row, refs[-1].shape).astype(LOW)


def lay(vectors):
    total = sum(vector.shape[1] for vector in vectors)
    return pl.pallas_call(
        lay_kernel,
        out_shape=jax.ShapeDtypeStruct((EXTRA, total), LOW),
        name="lay",
    )(*vectors)


def unpack_kernel(count, body, place_ref, *refs):
    vec_ref, bias_ref, group_ref = refs[count:]
    group_ref[...] = jnp.zeros_like(group_ref)
    hidden = bias_ref.shape[1] // count
    for i in range(count):
        packed = refs[i][body : body + EXTRA, :].astype(FULL)[0:1, :]
        owner = place_ref[i]
        start = pl.multiple_of(owner * LANES, LANES)
        for row in range(8):
            vec_ref[row : row + 1, pl.ds(start, LANES)] = packed[:, row * LANES : (row + 1) * LANES]
        first = pl.multiple_of(owner * hidden, LANES)
        bias_ref[:, pl.ds(first, hidden)] = packed[:, 8 * LANES : 8 * LANES + hidden]
        group = owner * LANES // WIDE
        for place, row in ((0, QUERY), (2, VALUE)):
            first = pl.multiple_of(group * 2 * WIDE + place * WIDE + start, LANES)
            group_ref[:, pl.ds(first, LANES)] = packed[:, row * LANES : (row + 1) * LANES]


def unpack(chunks, owners, body, hidden):
    count = len(chunks)
    return pl.pallas_call(
        functools.partial(unpack_kernel, count, body),
        in_specs=[pl.BlockSpec(memory_space=pltpu.SMEM)] + [pl.BlockSpec(memory_space=pltpu.VMEM)] * count,
        out_shape=[
            jax.ShapeDtypeStruct((8, D), FULL),
            jax.ShapeDtypeStruct((1, hidden), FULL),
            jax.ShapeDtypeStruct((1, 3 * D), FULL),
        ],
        compiler_params=LIMIT,
        name="unpack",
    )(jnp.stack(owners).astype(jnp.int32), *chunks)


def tie(*values):
    return lax.optimization_barrier(values)


class Links:
    def __init__(self, mesh):
        self.reps, self.size = mesh.shape["cross"] * mesh.shape["core"], mesh.shape["shard"]
        size = self.size
        self.direct = size > RING_MOST or size % 2 == 1
        self.order = list(range(0, size, 2)) + list(range(size - 1, 0, -2))
        self.far = size // 2
        self.near = size - 1 - self.far
        shard = lax.axis_index("shard")
        self.core = lax.axis_index("core")
        self.sign = 1 - 2 * self.core
        self.place = jnp.where(shard % 2 == 0, shard // 2, size - 1 - shard // 2)

    def owner(self, step):
        place = (self.place + self.sign * step + 2 * self.size) % self.size
        return jnp.where(place < self.size // 2, 2 * place, 2 * (self.size - place) - 1)

    def hop(self, values, sign):
        pairs = []
        for rep in range(self.reps):
            turn = sign if rep % 2 == 0 else -sign
            for i, shard in enumerate(self.order):
                target = self.order[(i + turn) % self.size]
                pairs.append((rep * self.size + shard, rep * self.size + target))
        return lax.ppermute(values, AXES, pairs)

    def swap(self, values, bit):
        pairs = []
        for rep in range(self.reps):
            for shard in range(self.size):
                pairs.append((rep * self.size + shard, (rep ^ bit) * self.size + shard))
        return lax.ppermute(values, AXES, pairs)

    def half_of(self, values):
        half = values.shape[0] // 2
        return lax.dynamic_slice_in_dim(values, self.core * half, half, axis=0)


    def vectors(self, packed, hidden):
        small = lax.all_gather(packed, "shard", axis=0).astype(FULL)
        width, share = D // self.size, hidden // self.size
        vec = small[:, : 8 * width].reshape(self.size, 8, width).swapaxes(0, 1).reshape(8, D)
        bias = small[:, 8 * width : 8 * width + share].reshape(1, hidden)
        none = jnp.zeros((WIDE,), FULL)
        spans = [slice(g * WIDE, (g + 1) * WIDE) for g in range(GROUPS)]
        parts = [part for span in spans for part in (vec[QUERY, span], none, vec[VALUE, span])]
        return vec, bias, jnp.concatenate(parts).reshape(1, 3 * D)

    def half_of(self, values):
        half = values.shape[0] // 2
        return lax.dynamic_slice_in_dim(values, self.core * half, half, axis=0)

    def gather(self, values, sent=None):
        if self.direct:
            return lax.all_gather(values, "shard", axis=0, tiled=True)
        rows = values.shape[0]
        body = rows // 2
        arrays = [values]
        moves = [(0, 0, rows)]
        places = [self.owner(0) * rows]
        chunks, owners = [sent], [self.owner(0)]

        def keep(chunk, mine, step):
            moves.append((len(arrays), 0, body))
            arrays.append(chunk)
            core = self.core if mine else 1 - self.core
            places.append(self.owner(step) * rows + core * body)
            if mine:
                chunks.append(chunk)
                owners.append(self.owner(step))

        ahead = back = self.half_of(values) if sent is None else sent
        for step in range(1, self.far + 2):
            flight = []
            if step > 1:
                keep(ahead, True, 1 - step)
                flight.append((self.swap(ahead, 1), step - 1))
                if step - 1 <= self.near:
                    keep(back, True, step - 1)
                    flight.append((self.swap(back, 1), 1 - step))
            if step <= self.far:
                ahead = self.hop(ahead, 1)
            if step <= self.near:
                back = self.hop(back, -1)
            ahead, back, *swapped = yield [ahead, back] + [chunk for chunk, _ in flight]
            for chunk, (_, place) in zip(swapped, flight):
                keep(chunk, False, place)
        whole = assemble(arrays, moves, places, self.size * rows)
        return whole if sent is None else (whole, chunks, owners)

    def gather_quarters(self, values):
        rows = values.shape[0] // self.reps
        index = lax.axis_index("cross") * 2 + self.core
        mine = lax.dynamic_slice_in_dim(values, index * rows, rows, axis=0)
        return lax.all_gather(mine, ("shard", "cross", "core"), axis=0, tiled=True)

    def finish(self, total):
        (cross,) = yield [self.swap(total, 2)]
        total = (total.astype(FULL) + cross.astype(FULL)).astype(LOW)
        (pair,) = yield [self.swap(total, 1)]
        low = jnp.where(self.core == 0, total, pair)
        high = jnp.where(self.core == 0, pair, total)
        return jnp.concatenate([low, high], axis=0).astype(FULL)

    def reduce(self, values):
        if self.direct:
            own = lax.psum_scatter(values, "shard", scatter_dimension=0, tiled=True)
            return lax.psum(own, ("cross", "core")).astype(FULL)
        width = values.shape[1]
        half = values.shape[0] // self.size // 2
        split = values.reshape(self.size, 2, half, width)
        other = self.swap(lax.dynamic_index_in_dim(split, 1 - self.core, axis=1, keepdims=False), 1)
        (other,) = yield [other]

        def piece(step):
            owner = self.owner(step)
            own = lax.dynamic_slice(split, (owner, self.core, 0, 0), (1, 1, half, width))
            pair = lax.dynamic_slice(other, (owner, 0, 0), (1, half, width))
            return own[0, 0].astype(FULL) + pair[0].astype(FULL)

        ahead = piece(self.far).astype(LOW)
        back = piece(-self.near).astype(LOW)
        for step in range(self.far - 1, -1, -1):
            moving = [self.hop(ahead, 1)]
            if step < self.near:
                moving.append(self.hop(back, -1))
            ahead, *rest = yield moving
            if step > 0:
                ahead = (ahead.astype(FULL) + piece(step)).astype(LOW)
            if rest:
                back = rest[0]
                if step > 0:
                    back = (back.astype(FULL) + piece(-step)).astype(LOW)
        total = (piece(0) + ahead.astype(FULL) + back.astype(FULL)).astype(LOW)
        return (yield from self.finish(total))


class Flow:
    def __init__(self):
        self.running = {}
        self.results = {}

    def start(self, name, steps):
        self._move(name, steps, None)

    def _move(self, name, steps, values):
        try:
            self.running[name] = (steps, steps.send(values))
        except StopIteration as end:
            self.running.pop(name, None)
            self.results[name] = end.value

    def advance(self, *values, near=None):
        running = [item for item in self.running.items() if near is None or item[0] in near]
        flat = list(values)
        for _, (_, flight) in running:
            flat += flight
        tied = tie(*flat) if flat else ()
        at = len(values)
        for name, (steps, flight) in running:
            self._move(name, steps, list(tied[at : at + len(flight)]))
            at += len(flight)
        return tied[0] if len(values) == 1 else tuple(tied[: len(values)])

    def take(self, name):
        while name in self.running:
            steps, flight = self.running[name]
            self._move(name, steps, flight)
        return self.results[name]


def shards(
    mesh,
    tokens,
    w_query,
    w_key,
    w_value,
    b_query,
    b_value,
    w_out,
    b_out,
    gain_one,
    shift_one,
    w_inner,
    b_inner,
    w_outer,
    b_outer,
    gain_two,
    shift_two,
    cotangent,
):
    links = Links(mesh)
    size = links.size
    width = D // size
    hidden = b_inner.shape[0]

    own_groups = [
        jnp.concatenate([w[:, g * WIDE : (g + 1) * WIDE] for w in (w_query, w_key, w_value)], axis=1)
        for g in range(GROUPS)
    ]
    vectors = (b_query, b_value, b_out, gain_one, shift_one, b_outer, gain_two, shift_two)
    used = len(vectors) * width + hidden
    ride = not links.direct and used <= 3 * WIDE and width == LANES
    rows_in = [v.reshape(1, -1) for v in vectors + (b_inner,)]
    packed = jnp.concatenate(rows_in, axis=1)
    sent = None
    if ride:
        extra = jnp.pad(lay(rows_in), ((0, 0), (0, 3 * WIDE - used)))
        halves = [links.half_of(w[:, :WIDE]) for w in (w_query, w_key, w_value)]
        sent = jnp.concatenate([jnp.concatenate(halves, axis=1), extra], axis=0)
        sent, w_inner, w_outer = tie(sent, w_inner, w_outer)
    flow = Flow()
    flow.start("group0", links.gather(own_groups[0], sent))
    whole_inner = links.gather_quarters(w_inner)
    whole_outer = links.gather_quarters(w_outer)
    flow.advance()
    own_groups[1] = flow.advance(own_groups[1])
    flow.start("group1", links.gather(own_groups[1]))
    tokens_turned, w_out = flow.advance(turn(tokens), w_out)
    flow.start("out", links.gather(w_out))
    flow.advance()
    if ride:
        first_group, chunks, owners = flow.take("group0")
        vec, bias_inner, bias_groups = unpack(chunks, owners, width // 2, size * hidden)
    else:
        first_group = flow.take("group0")
        vec, bias_inner, bias_groups = links.vectors(packed[0], size * hidden)
    whole_groups = [first_group]

    projected = []
    attended, lse = None, []
    for g in range(GROUPS):
        bias = bias_groups[:, g * 3 * WIDE : (g + 1) * 3 * WIDE]
        projected.append((project(tokens, whole_groups[g]) + bias).astype(LOW))
        if g == 0:
            projected[g] = flow.advance(projected[g])
            attended, logs = attend(projected[g], g, attended)
            attended = flow.advance(attended)
            whole_groups.append(flow.take("group1"))
        else:
            projected[g] = flow.advance(projected[g])
            attended, logs = attend(projected[g], g, attended)
            attended = flow.advance(attended)
        lse.append(logs)
    whole_out = flow.take("out")
    unit_one, inverse_one, first_low = out_norm(attended, whole_out, tokens, vec)
    active, slope = inner_gelu(first_low, whole_inner, bias_inner)
    output, d_second, d_mid, sums_two = outer_norms(active, whole_outer, unit_one, vec, cotangent)

    grad_outer, d_mid = tie(gram(active, d_mid).astype(LOW), d_mid)
    flow.start("outer_back", links.reduce(grad_outer))
    d_pre, sum_inner = outer_back(d_mid, whole_outer, slope)
    d_pre = flow.advance(d_pre)
    grad_inner, d_pre = flow.advance(gram(first_low, d_pre).astype(LOW), d_pre)
    flow.start("inner_back", links.reduce(grad_inner))
    sums_one, before = jnp.zeros((8, D), FULL), []
    for part in range(2):
        *before, sums_one = inner_back(
            part, d_pre, whole_inner, d_second, unit_one, inverse_one, vec, whole_out, sums_one, before
        )
        before[0], sums_one = flow.advance(before[0], sums_one)
    d_inner, d_branch, d_attended = before
    grad_out, d_attended = tie(gram(attended, d_branch).astype(LOW), d_attended)

    d_groups, sums_group = [], []
    for g in range(GROUPS):
        d_group, sums = attend_back(projected[g], d_attended, lse[g], g)
        d_group, sums, d_attended = flow.advance(d_group, sums, d_attended)
        sums_group.append(sums)
        small = None
        if g == GROUPS - 1:
            arrays = [sums_one, sums_two, sum_inner] + sums_group
            spans = [[(3 + h, 0, place * WIDE, WIDE) for h in range(GROUPS)] for place in (0, 2)]
            spans += [[(i, row, 0, D)] for i, row in ((0, 2), (0, 0), (0, 1), (1, 2), (1, 0), (1, 1))]
            spans += [[(2, 0, 0, size * hidden)]]
            small = pack(arrays, spans, size)
        if ride and g == GROUPS - 1:
            small = jnp.pad(small, ((0, 0), (0, 3 * WIDE - used)))
            grad_group = product(tokens_turned, d_group, small, size)
        else:
            grad_group = product(tokens_turned, d_group)
        if g == 0:
            grad_group = jnp.concatenate([grad_group, grad_out], axis=1)
            grad_group, d_attended = tie(grad_group, d_attended)
        else:
            grad_group, d_group = flow.advance(grad_group, d_group)
        flow.start(f"back{g}", links.reduce(grad_group))
        d_groups.append(d_group)
    d_tokens = flow.advance(tokens_back(d_inner, d_groups[0], whole_groups[0], FULL))
    d_tokens = flow.advance(tokens_back(d_tokens, d_groups[1], whole_groups[1], LOW))
    own_outer = flow.take("outer_back")
    own_inner = flow.take("inner_back")
    own_groups = [flow.take(f"back{g}") for g in range(GROUPS)]
    own_out = own_groups[0][:, 3 * WIDE :]
    if ride:
        body = width // 2
        last = own_groups[1]
        own_small = last[body]
        own_groups[1] = jnp.concatenate([last[:body], last[body + EXTRA : 2 * body + EXTRA]], axis=0)
    else:
        own_small = lax.psum_scatter(small, "shard", scatter_dimension=0)
        own_small = lax.psum(own_small, ("cross", "core"))

    def joined(parts, place):
        columns = slice(place * WIDE, (place + 1) * WIDE)
        return jnp.concatenate([part[..., columns] for part in parts], axis=-1)

    (
        own_bias_query,
        own_bias_value,
        own_bias_out,
        own_gain_one,
        own_shift_one,
        own_bias_outer,
        own_gain_two,
        own_shift_two,
    ) = (own_small[i * width : (i + 1) * width] for i in range(len(vectors)))
    own_bias_inner = own_small[used - hidden : used]
    return (
        output,
        d_tokens,
        joined(own_groups, 0),
        joined(own_groups, 1),
        joined(own_groups, 2),
        own_bias_query,
        own_bias_value,
        own_out,
        own_bias_out,
        own_gain_one,
        own_shift_one,
        own_inner,
        own_bias_inner,
        own_outer,
        own_bias_outer,
        own_gain_two,
        own_shift_two,
    )


def solution(mesh):
    reps, size = mesh.shape["rep"], mesh.shape["shard"]
    mesh = jax.sharding.Mesh(mesh.devices.reshape(reps // 2, 2, size), AXES)
    rows = P(AXES, None)
    matrix = P("shard", None)
    vector = P("shard")
    return jax.shard_map(
        functools.partial(shards, mesh),
        mesh=mesh,
        in_specs=(
            rows,
            matrix,
            matrix,
            matrix,
            vector,
            vector,
            matrix,
            vector,
            vector,
            vector,
            matrix,
            vector,
            matrix,
            vector,
            vector,
            vector,
            rows,
        ),
        out_specs=(
            rows,
            rows,
            matrix,
            matrix,
            matrix,
            vector,
            vector,
            matrix,
            vector,
            vector,
            vector,
            matrix,
            vector,
            matrix,
            vector,
            vector,
            vector,
        ),
        check_vma=False,
    )
```

profile of v0, /device:TPU:0, one launch (start us, length us, event | category | flops | bytes accessed | tf_op | source)
XLA Modules:
  0.0 504.9 jit_solution(5415722858231141369)
XLA Ops:
  19.4 6.2 %collective-permute-done.1.refs_2_ = bf16[80,1536]{1,0:T(8,128)(2,1)S(1)} collective-permute-done((bf16[80,1536]{1,0:T(8,128)(2,1)S(1)}, bf16[80,1536]{1,0:T(8,128)(2,1)S(1)}, u32[]{:S(2)}, u32[]{:S(2)}) %collective-permute-start.1) | collective-permute-done | bytes 245792 | tf_op jit(solution)/shard_map/ppermute | solution.py:563
  29.0 7.1 %collective-permute-done.2.refs_5_.refs_3_ = bf16[80,1536]{1,0:T(8,128)(2,1)S(1)} collective-permute-done((bf16[80,1536]{1,0:T(8,128)(2,1)S(1)}, bf16[80,1536]{1,0:T(8,128)(2,1)S(1)}, u32[]{:S(2)}, u32[]{:S(2)}) %collective-permute-start.2) | collective-permute-done | bytes 245792 | tf_op jit(solution)/shard_map/ppermute | solution.py:563
  50.0 4.2 turn.1.left_ref
  54.2 4.3 collective-permute-done.10.refs_1_
  64.6 4.6 collective-permute-done.20.refs_2_
  74.9 12.4 %collective-permute-done.16.refs_6_ = bf16[64,1536]{1,0:T(8,128)(2,1)S(1)} collective-permute-done((bf16[64,1536]{1,0:T(8,128)(2,1)}, bf16[64,1536]{1,0:T(8,128)(2,1)S(1)}, u32[]{:S(2)}, u32[]{:S(2)}) %collective-permute-start.16) | collective-permute-done | bytes 196640 | tf_op jit(solution)/shard_map/ppermute | solution.py:563
  99.2 5.2 %assemble.3.w_ref = bf16[1024,1536]{1,0:T(8,128)(2,1)S(1)} custom-call(s32[15]{0:T(128)S(1)} %stack.122.place_ref, bf16[128,1536]{1,0:T(8,128)(2,1)S(1)} %pad_maximum_fusion.4.refs_0_, bf16[80,1536]{1,0:T(8,128)(2,1)S(1)} %collective-permute-done.refs_1_, bf16[80,1536]{1,0:T(8,128)(2,1)S(1)} %collective-permute-done.1.refs_2_, ...), custom_call_target="tpu_custom_call" | custom-call | tf_op jit(solution)/shard_map/assemble/pallas_call | solution.py:448
  106.5 3.6 fusion.query_ref.key_ref.value_ref
  117.9 11.3 %attend.2 = (bf16[1024,1024]{1,0:T(8,128)(2,1)S(1)}, f32[8,2,512]{2,1,0:T(2,128)S(1)}) custom-call(bf16[1024,1536]{1,0:T(8,128)(2,1)S(1)} %fusion.query_ref.key_ref.value_ref, bf16[1024,1536]{1,0:T(8,128)(2,1)S(1)} %fusion.query_ref.key_ref.value_ref, bf16[1024,1536]{1,0:T(8,128)(2,1)S(1)} %fusion.query_ref.key_ref.value_ref), custom_call_target="tpu_custom_call" | custom-call | tf_op jit(solution)/shard_map/attend/pallas_call | solution.py:119
  132.0 4.1 assemble.4.w_ref
  136.1 4.8 fusion.1.query_ref.key_ref.value_ref
  146.3 11.3 %attend.3 = (bf16[1024,1024]{1,0:T(8,128)(2,1)S(1)}, f32[8,2,512]{2,1,0:T(2,128)S(1)}) custom-call(bf16[1024,1536]{1,0:T(8,128)(2,1)S(1)} %copy-done.2, bf16[1024,1536]{1,0:T(8,128)(2,1)S(1)} %copy-done.2, bf16[1024,1536]{1,0:T(8,128)(2,1)S(1)} %copy-done.2, bf16[1024,1024]{1,0:T(8,128)(2,1)S(1)} %copy-done.19), custom_call_target="tpu_custom_call", output_to_operand_aliasing={{0}: (3, {})} | custom-call | tf_op jit(solution)/shard_map/attend/pallas_call | solution.py:119
  163.8 7.3 %out_norm.1 = (f32[1024,1024]{1,0:T(8,128)}, f32[1024,128]{1,0:T(8,128)S(1)}, bf16[1024,1024]{1,0:T(8,128)(2,1)S(1)}) custom-call(bf16[1024,1024]{1,0:T(8,128)(2,1)S(1)} %copy-done.21, bf16[1024,1024]{1,0:T(8,128)(2,1)} %copy-done.4, bf16[1024,1024]{1,0:T(8,128)(2,1)} %tokens_ref.1, f32[8,1024]{1,0:T(8,128)S(1)} %copy-done.37), custom_call_target="tpu_custom_call" | custom-call | tf_op jit(solution)/shard_map/out_norm/pallas_call | solution.py:205
  174.8 19.0 %inner_gelu.1 = (bf16[1024,4096]{1,0:T(8,128)(2,1)}, bf16[1024,4096]{1,0:T(8,128)(2,1)}) custom-call(bf16[1024,1024]{1,0:T(8,128)(2,1)S(1)} %copy-done.29, bf16[1024,4096]{1,0:T(8,128)(2,1)} %all-gather.3.cloned.1.call-done.w_ref, f32[1,4096]{1,0:T(1,128)S(1)} %get-tuple-element.200.bias_ref), custom_call_target="tpu_custom_call" | custom-call | tf_op jit(solution)/shard_map/inner_gelu/pallas_call | solution.py:230
  195.4 18.4 %outer_norms.1 = (bf16[1024,1024]{1,0:T(8,128)(2,1)}, f32[1024,1024]{1,0:T(8,128)}, bf16[1024,1024]{1,0:T(8,128)(2,1)S(1)}, f32[8,1024]{1,0:T(8,128)S(1)}) custom-call(bf16[1024,4096]{1,0:T(8,128)(2,1)} %get-tuple-element.201.active_ref, bf16[4096,1024]{1,0:T(8,128)(2,1)} %all-gather.5.cloned.1.call-done.w_ref, f32[1024,1024]{1,0:T(8,128)} %get-tuple-element.203.unit_ref, ...), custom_call_target="tpu_custom_call" | custom-call | tf_op jit(solution)/shard_map/outer_norms/pallas_call | solution.py:259
  213.9 12.1 %convolution_convert_fusion.1 = bf16[4096,1024]{1,0:T(8,128)(2,1)S(1)} fusion(bf16[1024,4096]{1,0:T(8,128)(2,1)} %get-tuple-element.201.active_ref, bf16[1024,1024]{1,0:T(8,128)(2,1)S(1)} %get-tuple-element.206.d_ref), kind=kOutput, calls=%fused_computation.1 | convolution fusion | flops 8594128896 | bytes 18874368 | tf_op jit(solution)/shard_map/dot_general | solution.py:29
  226.1 3.3 copy-done.77
  233.4 15.5 %outer_back.1 = (bf16[1024,4096]{1,0:T(8,128)(2,1)}, f32[1,4096]{1,0:T(1,128)S(1)}) custom-call(bf16[1024,1024]{1,0:T(8,128)(2,1)S(1)} %copy-done.32, bf16[4096,1024]{1,0:T(8,128)(2,1)} %all-gather.5.cloned.1.call-done.w_ref, bf16[1024,4096]{1,0:T(8,128)(2,1)} %get-tuple-element.207.slope_ref), custom_call_target="tpu_custom_call" | custom-call | tf_op jit(solution)/shard_map/outer_back/pallas_call | solution.py:285
  251.4 11.4 %convolution_convert_fusion = bf16[1024,4096]{1,0:T(8,128)(2,1)S(1)} fusion(bf16[1024,1024]{1,0:T(8,128)(2,1)S(1)} %copy-done.30, bf16[1024,4096]{1,0:T(8,128)(2,1)} %get-tuple-element.212.d_pre_ref), kind=kOutput, calls=%fused_computation | convolution fusion | flops 8594128896 | bytes 18874368 | tf_op jit(solution)/shard_map/dot_general | solution.py:29
  274.6 16.1 %inner_back.2 = (f32[1024,1024]{1,0:T(8,128)}, bf16[1024,1024]{1,0:T(8,128)(2,1)S(1)}, bf16[1024,1024]{1,0:T(8,128)(2,1)S(1)}, f32[8,1024]{1,0:T(8,128)S(1)}) custom-call(bf16[1024,4096]{1,0:T(8,128)(2,1)} %get-tuple-element.212.d_pre_ref, bf16[1024,4096]{1,0:T(8,128)(2,1)} %all-gather.3.cloned.1.call-done.w_ref, f32[1024,1024]{1,0:T(8,128)} %get-tuple-element.213.d_ref, ...), custom_call_target="tpu_custom_call" | custom-call | tf_op jit(solution)/shard_map/inner_back/pallas_call | solution.py:337
  296.8 3.4 fusion.25
  306.5 15.9 %inner_back.3 = (f32[1024,1024]{1,0:T(8,128)}, bf16[1024,1024]{1,0:T(8,128)(2,1)S(1)}, bf16[1024,1024]{1,0:T(8,128)(2,1)S(1)}, f32[8,1024]{1,0:T(8,128)S(1)}) custom-call(bf16[1024,4096]{1,0:T(8,128)(2,1)} %get-tuple-element.212.d_pre_ref, ...), custom_call_target="tpu_custom_call", output_to_operand_aliasing={{0}: (8, {}), {1}: (9, {}), {2}: (10, {})} | custom-call | tf_op jit(solution)/shard_map/inner_back/pallas_call | solution.py:337
  334.3 18.4 %attend_back.2 = (bf16[1024,1536]{1,0:T(8,128)(2,1)S(1)}, f32[8,1536]{1,0:T(8,128)S(1)}) custom-call(bf16[1024,1536]{1,0:T(8,128)(2,1)S(1)} %fusion.query_ref.key_ref.value_ref, bf16[1024,1536]{1,0:T(8,128)(2,1)S(1)} %fusion.query_ref.key_ref.value_ref, bf16[1024,1536]{1,0:T(8,128)(2,1)S(1)} %fusion.query_ref.key_ref.value_ref, ...), custom_call_target="tpu_custom_call" | custom-call | tf_op jit(solution)/shard_map/attend_back/pallas_call | solution.py:136
  355.3 5.2 %product.2 = bf16[1024,1536]{1,0:T(8,128)(2,1)S(1)} custom-call(bf16[1024,1024]{1,0:T(8,128)(2,1)S(1)} %copy-done.9, bf16[1024,1536]{1,0:T(8,128)(2,1)} %copy-done.12), custom_call_target="tpu_custom_call" | custom-call | tf_op jit(solution)/shard_map/product/pallas_call | solution.py:422
  363.2 3.4 dynamic-slice_bitcast_fusion.2
  374.0 18.0 %attend_back.3 = (bf16[1024,1536]{1,0:T(8,128)(2,1)S(1)}, f32[8,1536]{1,0:T(8,128)S(1)}) custom-call(bf16[1024,1536]{1,0:T(8,128)(2,1)S(1)} %copy-done.3, bf16[1024,1536]{1,0:T(8,128)(2,1)S(1)} %copy-done.3, bf16[1024,1536]{1,0:T(8,128)(2,1)S(1)} %copy-done.3, bf16[1024,1024]{1,0:T(8,128)(2,1)S(1)} %copy-done.8, f32[8,2,512]{2,1,0:T(2,128)S(1)} %get-tuple-element.243.lse_ref), custom_call_target="tpu_custom_call" | custom-call | tf_op jit(solution)/shard_map/attend_back/pallas_call | solution.py:136
  394.6 3.3 fusion.3
  407.2 5.1 %product.3 = bf16[1280,1536]{1,0:T(8,128)(2,1)} custom-call(bf16[1024,1024]{1,0:T(8,128)(2,1)S(1)} %copy-done.10, bf16[1024,1536]{1,0:T(8,128)(2,1)S(1)} %copy-done.16, f32[8,1536]{1,0:T(8,128)S(1)} %copy-done.44), custom_call_target="tpu_custom_call" | custom-call | tf_op jit(solution)/shard_map/product/pallas_call | solution.py:422
  427.7 7.7 %tokens_back.2.base_ref = f32[1024,1024]{1,0:T(8,128)} custom-call(f32[1024,1024]{1,0:T(8,128)} %get-tuple-element.228.base_ref, bf16[1024,1536]{1,0:T(8,128)(2,1)S(1)} %copy-done.13, bf16[1024,1536]{1,0:T(8,128)(2,1)} %copy-done.11), custom_call_target="tpu_custom_call" | custom-call | tf_op jit(solution)/shard_map/tokens_back/pallas_call | solution.py:372
  445.2 7.3 %tokens_back.3 = bf16[1024,1024]{1,0:T(8,128)(2,1)} custom-call(f32[1024,1024]{1,0:T(8,128)} %tokens_back.2.base_ref, bf16[1024,1536]{1,0:T(8,128)(2,1)S(1)} %copy-done.17, bf16[1024,1536]{1,0:T(8,128)(2,1)} %copy-done.14), custom_call_target="tpu_custom_call" | custom-call | tf_op jit(solution)/shard_map/tokens_back/pallas_call | solution.py:372
  480.4 3.6 collective-permute-done.76
  486.4 5.9 %collective-permute-done.80 = bf16[80,1536]{1,0:T(8,128)(2,1)S(1)} collective-permute-done((bf16[80,1536]{1,0:T(8,128)(2,1)S(1)}, bf16[80,1536]{1,0:T(8,128)(2,1)S(1)}, u32[]{:S(2)}, u32[]{:S(2)}) %collective-permute-start.80) | collective-permute-done | bytes 245792 | tf_op jit(solution)/shard_map/ppermute | solution.py:570
  (410 shorter events, 209.4 us)
Async XLA Ops:
  7.2 166.0 %all-gather.3.cloned.1.call-start = ((), (), s32[]{:S(2)}) async-start(), calls=%async_computation | async-start | bytes 8650752 | tf_op jit(solution)/shard_map/all_gather | solution.py:633
  14.5 179.4 %all-gather.5.cloned.1.call-start = ((), (), s32[]{:S(2)}) async-start(), calls=%async_computation.1 | async-start | bytes 8650752 | tf_op jit(solution)/shard_map/all_gather | solution.py:633
  41.2 17.4 %collective-permute-start.8 = (bf16[80,1536]{1,0:T(8,128)(2,1)S(1)}, bf16[80,1536]{1,0:T(8,128)(2,1)S(1)}, u32[]{:S(2)}, u32[]{:S(2)}) collective-permute-start(bf16[80,1536]{1,0:T(8,128)(2,1)S(1)} %collective-permute-done.2.refs_5_.refs_3_), channel_id=1, source_target_pairs={{0,8},{1,9},{2,10},{3,11},{4,12},{5,13},{6,14},{7,15},{8,0},{9,1},... | collective-permute-start | bytes 737288 | tf_op jit(solution)/shard_map/ppermute | solution.py:570
  41.3 17.3 %collective-permute-start.6 = (bf16[80,1536]{1,0:T(8,128)(2,1)S(1)}, bf16[80,1536]{1,0:T(8,128)(2,1)S(1)}, u32[]{:S(2)}, u32[]{:S(2)}) collective-permute-start(bf16[80,1536]{1,0:T(8,128)(2,1)S(1)} %collective-permute-done.2.refs_5_.refs_3_), channel_id=1, source_target_pairs={{0,2},{2,4},{4,6},{6,7},{7,5},{5,3},{3,1},{1,0},{8,9},{10,8},{12,1... | collective-permute-start | bytes 737288 | tf_op jit(solution)/shard_map/ppermute | solution.py:563
  42.7 15.8 %collective-permute-start.9 = (bf16[80,1536]{1,0:T(8,128)(2,1)S(1)}, bf16[80,1536]{1,0:T(8,128)(2,1)}, u32[]{:S(2)}, u32[]{:S(2)}) collective-permute-start(bf16[80,1536]{1,0:T(8,128)(2,1)S(1)} %collective-permute-done.3.refs_6_.refs_4_), channel_id=1, source_target_pairs={{0,8},{1,9},{2,10},{3,11},{4,12},{5,13},{6,14},{7,15},{8,0},{9,1},... | collective-permute-start | bytes 737288 | tf_op jit(solution)/shard_map/ppermute | solution.py:570
  43.2 16.4 %collective-permute-start.7 = (bf16[80,1536]{1,0:T(8,128)(2,1)S(1)}, bf16[80,1536]{1,0:T(8,128)(2,1)S(1)}, u32[]{:S(2)}, u32[]{:S(2)}) collective-permute-start(bf16[80,1536]{1,0:T(8,128)(2,1)S(1)} %collective-permute-done.3.refs_6_.refs_4_), channel_id=1, source_target_pairs={{0,1},{2,0},{4,2},{6,4},{7,6},{5,7},{3,5},{1,3},{8,10},{10,12},{12... | collective-permute-start | bytes 737288 | tf_op jit(solution)/shard_map/ppermute | solution.py:563
  64.6 22.7 %collective-permute-start.13 = (bf16[80,1536]{1,0:T(8,128)(2,1)S(1)}, bf16[80,1536]{1,0:T(8,128)(2,1)S(1)}, u32[]{:S(2)}, u32[]{:S(2)}) collective-permute-start(bf16[80,1536]{1,0:T(8,128)(2,1)S(1)} %collective-permute-done.6.refs_9_.refs_5_), channel_id=1, source_target_pairs={{0,8},{1,9},{2,10},{3,11},{4,12},{5,13},{6,14},{7,15},{8,0},{9,1},... | collective-permute-start | bytes 737288 | tf_op jit(solution)/shard_map/ppermute | solution.py:570
  69.2 18.8 %collective-permute-start.12 = (bf16[80,1536]{1,0:T(8,128)(2,1)S(1)}, bf16[80,1536]{1,0:T(8,128)(2,1)S(1)}, u32[]{:S(2)}, u32[]{:S(2)}) collective-permute-start(bf16[80,1536]{1,0:T(8,128)(2,1)S(1)} %collective-permute-done.6.refs_9_.refs_5_), channel_id=1, source_target_pairs={{0,2},{2,4},{4,6},{6,7},{7,5},{5,3},{3,1},{1,0},{8,9},{10,8},{12,1... | collective-permute-start | bytes 737288 | tf_op jit(solution)/shard_map/ppermute | solution.py:563
  71.5 16.6 %collective-permute-start.14 = (bf16[80,1536]{1,0:T(8,128)(2,1)S(1)}, bf16[80,1536]{1,0:T(8,128)(2,1)S(1)}, u32[]{:S(2)}, u32[]{:S(2)}) collective-permute-start(bf16[80,1536]{1,0:T(8,128)(2,1)S(1)} %collective-permute-done.7.refs_10_.refs_6_), channel_id=1, source_target_pairs={{0,8},{1,9},{2,10},{3,11},{4,12},{5,13},{6,14},{7,15},{8,0},{9,1},... | collective-permute-start | bytes 737288 | tf_op jit(solution)/shard_map/ppermute | solution.py:570
  88.7 16.7 %collective-permute-start.26 = (bf16[64,1024]{1,0:T(8,128)(2,1)}, bf16[64,1024]{1,0:T(8,128)(2,1)}, u32[]{:S(2)}, u32[]{:S(2)}) collective-permute-start(bf16[64,1024]{1,0:T(8,128)(2,1)} %collective-permute-done.19.refs_1_), channel_id=1, source_target_pairs={{0,2},{2,4},{4,6},{6,7},{7,5},{5,3},{3,1},{1,0},{8,9},{10,8},{12,1... | collective-permute-start | bytes 393224 | tf_op jit(solution)/shard_map/ppermute | solution.py:563
  92.0 18.2 %collective-permute-start.27 = (bf16[64,1024]{1,0:T(8,128)(2,1)}, bf16[64,1024]{1,0:T(8,128)(2,1)S(1)}, u32[]{:S(2)}, u32[]{:S(2)}) collective-permute-start(bf16[64,1024]{1,0:T(8,128)(2,1)} %collective-permute-done.20.refs_2_), channel_id=1, source_target_pairs={{0,1},{2,0},{4,2},{6,4},{7,6},{5,7},{3,5},{1,3},{8,10},{10,12},{12... | collective-permute-start | bytes 393224 | tf_op jit(solution)/shard_map/ppermute | solution.py:563
  94.4 15.8 %collective-permute-start.24 = (bf16[64,1536]{1,0:T(8,128)(2,1)}, bf16[64,1536]{1,0:T(8,128)(2,1)S(1)}, u32[]{:S(2)}, u32[]{:S(2)}) collective-permute-start(bf16[64,1536]{1,0:T(8,128)(2,1)} %collective-permute-done.15.refs_5_), channel_id=1, source_target_pairs={{0,8},{1,9},{2,10},{3,11},{4,12},{5,13},{6,14},{7,15},{8,0},{9,1},... | collective-permute-start | bytes 589832 | tf_op jit(solution)/shard_map/ppermute | solution.py:570
  113.2 16.0 %collective-permute-start.31 = (bf16[64,1536]{1,0:T(8,128)(2,1)S(1)}, bf16[64,1536]{1,0:T(8,128)(2,1)S(1)}, u32[]{:S(2)}, u32[]{:S(2)}) collective-permute-start(bf16[64,1536]{1,0:T(8,128)(2,1)S(1)} %collective-permute-done.22.refs_9_), channel_id=1, source_target_pairs={{0,8},{1,9},{2,10},{3,11},{4,12},{5,13},{6,14},{7,15},{8,0},{9,1},... | collective-permute-start | bytes 589832 | tf_op jit(solution)/shard_map/ppermute | solution.py:570
  113.2 16.0 %collective-permute-start.30 = (bf16[64,1536]{1,0:T(8,128)(2,1)S(1)}, bf16[64,1536]{1,0:T(8,128)(2,1)S(1)}, u32[]{:S(2)}, u32[]{:S(2)}) collective-permute-start(bf16[64,1536]{1,0:T(8,128)(2,1)S(1)} %collective-permute-done.22.refs_9_), channel_id=1, source_target_pairs={{0,2},{2,4},{4,6},{6,7},{7,5},{5,3},{3,1},{1,0},{8,9},{10,8},{12,1... | collective-permute-start | bytes 589832 | tf_op jit(solution)/shard_map/ppermute | solution.py:563
  231.8 17.1 %collective-permute-start.42 = (bf16[8,256,1024]{2,1,0:T(8,128)(2,1)}, bf16[8,256,1024]{2,1,0:T(8,128)(2,1)}, u32[]{:S(2)}, u32[]{:S(2)}) collective-permute-start(bf16[8,256,1024]{2,1,0:T(8,128)(2,1)} %dynamic-slice_bitcast_fusion.1), channel_id=1, source_target_pairs={{0,8},{1,9},{2,10},{3,11},{4,12},{5,13},{6,14},{7,15},{8,0},{9,1},... | collective-permute-start | bytes 12582920 | tf_op jit(solution)/shard_map/ppermute | solution.py:570
  268.4 25.0 %collective-permute-start.46 = (bf16[8,64,4096]{2,1,0:T(8,128)(2,1)}, bf16[8,64,4096]{2,1,0:T(8,128)(2,1)}, u32[]{:S(2)}, u32[]{:S(2)}) collective-permute-start(bf16[8,64,4096]{2,1,0:T(8,128)(2,1)} %dynamic-slice_bitcast_fusion), channel_id=1, source_target_pairs={{0,8},{1,9},{2,10},{3,11},{4,12},{5,13},{6,14},{7,15},{8,0},{9,1},... | collective-permute-start | bytes 12582920 | tf_op jit(solution)/shard_map/ppermute | solution.py:570
  271.5 21.8 %collective-permute-start.45 = (bf16[256,1024]{1,0:T(8,128)(2,1)}, bf16[256,1024]{1,0:T(8,128)(2,1)}, u32[]{:S(2)}, u32[]{:S(2)}) collective-permute-start(bf16[256,1024]{1,0:T(8,128)(2,1)} %get-tuple-element.289), channel_id=1, source_target_pairs={{0,1},{2,0},{4,2},{6,4},{7,6},{5,7},{3,5},{1,3},{8,10},{10,12},{12... | collective-permute-start | bytes 1572872 | tf_op jit(solution)/shard_map/ppermute | solution.py:563
  272.5 20.8 %collective-permute-start.44 = (bf16[256,1024]{1,0:T(8,128)(2,1)}, bf16[256,1024]{1,0:T(8,128)(2,1)}, u32[]{:S(2)}, u32[]{:S(2)}) collective-permute-start(bf16[256,1024]{1,0:T(8,128)(2,1)} %get-tuple-element.290), channel_id=1, source_target_pairs={{0,2},{2,4},{4,6},{6,7},{7,5},{5,3},{3,1},{1,0},{8,9},{10,8},{12,1... | collective-permute-start | bytes 1572872 | tf_op jit(solution)/shard_map/ppermute | solution.py:563
  295.5 26.9 %collective-permute-start.49 = (bf16[64,4096]{1,0:T(8,128)(2,1)}, bf16[64,4096]{1,0:T(8,128)(2,1)}, u32[]{:S(2)}, u32[]{:S(2)}) collective-permute-start(bf16[64,4096]{1,0:T(8,128)(2,1)} %fusion.23), channel_id=1, source_target_pairs={{0,2},{2,4},{4,6},{6,7},{7,5},{5,3},{3,1},{1,0},{8,9},{10,8},{12,1... | collective-permute-start | bytes 1572872 | tf_op jit(solution)/shard_map/ppermute | solution.py:563
  300.3 22.1 %collective-permute-start.48 = (bf16[256,1024]{1,0:T(8,128)(2,1)}, bf16[256,1024]{1,0:T(8,128)(2,1)}, u32[]{:S(2)}, u32[]{:S(2)}) collective-permute-start(bf16[256,1024]{1,0:T(8,128)(2,1)} %get-tuple-element.287), channel_id=1, source_target_pairs={{0,1},{2,0},{4,2},{6,4},{7,6},{5,7},{3,5},{1,3},{8,10},{10,12},{12... | collective-permute-start | bytes 1572872 | tf_op jit(solution)/shard_map/ppermute | solution.py:563
  301.0 21.5 %collective-permute-start.47 = (bf16[256,1024]{1,0:T(8,128)(2,1)}, bf16[256,1024]{1,0:T(8,128)(2,1)}, u32[]{:S(2)}, u32[]{:S(2)}) collective-permute-start(bf16[256,1024]{1,0:T(8,128)(2,1)} %get-tuple-element.288), channel_id=1, source_target_pairs={{0,2},{2,4},{4,6},{6,7},{7,5},{5,3},{3,1},{1,0},{8,9},{10,8},{12,1... | collective-permute-start | bytes 1572872 | tf_op jit(solution)/shard_map/ppermute | solution.py:563
  325.3 29.3 %collective-permute-start.53 = (bf16[64,4096]{1,0:T(8,128)(2,1)S(1)}, bf16[64,4096]{1,0:T(8,128)(2,1)S(1)}, u32[]{:S(2)}, u32[]{:S(2)}) collective-permute-start(bf16[64,4096]{1,0:T(8,128)(2,1)S(1)} %get-tuple-element.283), channel_id=1, source_target_pairs={{0,1},{2,0},{4,2},{6,4},{7,6},{5,7},{3,5},{1,3},{8,10},{10,12},{12... | collective-permute-start | bytes 1572872 | tf_op jit(solution)/shard_map/ppermute | solution.py:563
  326.0 28.5 %collective-permute-start.52 = (bf16[64,4096]{1,0:T(8,128)(2,1)S(1)}, bf16[64,4096]{1,0:T(8,128)(2,1)S(1)}, u32[]{:S(2)}, u32[]{:S(2)}) collective-permute-start(bf16[64,4096]{1,0:T(8,128)(2,1)S(1)} %get-tuple-element.284), channel_id=1, source_target_pairs={{0,2},{2,4},{4,6},{6,7},{7,5},{5,3},{3,1},{1,0},{8,9},{10,8},{12,1... | collective-permute-start | bytes 1572872 | tf_op jit(solution)/shard_map/ppermute | solution.py:563
  329.8 24.7 %collective-permute-start.51 = (bf16[256,1024]{1,0:T(8,128)(2,1)S(1)}, bf16[256,1024]{1,0:T(8,128)(2,1)S(1)}, u32[]{:S(2)}, u32[]{:S(2)}) collective-permute-start(bf16[256,1024]{1,0:T(8,128)(2,1)S(1)} %get-tuple-element.285), channel_id=1, source_target_pairs={{0,1},{2,0},{4,2},{6,4},{7,6},{5,7},{3,5},{1,3},{8,10},{10,12},{12... | collective-permute-start | bytes 1572872 | tf_op jit(solution)/shard_map/ppermute | solution.py:563
  330.6 24.0 %collective-permute-start.50 = (bf16[256,1024]{1,0:T(8,128)(2,1)S(1)}, bf16[256,1024]{1,0:T(8,128)(2,1)S(1)}, u32[]{:S(2)}, u32[]{:S(2)}) collective-permute-start(bf16[256,1024]{1,0:T(8,128)(2,1)S(1)} %get-tuple-element.286), channel_id=1, source_target_pairs={{0,2},{2,4},{4,6},{6,7},{7,5},{5,3},{3,1},{1,0},{8,9},{10,8},{12,1... | collective-permute-start | bytes 1572872 | tf_op jit(solution)/shard_map/ppermute | solution.py:563
  366.6 27.8 %collective-permute-start.57 = (bf16[8,64,2560]{2,1,0:T(8,128)(2,1)}, bf16[8,64,2560]{2,1,0:T(8,128)(2,1)}, u32[]{:S(2)}, u32[]{:S(2)}) collective-permute-start(bf16[8,64,2560]{2,1,0:T(8,128)(2,1)} %dynamic-slice_bitcast_fusion.2), channel_id=1, source_target_pairs={{0,8},{1,9},{2,10},{3,11},{4,12},{5,13},{6,14},{7,15},{8,0},{9,1},... | collective-permute-start | bytes 7864328 | tf_op jit(solution)/shard_map/ppermute | solution.py:570
  368.6 25.7 %collective-permute-start.54 = (bf16[256,1024]{1,0:T(8,128)(2,1)S(1)}, bf16[256,1024]{1,0:T(8,128)(2,1)S(1)}, u32[]{:S(2)}, u32[]{:S(2)}) collective-permute-start(bf16[256,1024]{1,0:T(8,128)(2,1)S(1)} %fusion.12), channel_id=1, source_target_pairs={{0,16},{1,17},{2,18},{3,19},{4,20},{5,21},{6,22},{7,23},{8,24},{9,... | collective-permute-start | bytes 1572872 | tf_op jit(solution)/shard_map/ppermute | solution.py:570
  371.9 22.4 %collective-permute-start.56 = (bf16[64,4096]{1,0:T(8,128)(2,1)S(1)}, bf16[64,4096]{1,0:T(8,128)(2,1)S(1)}, u32[]{:S(2)}, u32[]{:S(2)}) collective-permute-start(bf16[64,4096]{1,0:T(8,128)(2,1)S(1)} %get-tuple-element.281), channel_id=1, source_target_pairs={{0,1},{2,0},{4,2},{6,4},{7,6},{5,7},{3,5},{1,3},{8,10},{10,12},{12... | collective-permute-start | bytes 1572872 | tf_op jit(solution)/shard_map/ppermute | solution.py:563
  372.9 21.4 %collective-permute-start.55 = (bf16[64,4096]{1,0:T(8,128)(2,1)S(1)}, bf16[64,4096]{1,0:T(8,128)(2,1)S(1)}, u32[]{:S(2)}, u32[]{:S(2)}) collective-permute-start(bf16[64,4096]{1,0:T(8,128)(2,1)S(1)} %get-tuple-element.282), channel_id=1, source_target_pairs={{0,2},{2,4},{4,6},{6,7},{7,5},{5,3},{3,1},{1,0},{8,9},{10,8},{12,1... | collective-permute-start | bytes 1572872 | tf_op jit(solution)/shard_map/ppermute | solution.py:563
  397.9 17.2 %collective-permute-start.60 = (bf16[64,4096]{1,0:T(8,128)(2,1)}, bf16[64,4096]{1,0:T(8,128)(2,1)}, u32[]{:S(2)}, u32[]{:S(2)}) collective-permute-start(bf16[64,4096]{1,0:T(8,128)(2,1)} %get-tuple-element.279), channel_id=1, source_target_pairs={{0,1},{2,0},{4,2},{6,4},{7,6},{5,7},{3,5},{1,3},{8,10},{10,12},{12... | collective-permute-start | bytes 1572872 | tf_op jit(solution)/shard_map/ppermute | solution.py:563
  398.9 16.2 %collective-permute-start.59 = (bf16[64,4096]{1,0:T(8,128)(2,1)}, bf16[64,4096]{1,0:T(8,128)(2,1)}, u32[]{:S(2)}, u32[]{:S(2)}) collective-permute-start(bf16[64,4096]{1,0:T(8,128)(2,1)} %get-tuple-element.280), channel_id=1, source_target_pairs={{0,2},{2,4},{4,6},{6,7},{7,5},{5,3},{3,1},{1,0},{8,9},{10,8},{12,1... | collective-permute-start | bytes 1572872 | tf_op jit(solution)/shard_map/ppermute | solution.py:563
  419.0 17.5 %collective-permute-start.65 = (bf16[8,80,1536]{2,1,0:T(8,128)(2,1)}, bf16[8,80,1536]{2,1,0:T(8,128)(2,1)}, u32[]{:S(2)}, u32[]{:S(2)}) collective-permute-start(bf16[8,80,1536]{2,1,0:T(8,128)(2,1)} %dynamic-slice_bitcast_fusion.3), channel_id=1, source_target_pairs={{0,8},{1,9},{2,10},{3,11},{4,12},{5,13},{6,14},{7,15},{8,0},{9,1},... | collective-permute-start | bytes 5898248 | tf_op jit(solution)/shard_map/ppermute | solution.py:570
  (144 other events, 1278.9 us)
Sparse Core Ops, SparseCore 0:
  14.6 88.3 all-gather.2
  106.4 80.6 all-gather.4
where the time goes:
time: 513 us; the launch traced here: 505 us
  Pallas kernels  197 us (38%)
  starting transfers between devices  71.5 us (14%)
  waiting for transfers between devices  70.7 us (14%)
  local copies, waits for them, and re-layouts  61.8 us (12%)
  other arithmetic  54 us (11%)
  matrix products  34.4 us (7%)
  between operations  15.8 us (3%)
    ppermute x49, waiting for transfers between devices, hop(): return lax.ppermute(values, AXES, pairs)  61 us
    ppermute x49, starting transfers between devices, hop(): return lax.ppermute(values, AXES, pairs)  58.9 us
    unnamed x184, local copies, waits for them, and re-layouts  43.8 us
    pallas_call x2, Pallas kernels, attend_back(): pl.pallas_call(attend_back_kernel, grid=(count // SEQ, PAIRS), in_specs=t...  36.4 us
    pallas_call x2, Pallas kernels, inner_back(): pl.pallas_call(inner_back_kernel, grid=(hidden // COLUMNS,), in_specs=[pl...  32 us
    dot_general x3, matrix products, gram(): lax.dot_general(left, right, (((0,), (0,)), ((), ())), preferred_element_...  26 us
    pallas_call x2, Pallas kernels, attend(): pl.pallas_call(attend_kernel, grid=(seqs, PAIRS), in_specs=triple() + [pl...  22.6 us
    pallas_call x1, Pallas kernels, inner_gelu(): pl.pallas_call(inner_kernel, grid=(hidden // COLUMNS,), in_specs=[kept((c...  19 us
  transfers between devices with their start and end apart: 84, of which 23 were waited for; matrix products, arithmetic and copies ran while one was open for 12% of the time, Pallas kernels for 34%

commit v1 on v0

--- a/solution.py
+++ b/solution.py
@@ -150,7 +150,7 @@
     )(qkv, qkv, qkv, d_attended, lse)
 
 
-ROWS = 256
+ROWS = 512
 COLUMNS = 512
 EXTRA = 16
 PARTS = 2
@@ -297,9 +297,8 @@
 
 
 def inner_back_kernel(
-    d_pre_ref, w_ref, d_ref, unit_ref, inverse_ref, vec_ref, w_out_ref, before_ref, *refs
+    d_pre_ref, w_ref, d_ref, unit_ref, inverse_ref, vec_ref, w_out_ref, out_ref, low_ref, attended_ref, sum_ref, total_ref
 ):
-    out_ref, low_ref, attended_ref, sum_ref, total_ref = refs[-5:]
     step = pl.program_id(0)
     part = against(d_pre_ref[...], w_ref[...])
 
@@ -313,8 +312,8 @@
 
     @pl.when(step == pl.num_programs(0) - 1)
     def _():
-        sum_ref[...] = before_ref[...]
-        for rows in pieces(total_ref.shape[0], 2):
+        sum_ref[...] = jnp.zeros_like(sum_ref)
+        for rows in pieces(total_ref.shape[0], 4):
             d_first = total_ref[rows, :]
             unit = unit_ref[rows, :]
             d_inner = normal_back(d_first * line(vec_ref, GAIN_ONE), unit, inverse_ref[rows, 0:1])
@@ -327,39 +326,31 @@
             add_line(sum_ref, 2, d_inner)
 
 
-def inner_back(part, d_pre, w_inner, d_second, unit, inverse, vec, w_out, sums, before):
+def inner_back(d_pre, w_inner, d_second, unit, inverse, vec, w_out):
     count, hidden = d_pre.shape
-    rows = count // 2
-
-    def own(width):
-        return pl.BlockSpec((rows, width), lambda i: (part, 0), pipeline_mode=pl.Buffered(1))
-
     return pl.pallas_call(
         inner_back_kernel,
-        grid=(hidden // COLUMNS,),
+        grid=(hidden // D,),
         in_specs=[
-            pl.BlockSpec((rows, COLUMNS), lambda i: (part, i)),
-            columns_of(D),
-            own(D),
-            own(D),
-            own(LANES),
+            pl.BlockSpec((count, D), lambda i: (0, i)),
+            pl.BlockSpec((D, D), lambda i: (0, i)),
+            kept((count, D)),
+            kept((count, D)),
+            kept((count, LANES)),
             kept((8, D)),
             kept((D, D)),
-            kept((8, D)),
-        ]
-        + [pl.BlockSpec(memory_space=pl.ANY)] * len(before),
-        out_specs=[own(D), own(D), own(D), kept((8, D))],
+        ],
+        out_specs=[kept((count, D)), kept((count, D)), kept((count, D)), kept((8, D))],
         out_shape=[
             jax.ShapeDtypeStruct((count, D), FULL),
             jax.ShapeDtypeStruct((count, D), LOW),
             jax.ShapeDtypeStruct((count, D), LOW),
             jax.ShapeDtypeStruct((8, D), FULL),
         ],
-        input_output_aliases={8 + i: i for i in range(len(before))},
-        scratch_shapes=[pltpu.VMEM((rows, D), FULL)],
+        scratch_shapes=[pltpu.VMEM((count, D), FULL)],
         compiler_params=LIMIT,
         name="inner_back",
-    )(d_pre, w_inner, d_second, unit, inverse, vec, w_out, sums, *before)
+    )(d_pre, w_inner, d_second, unit, inverse, vec, w_out)
 
 
 def tokens_kernel(base_ref, d_ref, w_ref, out_ref):
@@ -486,42 +477,43 @@
 
 
 def lay_kernel(*refs):
-    row = jnp.concatenate([ref[...].astype(FULL) for ref in refs[:-1]], axis=1)
-    refs[-1][...] = jnp.broadcast_to(row, refs[-1].shape).astype(LOW)
-
-
-def lay(vectors):
-    total = sum(vector.shape[1] for vector in vectors)
+    out_ref = refs[-1]
+    lines = []
+    for ref in refs[:-1]:
+        row = ref[...].astype(FULL)
+        lines += [row[:, first : first + LANES] for first in range(0, row.shape[1], LANES)]
+    spare = out_ref.shape[0] - len(lines)
+    out_ref[...] = jnp.concatenate(lines + [jnp.zeros((spare, LANES), FULL)], axis=0).astype(LOW)
+
+
+def lay(vectors, rows):
     return pl.pallas_call(
         lay_kernel,
-        out_shape=jax.ShapeDtypeStruct((EXTRA, total), LOW),
+        out_shape=jax.ShapeDtypeStruct((rows, LANES), LOW),
         name="lay",
     )(*vectors)
 
 
-def unpack_kernel(count, body, place_ref, *refs):
-    vec_ref, bias_ref, group_ref = refs[count:]
+def unpack_kernel(size, ref, vec_ref, bias_ref, group_ref):
     group_ref[...] = jnp.zeros_like(group_ref)
-    hidden = bias_ref.shape[1] // count
-    for i in range(count):
-        packed = refs[i][body : body + EXTRA, :].astype(FULL)[0:1, :]
-        owner = place_ref[i]
-        start = pl.multiple_of(owner * LANES, LANES)
-        for row in range(8):
-            vec_ref[row : row + 1, pl.ds(start, LANES)] = packed[:, row * LANES : (row + 1) * LANES]
-        first = pl.multiple_of(owner * hidden, LANES)
-        bias_ref[:, pl.ds(first, hidden)] = packed[:, 8 * LANES : 8 * LANES + hidden]
-        group = owner * LANES // WIDE
+    share = D // size
+    for shard in range(size):
+        packed = ref[shard * share : shard * share + EXTRA, :].astype(FULL)
+        start = shard * LANES
+        vec_ref[:, start : start + LANES] = packed[0:8, :]
+        lines = bias_ref.shape[1] // size // LANES
+        for i in range(lines):
+            first = (shard * lines + i) * LANES
+            bias_ref[:, first : first + LANES] = packed[8 + i : 9 + i, :]
+        group = start // WIDE
         for place, row in ((0, QUERY), (2, VALUE)):
-            first = pl.multiple_of(group * 2 * WIDE + place * WIDE + start, LANES)
-            group_ref[:, pl.ds(first, LANES)] = packed[:, row * LANES : (row + 1) * LANES]
-
-
-def unpack(chunks, owners, body, hidden):
-    count = len(chunks)
-    return pl.pallas_call(
-        functools.partial(unpack_kernel, count, body),
-        in_specs=[pl.BlockSpec(memory_space=pltpu.SMEM)] + [pl.BlockSpec(memory_space=pltpu.VMEM)] * count,
+            first = group * 2 * WIDE + place * WIDE + start
+            group_ref[:, first : first + LANES] = packed[row : row + 1, :]
+
+
+def unpack(lines, size, hidden):
+    return pl.pallas_call(
+        functools.partial(unpack_kernel, size),
         out_shape=[
             jax.ShapeDtypeStruct((8, D), FULL),
             jax.ShapeDtypeStruct((1, hidden), FULL),
@@ -529,7 +521,7 @@
         ],
         compiler_params=LIMIT,
         name="unpack",
-    )(jnp.stack(owners).astype(jnp.int32), *chunks)
+    )(lines)
 
 
 def tie(*values):
@@ -588,7 +580,7 @@
         half = values.shape[0] // 2
         return lax.dynamic_slice_in_dim(values, self.core * half, half, axis=0)
 
-    def gather(self, values, sent=None):
+    def gather(self, values):
         if self.direct:
             return lax.all_gather(values, "shard", axis=0, tiled=True)
         rows = values.shape[0]
@@ -596,18 +588,14 @@
         arrays = [values]
         moves = [(0, 0, rows)]
         places = [self.owner(0) * rows]
-        chunks, owners = [sent], [self.owner(0)]
 
         def keep(chunk, mine, step):
             moves.append((len(arrays), 0, body))
             arrays.append(chunk)
             core = self.core if mine else 1 - self.core
             places.append(self.owner(step) * rows + core * body)
-            if mine:
-                chunks.append(chunk)
-                owners.append(self.owner(step))
-
-        ahead = back = self.half_of(values) if sent is None else sent
+
+        ahead = back = self.half_of(values)
         for step in range(1, self.far + 2):
             flight = []
             if step > 1:
@@ -623,13 +611,14 @@
             ahead, back, *swapped = yield [ahead, back] + [chunk for chunk, _ in flight]
             for chunk, (_, place) in zip(swapped, flight):
                 keep(chunk, False, place)
-        whole = assemble(arrays, moves, places, self.size * rows)
-        return whole if sent is None else (whole, chunks, owners)
-
-    def gather_quarters(self, values):
+        return assemble(arrays, moves, places, self.size * rows)
+
+    def quarter_of(self, values):
         rows = values.shape[0] // self.reps
         index = lax.axis_index("cross") * 2 + self.core
-        mine = lax.dynamic_slice_in_dim(values, index * rows, rows, axis=0)
+        return lax.dynamic_slice_in_dim(values, index * rows, rows, axis=0)
+
+    def gather_quarters(self, mine):
         return lax.all_gather(mine, ("shard", "cross", "core"), axis=0, tiled=True)
 
     def finish(self, total):
@@ -738,31 +727,28 @@
     ]
     vectors = (b_query, b_value, b_out, gain_one, shift_one, b_outer, gain_two, shift_two)
     used = len(vectors) * width + hidden
-    ride = not links.direct and used <= 3 * WIDE and width == LANES
-    rows_in = [v.reshape(1, -1) for v in vectors + (b_inner,)]
-    packed = jnp.concatenate(rows_in, axis=1)
-    sent = None
+    ride = not links.direct and used <= 3 * WIDE and width == LANES and used <= width // links.reps * LANES
+    flow = Flow()
+    lines = [v.reshape(1, -1) for v in vectors + (b_inner,)]
     if ride:
-        extra = jnp.pad(lay(rows_in), ((0, 0), (0, 3 * WIDE - used)))
-        halves = [links.half_of(w[:, :WIDE]) for w in (w_query, w_key, w_value)]
-        sent = jnp.concatenate([jnp.concatenate(halves, axis=1), extra], axis=0)
-        sent, w_inner, w_outer = tie(sent, w_inner, w_outer)
-    flow = Flow()
-    flow.start("group0", links.gather(own_groups[0], sent))
-    whole_inner = links.gather_quarters(w_inner)
-    whole_outer = links.gather_quarters(w_outer)
+        first_own = [links.quarter_of(w[:, :WIDE]) for w in (w_query, w_key, w_value)]
+        first_own = jnp.concatenate(first_own + [lay(lines, width // links.reps)], axis=1)
+        first_whole = links.gather_quarters(first_own)
+    else:
+        first_whole = lax.all_gather(own_groups[0], "shard", axis=0, tiled=True)
+    whole_inner = links.gather_quarters(links.quarter_of(w_inner))
+    flow.start("group1", links.gather(own_groups[1]))
     flow.advance()
-    own_groups[1] = flow.advance(own_groups[1])
-    flow.start("group1", links.gather(own_groups[1]))
-    tokens_turned, w_out = flow.advance(turn(tokens), w_out)
+    w_out = flow.advance(w_out)
     flow.start("out", links.gather(w_out))
     flow.advance()
+    w_outer, tokens_turned = flow.advance(w_outer, turn(tokens))
+    flow.start("outer", links.gather(w_outer))
+    first_group = first_whole[:, : 3 * WIDE]
     if ride:
-        first_group, chunks, owners = flow.take("group0")
-        vec, bias_inner, bias_groups = unpack(chunks, owners, width // 2, size * hidden)
+        vec, bias_inner, bias_groups = unpack(first_whole[:, 3 * WIDE :], size, size * hidden)
     else:
-        first_group = flow.take("group0")
-        vec, bias_inner, bias_groups = links.vectors(packed[0], size * hidden)
+        vec, bias_inner, bias_groups = links.vectors(jnp.concatenate(lines, axis=1)[0], size * hidden)
     whole_groups = [first_group]
 
     projected = []
@@ -782,7 +768,9 @@
         lse.append(logs)
     whole_out = flow.take("out")
     unit_one, inverse_one, first_low = out_norm(attended, whole_out, tokens, vec)
+    first_low = flow.advance(first_low)
     active, slope = inner_gelu(first_low, whole_inner, bias_inner)
+    whole_outer = flow.take("outer")
     output, d_second, d_mid, sums_two = outer_norms(active, whole_outer, unit_one, vec, cotangent)
 
     grad_outer, d_mid = tie(gram(active, d_mid).astype(LOW), d_mid)
@@ -791,13 +779,10 @@
     d_pre = flow.advance(d_pre)
     grad_inner, d_pre = flow.advance(gram(first_low, d_pre).astype(LOW), d_pre)
     flow.start("inner_back", links.reduce(grad_inner))
-    sums_one, before = jnp.zeros((8, D), FULL), []
-    for part in range(2):
-        *before, sums_one = inner_back(
-            part, d_pre, whole_inner, d_second, unit_one, inverse_one, vec, whole_out, sums_one, before
-        )
-        before[0], sums_one = flow.advance(before[0], sums_one)
-    d_inner, d_branch, d_attended = before
+    d_inner, d_branch, d_attended, sums_one = inner_back(
+        d_pre, whole_inner, d_second, unit_one, inverse_one, vec, whole_out
+    )
+    d_branch, d_attended = flow.advance(d_branch, d_attended)
     grad_out, d_attended = tie(gram(attended, d_branch).astype(LOW), d_attended)
 
     d_groups, sums_group = [], []

time: 513 us -> 531 us (1.035)
  waiting for transfers between devices: 70.7 us -> 100 us
  Pallas kernels: 197 us -> 183 us
    all_gather x2, waiting for transfers between devices: 0.01 us -> 18 us  [gather_quarters(): return lax.all_gather(mine, ('shard', 'cross', 'core'), axis=0, tiled=True)]
    ppermute x49, waiting for transfers between devices: 61 us -> 73 us  [hop(): return lax.ppermute(values, AXES, pairs)]
    pallas_call x4 -> x3, Pallas kernels: 34 us -> 24 us  [the longest x1 22.5 us: inner_back(): pl.pallas_call(inner_back_kernel, grid=(hidden // D,), in_specs=[pl.Block...]
    unnamed x184 -> x206, local copies, waits for them, and re-layouts: 43.8 us -> 39.9 us
  transfers between devices with their start and end apart: 84 -> 84, of which waited for: 23 -> 24; matrix products, arithmetic and copies ran while one was open for 12% -> 13% of each run, Pallas kernels for 34% -> 27%
where the time goes in v1:
time: 531 us; the launch traced here: 522 us
  Pallas kernels  183 us (34%)
  waiting for transfers between devices  100 us (19%)
  starting transfers between devices  72.6 us (14%)
  local copies, waits for them, and re-layouts  61.4 us (12%)
  other arithmetic  53.3 us (10%)
  matrix products  35.5 us (7%)
  between operations  16 us (3%)
    ppermute x49, waiting for transfers between devices, hop(): return lax.ppermute(values, AXES, pairs)  73 us
    ppermute x49, starting transfers between devices, hop(): return lax.ppermute(values, AXES, pairs)  62 us
    unnamed x206, local copies, waits for them, and re-layouts  39.9 us
    pallas_call x2, Pallas kernels, attend_back(): pl.pallas_call(attend_back_kernel, grid=(count // SEQ, PAIRS), in_specs=t...  36.2 us
    dot_general x3, matrix products, gram(): lax.dot_general(left, right, (((0,), (0,)), ((), ())), preferred_element_...  25.9 us
    pallas_call x2, Pallas kernels, attend(): pl.pallas_call(attend_kernel, grid=(seqs, PAIRS), in_specs=triple() + [pl...  22.6 us
    pallas_call x1, Pallas kernels, inner_back(): pl.pallas_call(inner_back_kernel, grid=(hidden // D,), in_specs=[pl.Block...  22.5 us
    pallas_call x1, Pallas kernels, inner_gelu(): pl.pallas_call(inner_kernel, grid=(hidden // COLUMNS,), in_specs=[kept((c...  19 us
  transfers between devices with their start and end apart: 84, of which 24 were waited for; matrix products, arithmetic and copies ran while one was open for 13% of the time, Pallas kernels for 27%

profile of v1, /device:TPU:0, one launch (start us, length us, event | category | flops | bytes accessed | tf_op | source)
XLA Modules:
  0.0 522.2 jit_solution(18365408109522642196)
XLA Ops:
  17.7 5.1 collective-permute-done.1.refs_2_
  26.7 4.3 collective-permute-done.2.refs_5_
  40.1 3.3 collective-permute-done.10.refs_1_
  62.3 18.0 %all-gather.3.cloned.1.call-done = bf16[1024,1664]{1,0:T(8,128)(2,1)} async-done(((bf16[32,1664]{1,0:T(8,128)(2,1)}), bf16[1024,1664]{1,0:T(8,128)(2,1)}) %all-gather.3.cloned.1.call-update) | async-done | bytes 3407888 | tf_op jit(solution)/shard_map/all_gather | solution.py:622
  84.6 5.9 %fusion.query_ref.key_ref.value_ref = bf16[1024,1536]{1,0:T(8,128)(2,1)S(1)} fusion(bf16[1024,1024]{1,0:T(8,128)(2,1)} %tokens_ref.1, f32[1536]{0:T(1024)S(1)} %get-tuple-element.264, bf16[1024,1664]{1,0:T(8,128)(2,1)} %all-gather.3.cloned.1.call-done), kind=kOutput, calls=%fused_computation.7 | convolution fusion | flops 3224371200 | bytes 8394752 | tf_op jit(solution)/shard_map/dot_general | solution.py:25
  98.3 13.5 %collective-permute-done.26.refs_13_ = bf16[64,1024]{1,0:T(8,128)(2,1)} collective-permute-done((bf16[64,1024]{1,0:T(8,128)(2,1)}, bf16[64,1024]{1,0:T(8,128)(2,1)}, u32[]{:S(2)}, u32[]{:S(2)}) %collective-permute-start.26) | collective-permute-done | bytes 131104 | tf_op jit(solution)/shard_map/ppermute | solution.py:555
  113.8 11.3 %attend.2 = (bf16[1024,1024]{1,0:T(8,128)(2,1)S(1)}, f32[8,2,512]{2,1,0:T(2,128)S(1)}) custom-call(bf16[1024,1536]{1,0:T(8,128)(2,1)S(1)} %fusion.query_ref.key_ref.value_ref, bf16[1024,1536]{1,0:T(8,128)(2,1)S(1)} %fusion.query_ref.key_ref.value_ref, bf16[1024,1536]{1,0:T(8,128)(2,1)S(1)} %fusion.query_ref.key_ref.value_ref), custom_call_target="tpu_custom_call" | custom-call | tf_op jit(solution)/shard_map/attend/pallas_call | solution.py:119
  125.3 5.2 assemble.3.w_ref
  133.9 3.6 fusion.1.query_ref.key_ref.value_ref
  139.5 16.4 %collective-permute-done.34.refs_9_ = bf16[256,1024]{1,0:T(8,128)(2,1)S(1)} collective-permute-done((bf16[256,1024]{1,0:T(8,128)(2,1)}, bf16[256,1024]{1,0:T(8,128)(2,1)S(1)}, u32[]{:S(2)}, u32[]{:S(2)}) %collective-permute-start.34) | collective-permute-done | bytes 524320 | tf_op jit(solution)/shard_map/ppermute | solution.py:555
  156.7 11.1 %collective-permute-done.35.refs_10_ = bf16[256,1024]{1,0:T(8,128)(2,1)S(1)} collective-permute-done((bf16[256,1024]{1,0:T(8,128)(2,1)}, bf16[256,1024]{1,0:T(8,128)(2,1)S(1)}, u32[]{:S(2)}, u32[]{:S(2)}) %collective-permute-start.35) | collective-permute-done | bytes 524320 | tf_op jit(solution)/shard_map/ppermute | solution.py:555
  170.1 11.3 %attend.3 = (bf16[1024,1024]{1,0:T(8,128)(2,1)S(1)}, f32[8,2,512]{2,1,0:T(2,128)S(1)}) custom-call(bf16[1024,1536]{1,0:T(8,128)(2,1)S(1)} %fusion.1.query_ref.key_ref.value_ref, bf16[1024,1536]{1,0:T(8,128)(2,1)S(1)} %fusion.1.query_ref.key_ref.value_ref, bf16[1024,1536]{1,0:T(8,128)(2,1)S(1)} %fusion.1.query_ref.key_ref.value_ref, ...), custom_call_target="tpu_custom_call", output_to_operand_aliasing={{0}: (3, {})} | custom-call | tf_op jit(solution)/shard_map/attend/pallas_call | solution.py:119
  192.9 6.9 %out_norm.1 = (f32[1024,1024]{1,0:T(8,128)}, f32[1024,128]{1,0:T(8,128)S(1)}, bf16[1024,1024]{1,0:T(8,128)(2,1)S(1)}) custom-call(bf16[1024,1024]{1,0:T(8,128)(2,1)S(1)} %copy-done.15, bf16[1024,1024]{1,0:T(8,128)(2,1)} %copy-done.7, bf16[1024,1024]{1,0:T(8,128)(2,1)} %tokens_ref.1, f32[8,1024]{1,0:T(8,128)S(1)} %copy-done.44), custom_call_target="tpu_custom_call" | custom-call | tf_op jit(solution)/shard_map/out_norm/pallas_call | solution.py:205
  204.9 3.2 copy-done.4
  209.7 19.0 %inner_gelu.1 = (bf16[1024,4096]{1,0:T(8,128)(2,1)}, bf16[1024,4096]{1,0:T(8,128)(2,1)}) custom-call(bf16[1024,1024]{1,0:T(8,128)(2,1)S(1)} %copy-done.22, bf16[1024,4096]{1,0:T(8,128)(2,1)} %all-gather.5.cloned.1.call-done.w_ref, f32[1,4096]{1,0:T(1,128)S(1)} %get-tuple-element.187.bias_ref), custom_call_target="tpu_custom_call" | custom-call | tf_op jit(solution)/shard_map/inner_gelu/pallas_call | solution.py:230
  228.7 18.6 %outer_norms.1 = (bf16[1024,1024]{1,0:T(8,128)(2,1)}, f32[1024,1024]{1,0:T(8,128)}, bf16[1024,1024]{1,0:T(8,128)(2,1)S(1)}, f32[8,1024]{1,0:T(8,128)S(1)}) custom-call(bf16[1024,4096]{1,0:T(8,128)(2,1)} %get-tuple-element.188.active_ref, bf16[4096,1024]{1,0:T(8,128)(2,1)} %copy-done.4, f32[1024,1024]{1,0:T(8,128)} %get-tuple-element.196.unit_ref, ...), custom_call_target="tpu_custom_call" | custom-call | tf_op jit(solution)/shard_map/outer_norms/pallas_call | solution.py:259
  247.3 12.1 %convolution_convert_fusion.1 = bf16[4096,1024]{1,0:T(8,128)(2,1)S(1)} fusion(bf16[1024,4096]{1,0:T(8,128)(2,1)} %get-tuple-element.188.active_ref, bf16[1024,1024]{1,0:T(8,128)(2,1)S(1)} %get-tuple-element.199.d_ref), kind=kOutput, calls=%fused_computation.1 | convolution fusion | flops 8594128896 | bytes 18874368 | tf_op jit(solution)/shard_map/dot_general | solution.py:29
  266.2 15.4 %outer_back.1 = (bf16[1024,4096]{1,0:T(8,128)(2,1)}, f32[1,4096]{1,0:T(1,128)S(1)}) custom-call(bf16[1024,1024]{1,0:T(8,128)(2,1)S(1)} %copy-done.25, bf16[4096,1024]{1,0:T(8,128)(2,1)} %copy-done.4, bf16[1024,4096]{1,0:T(8,128)(2,1)} %get-tuple-element.200.slope_ref), custom_call_target="tpu_custom_call" | custom-call | tf_op jit(solution)/shard_map/outer_back/pallas_call | solution.py:285
  283.2 11.4 %convolution_convert_fusion = bf16[1024,4096]{1,0:T(8,128)(2,1)S(1)} fusion(bf16[1024,1024]{1,0:T(8,128)(2,1)S(1)} %copy-done.23, bf16[1024,4096]{1,0:T(8,128)(2,1)} %get-tuple-element.205.d_pre_ref), kind=kOutput, calls=%fused_computation | convolution fusion | flops 8594128896 | bytes 18874368 | tf_op jit(solution)/shard_map/dot_general | solution.py:29
  306.0 22.5 %inner_back.1 = (f32[1024,1024]{1,0:T(8,128)}, bf16[1024,1024]{1,0:T(8,128)(2,1)S(1)}, bf16[1024,1024]{1,0:T(8,128)(2,1)S(1)}, f32[8,1024]{1,0:T(8,128)S(1)}) custom-call(bf16[1024,4096]{1,0:T(8,128)(2,1)} %get-tuple-element.205.d_pre_ref, bf16[1024,4096]{1,0:T(8,128)(2,1)} %all-gather.5.cloned.1.call-done.w_ref, f32[1024,1024]{1,0:T(8,128)} %get-tuple-element.206.d_ref, ...), custom_call_target="tpu_custom_call" | custom-call | tf_op jit(solution)/shard_map/inner_back/pallas_call | solution.py:331
  339.6 18.2 %attend_back.2 = (bf16[1024,1536]{1,0:T(8,128)(2,1)S(1)}, f32[8,1536]{1,0:T(8,128)S(1)}) custom-call(bf16[1024,1536]{1,0:T(8,128)(2,1)S(1)} %fusion.query_ref.key_ref.value_ref, bf16[1024,1536]{1,0:T(8,128)(2,1)S(1)} %fusion.query_ref.key_ref.value_ref, bf16[1024,1536]{1,0:T(8,128)(2,1)S(1)} %fusion.query_ref.key_ref.value_ref, ...), custom_call_target="tpu_custom_call" | custom-call | tf_op jit(solution)/shard_map/attend_back/pallas_call | solution.py:136
  360.9 5.2 product.2
  375.7 3.4 fusion.17
  382.8 18.0 %attend_back.3 = (bf16[1024,1536]{1,0:T(8,128)(2,1)S(1)}, f32[8,1536]{1,0:T(8,128)S(1)}) custom-call(bf16[1024,1536]{1,0:T(8,128)(2,1)S(1)} %copy-done.3, bf16[1024,1536]{1,0:T(8,128)(2,1)S(1)} %copy-done.3, bf16[1024,1536]{1,0:T(8,128)(2,1)S(1)} %copy-done.3, bf16[1024,1024]{1,0:T(8,128)(2,1)S(1)} %copy-done.18, f32[8,2,512]{2,1,0:T(2,128)S(1)} %get-tuple-element.227.lse_ref), custom_call_target="tpu_custom_call" | custom-call | tf_op jit(solution)/shard_map/attend_back/pallas_call | solution.py:136
  400.9 4.4 fusion.10
  416.4 5.1 product.3
  430.3 3.3 fusion.6
  438.3 3.7 slice.158.w_ref
  442.1 7.9 %tokens_back.2.base_ref = f32[1024,1024]{1,0:T(8,128)} custom-call(f32[1024,1024]{1,0:T(8,128)} %get-tuple-element.208.base_ref, bf16[1024,1536]{1,0:T(8,128)(2,1)S(1)} %copy-done.9, bf16[1024,1536]{1,0:T(8,128)(2,1)} %slice.158.w_ref), custom_call_target="tpu_custom_call" | custom-call | tf_op jit(solution)/shard_map/tokens_back/pallas_call | solution.py:363
  461.7 7.2 %tokens_back.3 = bf16[1024,1024]{1,0:T(8,128)(2,1)} custom-call(f32[1024,1024]{1,0:T(8,128)} %tokens_back.2.base_ref, bf16[1024,1536]{1,0:T(8,128)(2,1)S(1)} %copy-done.13, bf16[1024,1536]{1,0:T(8,128)(2,1)} %copy-done.10), custom_call_target="tpu_custom_call" | custom-call | tf_op jit(solution)/shard_map/tokens_back/pallas_call | solution.py:363
  497.2 3.9 collective-permute-done.75
  502.7 6.7 %collective-permute-done.79 = bf16[80,1536]{1,0:T(8,128)(2,1)S(1)} collective-permute-done((bf16[80,1536]{1,0:T(8,128)(2,1)S(1)}, bf16[80,1536]{1,0:T(8,128)(2,1)S(1)}, u32[]{:S(2)}, u32[]{:S(2)}) %collective-permute-start.79) | collective-permute-done | bytes 245792 | tf_op jit(solution)/shard_map/ppermute | solution.py:562
  (431 shorter events, 201.0 us)
Async XLA Ops:
  7.2 73.1 %all-gather.3.cloned.1.call-start = ((), (), s32[]{:S(2)}) async-start(), calls=%async_computation | async-start | bytes 3514368 | tf_op jit(solution)/shard_map/all_gather | solution.py:622
  13.7 194.4 %all-gather.5.cloned.1.call-start = ((), (), s32[]{:S(2)}) async-start(), calls=%async_computation.1 | async-start | bytes 8650752 | tf_op jit(solution)/shard_map/all_gather | solution.py:622
  56.8 25.2 %collective-permute-start.22 = (bf16[64,1024]{1,0:T(8,128)(2,1)}, bf16[64,1024]{1,0:T(8,128)(2,1)}, u32[]{:S(2)}, u32[]{:S(2)}) collective-permute-start(bf16[64,1024]{1,0:T(8,128)(2,1)} %copy-done.76), channel_id=1, source_target_pairs={{0,8},{1,9},{2,10},{3,11},{4,12},{5,13},{6,14},{7,15},{8,0},{9,1},... | collective-permute-start | bytes 393224 | tf_op jit(solution)/shard_map/ppermute | solution.py:562
  56.8 27.7 %collective-permute-start.20 = (bf16[64,1024]{1,0:T(8,128)(2,1)}, bf16[64,1024]{1,0:T(8,128)(2,1)}, u32[]{:S(2)}, u32[]{:S(2)}) collective-permute-start(bf16[64,1024]{1,0:T(8,128)(2,1)} %copy-done.76), channel_id=1, source_target_pairs={{0,2},{2,4},{4,6},{6,7},{7,5},{5,3},{3,1},{1,0},{8,9},{10,8},{12,1... | collective-permute-start | bytes 393224 | tf_op jit(solution)/shard_map/ppermute | solution.py:555
  59.1 31.5 %collective-permute-start.23 = (bf16[64,1024]{1,0:T(8,128)(2,1)}, bf16[64,1024]{1,0:T(8,128)(2,1)}, u32[]{:S(2)}, u32[]{:S(2)}) collective-permute-start(bf16[64,1024]{1,0:T(8,128)(2,1)} %collective-permute-done.16.refs_6_), channel_id=1, source_target_pairs={{0,8},{1,9},{2,10},{3,11},{4,12},{5,13},{6,14},{7,15},{8,0},{9,1},... | collective-permute-start | bytes 393224 | tf_op jit(solution)/shard_map/ppermute | solution.py:562
  59.1 31.5 %collective-permute-start.21 = (bf16[64,1024]{1,0:T(8,128)(2,1)}, bf16[64,1024]{1,0:T(8,128)(2,1)}, u32[]{:S(2)}, u32[]{:S(2)}) collective-permute-start(bf16[64,1024]{1,0:T(8,128)(2,1)} %collective-permute-done.16.refs_6_), channel_id=1, source_target_pairs={{0,1},{2,0},{4,2},{6,4},{7,6},{5,7},{3,5},{1,3},{8,10},{10,12},{12... | collective-permute-start | bytes 393224 | tf_op jit(solution)/shard_map/ppermute | solution.py:555
  60.0 31.3 %collective-permute-start.25 = (bf16[256,1024]{1,0:T(8,128)(2,1)}, bf16[256,1024]{1,0:T(8,128)(2,1)}, u32[]{:S(2)}, u32[]{:S(2)}) collective-permute-start(bf16[256,1024]{1,0:T(8,128)(2,1)} %constant_dynamic-slice_fusion.1), channel_id=1, source_target_pairs={{0,1},{2,0},{4,2},{6,4},{7,6},{5,7},{3,5},{1,3},{8,10},{10,12},{12... | collective-permute-start | bytes 1572872 | tf_op jit(solution)/shard_map/ppermute | solution.py:555
  91.6 38.9 %collective-permute-start.31 = (bf16[256,1024]{1,0:T(8,128)(2,1)}, bf16[256,1024]{1,0:T(8,128)(2,1)}, u32[]{:S(2)}, u32[]{:S(2)}) collective-permute-start(bf16[256,1024]{1,0:T(8,128)(2,1)} %collective-permute-done.24.refs_1_), channel_id=1, source_target_pairs={{0,8},{1,9},{2,10},{3,11},{4,12},{5,13},{6,14},{7,15},{8,0},{9,1},... | collective-permute-start | bytes 1572872 | tf_op jit(solution)/shard_map/ppermute | solution.py:562
  91.8 38.7 %collective-permute-start.29 = (bf16[256,1024]{1,0:T(8,128)(2,1)}, bf16[256,1024]{1,0:T(8,128)(2,1)}, u32[]{:S(2)}, u32[]{:S(2)}) collective-permute-start(bf16[256,1024]{1,0:T(8,128)(2,1)} %collective-permute-done.24.refs_1_), channel_id=1, source_target_pairs={{0,2},{2,4},{4,6},{6,7},{7,5},{5,3},{3,1},{1,0},{8,9},{10,8},{12,1... | collective-permute-start | bytes 1572872 | tf_op jit(solution)/shard_map/ppermute | solution.py:555
  94.0 36.5 %collective-permute-start.32 = (bf16[256,1024]{1,0:T(8,128)(2,1)}, bf16[256,1024]{1,0:T(8,128)(2,1)}, u32[]{:S(2)}, u32[]{:S(2)}) collective-permute-start(bf16[256,1024]{1,0:T(8,128)(2,1)} %collective-permute-done.25.refs_2_), channel_id=1, source_target_pairs={{0,8},{1,9},{2,10},{3,11},{4,12},{5,13},{6,14},{7,15},{8,0},{9,1},... | collective-permute-start | bytes 1572872 | tf_op jit(solution)/shard_map/ppermute | solution.py:562
  94.0 36.5 %collective-permute-start.30 = (bf16[256,1024]{1,0:T(8,128)(2,1)}, bf16[256,1024]{1,0:T(8,128)(2,1)}, u32[]{:S(2)}, u32[]{:S(2)}) collective-permute-start(bf16[256,1024]{1,0:T(8,128)(2,1)} %collective-permute-done.25.refs_2_), channel_id=1, source_target_pairs={{0,1},{2,0},{4,2},{6,4},{7,6},{5,7},{3,5},{1,3},{8,10},{10,12},{12... | collective-permute-start | bytes 1572872 | tf_op jit(solution)/shard_map/ppermute | solution.py:555
  111.8 18.7 %collective-permute-start.28 = (bf16[64,1024]{1,0:T(8,128)(2,1)}, bf16[64,1024]{1,0:T(8,128)(2,1)}, u32[]{:S(2)}, u32[]{:S(2)}) collective-permute-start(bf16[64,1024]{1,0:T(8,128)(2,1)} %collective-permute-done.21.refs_10_), channel_id=1, source_target_pairs={{0,8},{1,9},{2,10},{3,11},{4,12},{5,13},{6,14},{7,15},{8,0},{9,1},... | collective-permute-start | bytes 393224 | tf_op jit(solution)/shard_map/ppermute | solution.py:562
  130.6 25.2 %collective-permute-start.34 = (bf16[256,1024]{1,0:T(8,128)(2,1)}, bf16[256,1024]{1,0:T(8,128)(2,1)S(1)}, u32[]{:S(2)}, u32[]{:S(2)}) collective-permute-start(bf16[256,1024]{1,0:T(8,128)(2,1)} %collective-permute-done.29.refs_5_), channel_id=1, source_target_pairs={{0,2},{2,4},{4,6},{6,7},{7,5},{5,3},{3,1},{1,0},{8,9},{10,8},{12,1... | collective-permute-start | bytes 1572872 | tf_op jit(solution)/shard_map/ppermute | solution.py:555
  132.3 23.5 %collective-permute-start.37 = (bf16[256,1024]{1,0:T(8,128)(2,1)}, bf16[256,1024]{1,0:T(8,128)(2,1)S(1)}, u32[]{:S(2)}, u32[]{:S(2)}) collective-permute-start(bf16[256,1024]{1,0:T(8,128)(2,1)} %collective-permute-done.30.refs_6_), channel_id=1, source_target_pairs={{0,8},{1,9},{2,10},{3,11},{4,12},{5,13},{6,14},{7,15},{8,0},{9,1},... | collective-permute-start | bytes 1572872 | tf_op jit(solution)/shard_map/ppermute | solution.py:562
  132.4 35.3 %collective-permute-start.35 = (bf16[256,1024]{1,0:T(8,128)(2,1)}, bf16[256,1024]{1,0:T(8,128)(2,1)S(1)}, u32[]{:S(2)}, u32[]{:S(2)}) collective-permute-start(bf16[256,1024]{1,0:T(8,128)(2,1)} %collective-permute-done.30.refs_6_), channel_id=1, source_target_pairs={{0,1},{2,0},{4,2},{6,4},{7,6},{5,7},{3,5},{1,3},{8,10},{10,12},{12... | collective-permute-start | bytes 1572872 | tf_op jit(solution)/shard_map/ppermute | solution.py:555
  264.1 17.5 %collective-permute-start.42 = (bf16[8,256,1024]{2,1,0:T(8,128)(2,1)}, bf16[8,256,1024]{2,1,0:T(8,128)(2,1)}, u32[]{:S(2)}, u32[]{:S(2)}) collective-permute-start(bf16[8,256,1024]{2,1,0:T(8,128)(2,1)} %dynamic-slice_bitcast_fusion.1), channel_id=1, source_target_pairs={{0,8},{1,9},{2,10},{3,11},{4,12},{5,13},{6,14},{7,15},{8,0},{9,1},... | collective-permute-start | bytes 12582920 | tf_op jit(solution)/shard_map/ppermute | solution.py:562
  299.3 29.2 %collective-permute-start.46 = (bf16[8,64,4096]{2,1,0:T(8,128)(2,1)}, bf16[8,64,4096]{2,1,0:T(8,128)(2,1)}, u32[]{:S(2)}, u32[]{:S(2)}) collective-permute-start(bf16[8,64,4096]{2,1,0:T(8,128)(2,1)} %dynamic-slice_bitcast_fusion), channel_id=1, source_target_pairs={{0,8},{1,9},{2,10},{3,11},{4,12},{5,13},{6,14},{7,15},{8,0},{9,1},... | collective-permute-start | bytes 12582920 | tf_op jit(solution)/shard_map/ppermute | solution.py:562
  302.9 25.6 %collective-permute-start.45 = (bf16[256,1024]{1,0:T(8,128)(2,1)}, bf16[256,1024]{1,0:T(8,128)(2,1)}, u32[]{:S(2)}, u32[]{:S(2)}) collective-permute-start(bf16[256,1024]{1,0:T(8,128)(2,1)} %get-tuple-element.275), channel_id=1, source_target_pairs={{0,1},{2,0},{4,2},{6,4},{7,6},{5,7},{3,5},{1,3},{8,10},{10,12},{12... | collective-permute-start | bytes 1572872 | tf_op jit(solution)/shard_map/ppermute | solution.py:555
  304.8 23.7 %collective-permute-start.44 = (bf16[256,1024]{1,0:T(8,128)(2,1)}, bf16[256,1024]{1,0:T(8,128)(2,1)}, u32[]{:S(2)}, u32[]{:S(2)}) collective-permute-start(bf16[256,1024]{1,0:T(8,128)(2,1)} %get-tuple-element.276), channel_id=1, source_target_pairs={{0,2},{2,4},{4,6},{6,7},{7,5},{5,3},{3,1},{1,0},{8,9},{10,8},{12,1... | collective-permute-start | bytes 1572872 | tf_op jit(solution)/shard_map/ppermute | solution.py:555
  330.6 29.5 %collective-permute-start.49 = (bf16[64,4096]{1,0:T(8,128)(2,1)S(1)}, bf16[64,4096]{1,0:T(8,128)(2,1)S(1)}, u32[]{:S(2)}, u32[]{:S(2)}) collective-permute-start(bf16[64,4096]{1,0:T(8,128)(2,1)S(1)} %fusion.23), channel_id=1, source_target_pairs={{0,2},{2,4},{4,6},{6,7},{7,5},{5,3},{3,1},{1,0},{8,9},{10,8},{12,1... | collective-permute-start | bytes 1572872 | tf_op jit(solution)/shard_map/ppermute | solution.py:555
  335.0 25.1 %collective-permute-start.48 = (bf16[256,1024]{1,0:T(8,128)(2,1)S(1)}, bf16[256,1024]{1,0:T(8,128)(2,1)S(1)}, u32[]{:S(2)}, u32[]{:S(2)}) collective-permute-start(bf16[256,1024]{1,0:T(8,128)(2,1)S(1)} %get-tuple-element.273), channel_id=1, source_target_pairs={{0,1},{2,0},{4,2},{6,4},{7,6},{5,7},{3,5},{1,3},{8,10},{10,12},{12... | collective-permute-start | bytes 1572872 | tf_op jit(solution)/shard_map/ppermute | solution.py:555
  335.3 24.9 %collective-permute-start.47 = (bf16[256,1024]{1,0:T(8,128)(2,1)S(1)}, bf16[256,1024]{1,0:T(8,128)(2,1)S(1)}, u32[]{:S(2)}, u32[]{:S(2)}) collective-permute-start(bf16[256,1024]{1,0:T(8,128)(2,1)S(1)} %get-tuple-element.274), channel_id=1, source_target_pairs={{0,2},{2,4},{4,6},{6,7},{7,5},{5,3},{3,1},{1,0},{8,9},{10,8},{12,1... | collective-permute-start | bytes 1572872 | tf_op jit(solution)/shard_map/ppermute | solution.py:555
  370.6 30.3 %collective-permute-start.54 = (bf16[8,64,2560]{2,1,0:T(8,128)(2,1)}, bf16[8,64,2560]{2,1,0:T(8,128)(2,1)}, u32[]{:S(2)}, u32[]{:S(2)}) collective-permute-start(bf16[8,64,2560]{2,1,0:T(8,128)(2,1)} %dynamic-slice_bitcast_fusion.2), channel_id=1, source_target_pairs={{0,8},{1,9},{2,10},{3,11},{4,12},{5,13},{6,14},{7,15},{8,0},{9,1},... | collective-permute-start | bytes 7864328 | tf_op jit(solution)/shard_map/ppermute | solution.py:562
  373.7 27.1 %collective-permute-start.53 = (bf16[64,4096]{1,0:T(8,128)(2,1)}, bf16[64,4096]{1,0:T(8,128)(2,1)}, u32[]{:S(2)}, u32[]{:S(2)}) collective-permute-start(bf16[64,4096]{1,0:T(8,128)(2,1)} %get-tuple-element.269), channel_id=1, source_target_pairs={{0,1},{2,0},{4,2},{6,4},{7,6},{5,7},{3,5},{1,3},{8,10},{10,12},{12... | collective-permute-start | bytes 1572872 | tf_op jit(solution)/shard_map/ppermute | solution.py:555
  373.9 26.9 %collective-permute-start.52 = (bf16[64,4096]{1,0:T(8,128)(2,1)}, bf16[64,4096]{1,0:T(8,128)(2,1)}, u32[]{:S(2)}, u32[]{:S(2)}) collective-permute-start(bf16[64,4096]{1,0:T(8,128)(2,1)} %get-tuple-element.270), channel_id=1, source_target_pairs={{0,2},{2,4},{4,6},{6,7},{7,5},{5,3},{3,1},{1,0},{8,9},{10,8},{12,1... | collective-permute-start | bytes 1572872 | tf_op jit(solution)/shard_map/ppermute | solution.py:555
  379.2 21.7 %collective-permute-start.51 = (bf16[256,1024]{1,0:T(8,128)(2,1)}, bf16[256,1024]{1,0:T(8,128)(2,1)}, u32[]{:S(2)}, u32[]{:S(2)}) collective-permute-start(bf16[256,1024]{1,0:T(8,128)(2,1)} %get-tuple-element.271), channel_id=1, source_target_pairs={{0,1},{2,0},{4,2},{6,4},{7,6},{5,7},{3,5},{1,3},{8,10},{10,12},{12... | collective-permute-start | bytes 1572872 | tf_op jit(solution)/shard_map/ppermute | solution.py:555
  379.3 21.5 %collective-permute-start.50 = (bf16[256,1024]{1,0:T(8,128)(2,1)}, bf16[256,1024]{1,0:T(8,128)(2,1)}, u32[]{:S(2)}, u32[]{:S(2)}) collective-permute-start(bf16[256,1024]{1,0:T(8,128)(2,1)} %get-tuple-element.272), channel_id=1, source_target_pairs={{0,2},{2,4},{4,6},{6,7},{7,5},{5,3},{3,1},{1,0},{8,9},{10,8},{12,1... | collective-permute-start | bytes 1572872 | tf_op jit(solution)/shard_map/ppermute | solution.py:555
  424.3 27.4 %collective-permute-start.59 = (bf16[256,1024]{1,0:T(8,128)(2,1)}, bf16[256,1024]{1,0:T(8,128)(2,1)}, u32[]{:S(2)}, u32[]{:S(2)}) collective-permute-start(bf16[256,1024]{1,0:T(8,128)(2,1)} %add_convert_fusion.3), channel_id=1, source_target_pairs={{0,8},{1,9},{2,10},{3,11},{4,12},{5,13},{6,14},{7,15},{8,0},{9,1},... | collective-permute-start | bytes 1572872 | tf_op jit(solution)/shard_map/ppermute | solution.py:562
  427.3 24.4 %collective-permute-start.64 = (bf16[8,80,1536]{2,1,0:T(8,128)(2,1)}, bf16[8,80,1536]{2,1,0:T(8,128)(2,1)}, u32[]{:S(2)}, u32[]{:S(2)}) collective-permute-start(bf16[8,80,1536]{2,1,0:T(8,128)(2,1)} %dynamic-slice_bitcast_fusion.3), channel_id=1, source_target_pairs={{0,8},{1,9},{2,10},{3,11},{4,12},{5,13},{6,14},{7,15},{8,0},{9,1},... | collective-permute-start | bytes 5898248 | tf_op jit(solution)/shard_map/ppermute | solution.py:562
  433.6 18.1 %collective-permute-start.61 = (bf16[64,4096]{1,0:T(8,128)(2,1)}, bf16[64,4096]{1,0:T(8,128)(2,1)}, u32[]{:S(2)}, u32[]{:S(2)}) collective-permute-start(bf16[64,4096]{1,0:T(8,128)(2,1)} %get-tuple-element.265), channel_id=1, source_target_pairs={{0,1},{2,0},{4,2},{6,4},{7,6},{5,7},{3,5},{1,3},{8,10},{10,12},{12... | collective-permute-start | bytes 1572872 | tf_op jit(solution)/shard_map/ppermute | solution.py:555
  452.8 17.6 %collective-permute-start.68 = (bf16[80,1536]{1,0:T(8,128)(2,1)S(1)}, bf16[80,1536]{1,0:T(8,128)(2,1)S(1)}, u32[]{:S(2)}, u32[]{:S(2)}) collective-permute-start(bf16[80,1536]{1,0:T(8,128)(2,1)S(1)} %fusion.62), channel_id=1, source_target_pairs={{0,2},{2,4},{4,6},{6,7},{7,5},{5,3},{3,1},{1,0},{8,9},{10,8},{12,1... | collective-permute-start | bytes 737288 | tf_op jit(solution)/shard_map/ppermute | solution.py:555
  477.4 17.6 %collective-permute-start.81 = (bf16[64,4096]{1,0:T(8,128)(2,1)S(1)}, bf16[64,4096]{1,0:T(8,128)(2,1)S(1)}, u32[]{:S(2)}, u32[]{:S(2)}) collective-permute-start(bf16[64,4096]{1,0:T(8,128)(2,1)S(1)} %add_convert_fusion.2), channel_id=1, source_target_pairs={{0,8},{1,9},{2,10},{3,11},{4,12},{5,13},{6,14},{7,15},{8,0},{9,1},... | collective-permute-start | bytes 1572872 | tf_op jit(solution)/shard_map/ppermute | solution.py:562
  (155 other events, 1736.3 us)
Sparse Core Ops, SparseCore 0:
  13.8 66.4 all-gather.2
  83.2 87.2 all-gather.4

commit v2 on v0

--- a/solution.py
+++ b/solution.py
@@ -150,7 +150,7 @@
     )(qkv, qkv, qkv, d_attended, lse)
 
 
-ROWS = 256
+ROWS = 512
 COLUMNS = 512
 EXTRA = 16
 PARTS = 2
@@ -297,9 +297,8 @@
 
 
 def inner_back_kernel(
-    d_pre_ref, w_ref, d_ref, unit_ref, inverse_ref, vec_ref, w_out_ref, before_ref, *refs
+    d_pre_ref, w_ref, d_ref, unit_ref, inverse_ref, vec_ref, w_out_ref, out_ref, low_ref, attended_ref, sum_ref, total_ref
 ):
-    out_ref, low_ref, attended_ref, sum_ref, total_ref = refs[-5:]
     step = pl.program_id(0)
     part = against(d_pre_ref[...], w_ref[...])
 
@@ -313,8 +312,8 @@
 
     @pl.when(step == pl.num_programs(0) - 1)
     def _():
-        sum_ref[...] = before_ref[...]
-        for rows in pieces(total_ref.shape[0], 2):
+        sum_ref[...] = jnp.zeros_like(sum_ref)
+        for rows in pieces(total_ref.shape[0], 4):
             d_first = total_ref[rows, :]
             unit = unit_ref[rows, :]
             d_inner = normal_back(d_first * line(vec_ref, GAIN_ONE), unit, inverse_ref[rows, 0:1])
@@ -327,39 +326,31 @@
             add_line(sum_ref, 2, d_inner)
 
 
-def inner_back(part, d_pre, w_inner, d_second, unit, inverse, vec, w_out, sums, before):
+def inner_back(d_pre, w_inner, d_second, unit, inverse, vec, w_out):
     count, hidden = d_pre.shape
-    rows = count // 2
-
-    def own(width):
-        return pl.BlockSpec((rows, width), lambda i: (part, 0), pipeline_mode=pl.Buffered(1))
-
     return pl.pallas_call(
         inner_back_kernel,
-        grid=(hidden // COLUMNS,),
+        grid=(hidden // D,),
         in_specs=[
-            pl.BlockSpec((rows, COLUMNS), lambda i: (part, i)),
-            columns_of(D),
-            own(D),
-            own(D),
-            own(LANES),
+            pl.BlockSpec((count, D), lambda i: (0, i)),
+            pl.BlockSpec((D, D), lambda i: (0, i)),
+            kept((count, D)),
+            kept((count, D)),
+            kept((count, LANES)),
             kept((8, D)),
             kept((D, D)),
-            kept((8, D)),
-        ]
-        + [pl.BlockSpec(memory_space=pl.ANY)] * len(before),
-        out_specs=[own(D), own(D), own(D), kept((8, D))],
+        ],
+        out_specs=[kept((count, D)), kept((count, D)), kept((count, D)), kept((8, D))],
         out_shape=[
             jax.ShapeDtypeStruct((count, D), FULL),
             jax.ShapeDtypeStruct((count, D), LOW),
             jax.ShapeDtypeStruct((count, D), LOW),
             jax.ShapeDtypeStruct((8, D), FULL),
         ],
-        input_output_aliases={8 + i: i for i in range(len(before))},
-        scratch_shapes=[pltpu.VMEM((rows, D), FULL)],
+        scratch_shapes=[pltpu.VMEM((count, D), FULL)],
         compiler_params=LIMIT,
         name="inner_back",
-    )(d_pre, w_inner, d_second, unit, inverse, vec, w_out, sums, *before)
+    )(d_pre, w_inner, d_second, unit, inverse, vec, w_out)
 
 
 def tokens_kernel(base_ref, d_ref, w_ref, out_ref):
@@ -754,9 +745,9 @@
     flow.advance()
     own_groups[1] = flow.advance(own_groups[1])
     flow.start("group1", links.gather(own_groups[1]))
-    tokens_turned, w_out = flow.advance(turn(tokens), w_out)
+    w_out = flow.advance(w_out)
     flow.start("out", links.gather(w_out))
-    flow.advance()
+    tokens_turned = flow.advance(turn(tokens))
     if ride:
         first_group, chunks, owners = flow.take("group0")
         vec, bias_inner, bias_groups = unpack(chunks, owners, width // 2, size * hidden)
@@ -791,13 +782,10 @@
     d_pre = flow.advance(d_pre)
     grad_inner, d_pre = flow.advance(gram(first_low, d_pre).astype(LOW), d_pre)
     flow.start("inner_back", links.reduce(grad_inner))
-    sums_one, before = jnp.zeros((8, D), FULL), []
-    for part in range(2):
-        *before, sums_one = inner_back(
-            part, d_pre, whole_inner, d_second, unit_one, inverse_one, vec, whole_out, sums_one, before
-        )
-        before[0], sums_one = flow.advance(before[0], sums_one)
-    d_inner, d_branch, d_attended = before
+    d_inner, d_branch, d_attended, sums_one = inner_back(
+        d_pre, whole_inner, d_second, unit_one, inverse_one, vec, whole_out
+    )
+    d_branch, d_attended = flow.advance(d_branch, d_attended)
     grad_out, d_attended = tie(gram(attended, d_branch).astype(LOW), d_attended)
 
     d_groups, sums_group = [], []

time: 513 us -> 500 us (0.975)
  Pallas kernels: 197 us -> 185 us
  local copies, waits for them, and re-layouts: 61.8 us -> 55.7 us
    pallas_call x2 -> x1, Pallas kernels: 32 us -> 22.7 us  [inner_back(): pl.pallas_call(inner_back_kernel, grid=(hidden // D,), in_specs=[pl.Block...]
    ppermute x49, waiting for transfers between devices: 61 us -> 66.8 us  [hop(): return lax.ppermute(values, AXES, pairs)]
    unnamed x184 -> x162, local copies, waits for them, and re-layouts: 43.8 us -> 38.5 us
  transfers between devices with their start and end apart: 84 -> 84, of which waited for: 23 -> 21; matrix products, arithmetic and copies ran while one was open for 12% -> 13% of each run, Pallas kernels for 34% -> 32%
where the time goes in v2:
time: 500 us; the launch traced here: 492 us
  Pallas kernels  185 us (37%)
  waiting for transfers between devices  73.4 us (15%)
  starting transfers between devices  70.9 us (14%)
  other arithmetic  56.7 us (11%)
  local copies, waits for them, and re-layouts  55.7 us (11%)
  matrix products  34.4 us (7%)
  between operations  15.7 us (3%)
    ppermute x49, waiting for transfers between devices, hop(): return lax.ppermute(values, AXES, pairs)  66.8 us
    ppermute x49, starting transfers between devices, hop(): return lax.ppermute(values, AXES, pairs)  58.4 us
    unnamed x162, local copies, waits for them, and re-layouts  38.5 us
    pallas_call x2, Pallas kernels, attend_back(): pl.pallas_call(attend_back_kernel, grid=(count // SEQ, PAIRS), in_specs=t...  36.2 us
    dot_general x3, matrix products, gram(): lax.dot_general(left, right, (((0,), (0,)), ((), ())), preferred_element_...  25.9 us
    pallas_call x1, Pallas kernels, inner_back(): pl.pallas_call(inner_back_kernel, grid=(hidden // D,), in_specs=[pl.Block...  22.7 us
    pallas_call x2, Pallas kernels, attend(): pl.pallas_call(attend_kernel, grid=(seqs, PAIRS), in_specs=triple() + [pl...  22.6 us
    pallas_call x1, Pallas kernels, inner_gelu(): pl.pallas_call(inner_kernel, grid=(hidden // COLUMNS,), in_specs=[kept((c...  18.9 us
  transfers between devices with their start and end apart: 84, of which 21 were waited for; matrix products, arithmetic and copies ran while one was open for 13% of the time, Pallas kernels for 32%

profile of v2, /device:TPU:0, one launch (start us, length us, event | category | flops | bytes accessed | tf_op | source)
XLA Modules:
  0.0 491.9 jit_solution(7181554911076670207)
XLA Ops:
  19.4 6.2 %collective-permute-done.1.refs_2_ = bf16[80,1536]{1,0:T(8,128)(2,1)S(1)} collective-permute-done((bf16[80,1536]{1,0:T(8,128)(2,1)S(1)}, bf16[80,1536]{1,0:T(8,128)(2,1)S(1)}, u32[]{:S(2)}, u32[]{:S(2)}) %collective-permute-start.1) | collective-permute-done | bytes 245792 | tf_op jit(solution)/shard_map/ppermute | solution.py:554
  29.0 7.1 %collective-permute-done.2.refs_5_.refs_3_ = bf16[80,1536]{1,0:T(8,128)(2,1)S(1)} collective-permute-done((bf16[80,1536]{1,0:T(8,128)(2,1)S(1)}, bf16[80,1536]{1,0:T(8,128)(2,1)S(1)}, u32[]{:S(2)}, u32[]{:S(2)}) %collective-permute-start.2) | collective-permute-done | bytes 245792 | tf_op jit(solution)/shard_map/ppermute | solution.py:554
  48.9 8.2 %collective-permute-done.10.refs_1_ = bf16[64,1536]{1,0:T(8,128)(2,1)S(1)} collective-permute-done((bf16[64,1536]{1,0:T(8,128)(2,1)S(1)}, bf16[64,1536]{1,0:T(8,128)(2,1)S(1)}, u32[]{:S(2)}, u32[]{:S(2)}) %collective-permute-start.10) | collective-permute-done | bytes 196640 | tf_op jit(solution)/shard_map/ppermute | solution.py:554
  65.2 4.5 collective-permute-done.20.refs_2_
  76.8 11.6 %collective-permute-done.16.refs_6_ = bf16[64,1536]{1,0:T(8,128)(2,1)} collective-permute-done((bf16[64,1536]{1,0:T(8,128)(2,1)}, bf16[64,1536]{1,0:T(8,128)(2,1)}, u32[]{:S(2)}, u32[]{:S(2)}) %collective-permute-start.16) | collective-permute-done | bytes 196640 | tf_op jit(solution)/shard_map/ppermute | solution.py:554
  98.1 5.2 %assemble.3.w_ref = bf16[1024,1536]{1,0:T(8,128)(2,1)S(1)} custom-call(s32[15]{0:T(128)S(1)} %stack.122.place_ref, bf16[128,1536]{1,0:T(8,128)(2,1)S(1)} %pad_maximum_fusion.4.refs_0_, bf16[80,1536]{1,0:T(8,128)(2,1)S(1)} %collective-permute-done.refs_1_, bf16[80,1536]{1,0:T(8,128)(2,1)S(1)} %collective-permute-done.1.refs_2_, ...), custom_call_target="tpu_custom_call" | custom-call | tf_op jit(solution)/shard_map/assemble/pallas_call | solution.py:439
  105.8 3.6 fusion.query_ref.key_ref.value_ref
  118.4 11.3 %attend.2 = (bf16[1024,1024]{1,0:T(8,128)(2,1)S(1)}, f32[8,2,512]{2,1,0:T(2,128)S(1)}) custom-call(bf16[1024,1536]{1,0:T(8,128)(2,1)S(1)} %fusion.query_ref.key_ref.value_ref, bf16[1024,1536]{1,0:T(8,128)(2,1)S(1)} %fusion.query_ref.key_ref.value_ref, bf16[1024,1536]{1,0:T(8,128)(2,1)S(1)} %fusion.query_ref.key_ref.value_ref), custom_call_target="tpu_custom_call" | custom-call | tf_op jit(solution)/shard_map/attend/pallas_call | solution.py:119
  131.3 3.9 assemble.4.w_ref
  135.2 4.8 fusion.1.query_ref.key_ref.value_ref
  145.1 11.3 %attend.3 = (bf16[1024,1024]{1,0:T(8,128)(2,1)S(1)}, f32[8,2,512]{2,1,0:T(2,128)S(1)}) custom-call(bf16[1024,1536]{1,0:T(8,128)(2,1)S(1)} %copy-done.2, bf16[1024,1536]{1,0:T(8,128)(2,1)S(1)} %copy-done.2, bf16[1024,1536]{1,0:T(8,128)(2,1)S(1)} %copy-done.2, bf16[1024,1024]{1,0:T(8,128)(2,1)S(1)} %copy-done.15), custom_call_target="tpu_custom_call", output_to_operand_aliasing={{0}: (3, {})} | custom-call | tf_op jit(solution)/shard_map/attend/pallas_call | solution.py:119
  162.5 6.7 %out_norm.1 = (f32[1024,1024]{1,0:T(8,128)}, f32[1024,128]{1,0:T(8,128)S(1)}, bf16[1024,1024]{1,0:T(8,128)(2,1)S(1)}) custom-call(bf16[1024,1024]{1,0:T(8,128)(2,1)S(1)} %copy-done.17, bf16[1024,1024]{1,0:T(8,128)(2,1)} %copy-done.6, bf16[1024,1024]{1,0:T(8,128)(2,1)} %tokens_ref.1, f32[8,1024]{1,0:T(8,128)S(1)} %copy-done.32), custom_call_target="tpu_custom_call" | custom-call | tf_op jit(solution)/shard_map/out_norm/pallas_call | solution.py:205
  173.0 18.9 %inner_gelu.1 = (bf16[1024,4096]{1,0:T(8,128)(2,1)}, bf16[1024,4096]{1,0:T(8,128)(2,1)}) custom-call(bf16[1024,1024]{1,0:T(8,128)(2,1)S(1)} %copy-done.22, bf16[1024,4096]{1,0:T(8,128)(2,1)} %all-gather.3.cloned.1.call-done.w_ref, f32[1,4096]{1,0:T(1,128)S(1)} %get-tuple-element.193.bias_ref), custom_call_target="tpu_custom_call" | custom-call | tf_op jit(solution)/shard_map/inner_gelu/pallas_call | solution.py:230
  193.5 18.6 %outer_norms.1 = (bf16[1024,1024]{1,0:T(8,128)(2,1)}, f32[1024,1024]{1,0:T(8,128)}, bf16[1024,1024]{1,0:T(8,128)(2,1)S(1)}, f32[8,1024]{1,0:T(8,128)S(1)}) custom-call(bf16[1024,4096]{1,0:T(8,128)(2,1)} %get-tuple-element.194.active_ref, bf16[4096,1024]{1,0:T(8,128)(2,1)} %all-gather.5.cloned.1.call-done.w_ref, f32[1024,1024]{1,0:T(8,128)} %get-tuple-element.196.unit_ref, ...), custom_call_target="tpu_custom_call" | custom-call | tf_op jit(solution)/shard_map/outer_norms/pallas_call | solution.py:259
  212.1 12.1 %convolution_convert_fusion.1 = bf16[4096,1024]{1,0:T(8,128)(2,1)S(1)} fusion(bf16[1024,4096]{1,0:T(8,128)(2,1)} %get-tuple-element.194.active_ref, bf16[1024,1024]{1,0:T(8,128)(2,1)S(1)} %get-tuple-element.199.d_ref), kind=kOutput, calls=%fused_computation.1 | convolution fusion | flops 8594128896 | bytes 18874368 | tf_op jit(solution)/shard_map/dot_general | solution.py:29
  224.3 3.4 copy-done.70
  232.1 15.5 %outer_back.1 = (bf16[1024,4096]{1,0:T(8,128)(2,1)}, f32[1,4096]{1,0:T(1,128)S(1)}) custom-call(bf16[1024,1024]{1,0:T(8,128)(2,1)S(1)} %copy-done.25, bf16[4096,1024]{1,0:T(8,128)(2,1)} %all-gather.5.cloned.1.call-done.w_ref, bf16[1024,4096]{1,0:T(8,128)(2,1)} %get-tuple-element.200.slope_ref), custom_call_target="tpu_custom_call" | custom-call | tf_op jit(solution)/shard_map/outer_back/pallas_call | solution.py:285
  250.5 11.4 %convolution_convert_fusion = bf16[1024,4096]{1,0:T(8,128)(2,1)S(1)} fusion(bf16[1024,1024]{1,0:T(8,128)(2,1)S(1)} %copy-done.23, bf16[1024,4096]{1,0:T(8,128)(2,1)} %get-tuple-element.205.d_pre_ref), kind=kOutput, calls=%fused_computation | convolution fusion | flops 8594128896 | bytes 18874368 | tf_op jit(solution)/shard_map/dot_general | solution.py:29
  273.7 22.7 %inner_back.1 = (f32[1024,1024]{1,0:T(8,128)}, bf16[1024,1024]{1,0:T(8,128)(2,1)S(1)}, bf16[1024,1024]{1,0:T(8,128)(2,1)S(1)}, f32[8,1024]{1,0:T(8,128)S(1)}) custom-call(bf16[1024,4096]{1,0:T(8,128)(2,1)} %get-tuple-element.205.d_pre_ref, bf16[1024,4096]{1,0:T(8,128)(2,1)} %all-gather.3.cloned.1.call-done.w_ref, f32[1024,1024]{1,0:T(8,128)} %get-tuple-element.206.d_ref, ...), custom_call_target="tpu_custom_call" | custom-call | tf_op jit(solution)/shard_map/inner_back/pallas_call | solution.py:331
  306.4 18.2 %attend_back.2 = (bf16[1024,1536]{1,0:T(8,128)(2,1)S(1)}, f32[8,1536]{1,0:T(8,128)S(1)}) custom-call(bf16[1024,1536]{1,0:T(8,128)(2,1)S(1)} %fusion.query_ref.key_ref.value_ref, bf16[1024,1536]{1,0:T(8,128)(2,1)S(1)} %fusion.query_ref.key_ref.value_ref, bf16[1024,1536]{1,0:T(8,128)(2,1)S(1)} %fusion.query_ref.key_ref.value_ref, ...), custom_call_target="tpu_custom_call" | custom-call | tf_op jit(solution)/shard_map/attend_back/pallas_call | solution.py:136
  327.2 5.2 %product.2 = bf16[1024,1536]{1,0:T(8,128)(2,1)S(1)} custom-call(bf16[1024,1024]{1,0:T(8,128)(2,1)S(1)} %copy-done.4, bf16[1024,1536]{1,0:T(8,128)(2,1)} %copy-done.8), custom_call_target="tpu_custom_call" | custom-call | tf_op jit(solution)/shard_map/product/pallas_call | solution.py:413
  335.0 3.4 dynamic-slice_bitcast_fusion.2
  343.6 3.4 fusion.17
  350.6 18.0 %attend_back.3 = (bf16[1024,1536]{1,0:T(8,128)(2,1)S(1)}, f32[8,1536]{1,0:T(8,128)S(1)}) custom-call(bf16[1024,1536]{1,0:T(8,128)(2,1)S(1)} %copy-done.3, bf16[1024,1536]{1,0:T(8,128)(2,1)S(1)} %copy-done.3, bf16[1024,1536]{1,0:T(8,128)(2,1)S(1)} %copy-done.3, bf16[1024,1024]{1,0:T(8,128)(2,1)S(1)} %copy-done.20, f32[8,2,512]{2,1,0:T(2,128)S(1)} %get-tuple-element.227.lse_ref), custom_call_target="tpu_custom_call" | custom-call | tf_op jit(solution)/shard_map/attend_back/pallas_call | solution.py:136
  371.0 3.4 fusion.10
  387.6 5.1 %product.3 = bf16[1280,1536]{1,0:T(8,128)(2,1)} custom-call(bf16[1024,1024]{1,0:T(8,128)(2,1)S(1)} %copy-done.5, bf16[1024,1536]{1,0:T(8,128)(2,1)S(1)} %copy-done.12, f32[8,1536]{1,0:T(8,128)S(1)} %copy-done.39), custom_call_target="tpu_custom_call" | custom-call | tf_op jit(solution)/shard_map/product/pallas_call | solution.py:413
  408.6 7.7 %tokens_back.2.base_ref = f32[1024,1024]{1,0:T(8,128)} custom-call(f32[1024,1024]{1,0:T(8,128)} %get-tuple-element.208.base_ref, bf16[1024,1536]{1,0:T(8,128)(2,1)S(1)} %copy-done.9, bf16[1024,1536]{1,0:T(8,128)(2,1)} %copy-done.7), custom_call_target="tpu_custom_call" | custom-call | tf_op jit(solution)/shard_map/tokens_back/pallas_call | solution.py:363
  416.4 5.8 %collective-permute-done.62 = bf16[64,2560]{1,0:T(8,128)(2,1)} collective-permute-done((bf16[64,2560]{1,0:T(8,128)(2,1)}, bf16[64,2560]{1,0:T(8,128)(2,1)}, u32[]{:S(2)}, u32[]{:S(2)}) %collective-permute-start.62) | collective-permute-done | bytes 327712 | tf_op jit(solution)/shard_map/ppermute | solution.py:554
  433.2 7.2 %tokens_back.3 = bf16[1024,1024]{1,0:T(8,128)(2,1)} custom-call(f32[1024,1024]{1,0:T(8,128)} %tokens_back.2.base_ref, bf16[1024,1536]{1,0:T(8,128)(2,1)S(1)} %copy-done.13, bf16[1024,1536]{1,0:T(8,128)(2,1)} %copy-done.10), custom_call_target="tpu_custom_call" | custom-call | tf_op jit(solution)/shard_map/tokens_back/pallas_call | solution.py:363
  455.7 3.5 collective-permute-done.69
  468.4 3.5 collective-permute-done.75
  473.8 5.5 %collective-permute-done.79 = bf16[80,1536]{1,0:T(8,128)(2,1)S(1)} collective-permute-done((bf16[80,1536]{1,0:T(8,128)(2,1)S(1)}, bf16[80,1536]{1,0:T(8,128)(2,1)S(1)}, u32[]{:S(2)}, u32[]{:S(2)}) %collective-permute-start.79) | collective-permute-done | bytes 245792 | tf_op jit(solution)/shard_map/ppermute | solution.py:561
  (386 shorter events, 199.3 us)
Async XLA Ops:
  7.2 164.2 %all-gather.3.cloned.1.call-start = ((), (), s32[]{:S(2)}) async-start(), calls=%async_computation | async-start | bytes 8650752 | tf_op jit(solution)/shard_map/all_gather | solution.py:624
  14.5 177.4 %all-gather.5.cloned.1.call-start = ((), (), s32[]{:S(2)}) async-start(), calls=%async_computation.1 | async-start | bytes 8650752 | tf_op jit(solution)/shard_map/all_gather | solution.py:624
  40.6 16.5 %collective-permute-start.8 = (bf16[80,1536]{1,0:T(8,128)(2,1)S(1)}, bf16[80,1536]{1,0:T(8,128)(2,1)S(1)}, u32[]{:S(2)}, u32[]{:S(2)}) collective-permute-start(bf16[80,1536]{1,0:T(8,128)(2,1)S(1)} %collective-permute-done.2.refs_5_.refs_3_), channel_id=1, source_target_pairs={{0,8},{1,9},{2,10},{3,11},{4,12},{5,13},{6,14},{7,15},{8,0},{9,1},... | collective-permute-start | bytes 737288 | tf_op jit(solution)/shard_map/ppermute | solution.py:561
  40.7 17.1 %collective-permute-start.6 = (bf16[80,1536]{1,0:T(8,128)(2,1)S(1)}, bf16[80,1536]{1,0:T(8,128)(2,1)S(1)}, u32[]{:S(2)}, u32[]{:S(2)}) collective-permute-start(bf16[80,1536]{1,0:T(8,128)(2,1)S(1)} %collective-permute-done.2.refs_5_.refs_3_), channel_id=1, source_target_pairs={{0,2},{2,4},{4,6},{6,7},{7,5},{5,3},{3,1},{1,0},{8,9},{10,8},{12,1... | collective-permute-start | bytes 737288 | tf_op jit(solution)/shard_map/ppermute | solution.py:554
  65.2 23.3 %collective-permute-start.13 = (bf16[80,1536]{1,0:T(8,128)(2,1)S(1)}, bf16[80,1536]{1,0:T(8,128)(2,1)S(1)}, u32[]{:S(2)}, u32[]{:S(2)}) collective-permute-start(bf16[80,1536]{1,0:T(8,128)(2,1)S(1)} %collective-permute-done.6.refs_9_.refs_5_), channel_id=1, source_target_pairs={{0,8},{1,9},{2,10},{3,11},{4,12},{5,13},{6,14},{7,15},{8,0},{9,1},... | collective-permute-start | bytes 737288 | tf_op jit(solution)/shard_map/ppermute | solution.py:561
  69.6 19.5 %collective-permute-start.12 = (bf16[80,1536]{1,0:T(8,128)(2,1)S(1)}, bf16[80,1536]{1,0:T(8,128)(2,1)S(1)}, u32[]{:S(2)}, u32[]{:S(2)}) collective-permute-start(bf16[80,1536]{1,0:T(8,128)(2,1)S(1)} %collective-permute-done.6.refs_9_.refs_5_), channel_id=1, source_target_pairs={{0,2},{2,4},{4,6},{6,7},{7,5},{5,3},{3,1},{1,0},{8,9},{10,8},{12,1... | collective-permute-start | bytes 737288 | tf_op jit(solution)/shard_map/ppermute | solution.py:554
  71.3 17.9 %collective-permute-start.14 = (bf16[80,1536]{1,0:T(8,128)(2,1)S(1)}, bf16[80,1536]{1,0:T(8,128)(2,1)}, u32[]{:S(2)}, u32[]{:S(2)}) collective-permute-start(bf16[80,1536]{1,0:T(8,128)(2,1)S(1)} %collective-permute-done.7.refs_10_.refs_6_), channel_id=1, source_target_pairs={{0,8},{1,9},{2,10},{3,11},{4,12},{5,13},{6,14},{7,15},{8,0},{9,1},... | collective-permute-start | bytes 737288 | tf_op jit(solution)/shard_map/ppermute | solution.py:561
  72.5 16.0 %collective-permute-start.16 = (bf16[64,1536]{1,0:T(8,128)(2,1)}, bf16[64,1536]{1,0:T(8,128)(2,1)}, u32[]{:S(2)}, u32[]{:S(2)}) collective-permute-start(bf16[64,1536]{1,0:T(8,128)(2,1)} %collective-permute-done.11.refs_2_), channel_id=1, source_target_pairs={{0,1},{2,0},{4,2},{6,4},{7,6},{5,7},{3,5},{1,3},{8,10},{10,12},{12... | collective-permute-start | bytes 589832 | tf_op jit(solution)/shard_map/ppermute | solution.py:554
  89.2 16.3 %collective-permute-start.26 = (bf16[64,1024]{1,0:T(8,128)(2,1)}, bf16[64,1024]{1,0:T(8,128)(2,1)}, u32[]{:S(2)}, u32[]{:S(2)}) collective-permute-start(bf16[64,1024]{1,0:T(8,128)(2,1)} %collective-permute-done.19.refs_1_), channel_id=1, source_target_pairs={{0,2},{2,4},{4,6},{6,7},{7,5},{5,3},{3,1},{1,0},{8,9},{10,8},{12,1... | collective-permute-start | bytes 393224 | tf_op jit(solution)/shard_map/ppermute | solution.py:554
  92.1 17.4 %collective-permute-start.27 = (bf16[64,1024]{1,0:T(8,128)(2,1)}, bf16[64,1024]{1,0:T(8,128)(2,1)S(1)}, u32[]{:S(2)}, u32[]{:S(2)}) collective-permute-start(bf16[64,1024]{1,0:T(8,128)(2,1)} %collective-permute-done.20.refs_2_), channel_id=1, source_target_pairs={{0,1},{2,0},{4,2},{6,4},{7,6},{5,7},{3,5},{1,3},{8,10},{10,12},{12... | collective-permute-start | bytes 393224 | tf_op jit(solution)/shard_map/ppermute | solution.py:554
  113.5 16.3 %collective-permute-start.31 = (bf16[64,1536]{1,0:T(8,128)(2,1)S(1)}, bf16[64,1536]{1,0:T(8,128)(2,1)S(1)}, u32[]{:S(2)}, u32[]{:S(2)}) collective-permute-start(bf16[64,1536]{1,0:T(8,128)(2,1)S(1)} %collective-permute-done.22.refs_9_), channel_id=1, source_target_pairs={{0,8},{1,9},{2,10},{3,11},{4,12},{5,13},{6,14},{7,15},{8,0},{9,1},... | collective-permute-start | bytes 589832 | tf_op jit(solution)/shard_map/ppermute | solution.py:561
  113.5 16.3 %collective-permute-start.30 = (bf16[64,1536]{1,0:T(8,128)(2,1)S(1)}, bf16[64,1536]{1,0:T(8,128)(2,1)S(1)}, u32[]{:S(2)}, u32[]{:S(2)}) collective-permute-start(bf16[64,1536]{1,0:T(8,128)(2,1)S(1)} %collective-permute-done.22.refs_9_), channel_id=1, source_target_pairs={{0,2},{2,4},{4,6},{6,7},{7,5},{5,3},{3,1},{1,0},{8,9},{10,8},{12,1... | collective-permute-start | bytes 589832 | tf_op jit(solution)/shard_map/ppermute | solution.py:554
  230.1 17.5 %collective-permute-start.42 = (bf16[8,256,1024]{2,1,0:T(8,128)(2,1)}, bf16[8,256,1024]{2,1,0:T(8,128)(2,1)}, u32[]{:S(2)}, u32[]{:S(2)}) collective-permute-start(bf16[8,256,1024]{2,1,0:T(8,128)(2,1)} %dynamic-slice_bitcast_fusion.1), channel_id=1, source_target_pairs={{0,8},{1,9},{2,10},{3,11},{4,12},{5,13},{6,14},{7,15},{8,0},{9,1},... | collective-permute-start | bytes 12582920 | tf_op jit(solution)/shard_map/ppermute | solution.py:561
  267.5 29.0 %collective-permute-start.46 = (bf16[8,64,4096]{2,1,0:T(8,128)(2,1)}, bf16[8,64,4096]{2,1,0:T(8,128)(2,1)}, u32[]{:S(2)}, u32[]{:S(2)}) collective-permute-start(bf16[8,64,4096]{2,1,0:T(8,128)(2,1)} %dynamic-slice_bitcast_fusion), channel_id=1, source_target_pairs={{0,8},{1,9},{2,10},{3,11},{4,12},{5,13},{6,14},{7,15},{8,0},{9,1},... | collective-permute-start | bytes 12582920 | tf_op jit(solution)/shard_map/ppermute | solution.py:561
  270.6 25.8 %collective-permute-start.45 = (bf16[256,1024]{1,0:T(8,128)(2,1)}, bf16[256,1024]{1,0:T(8,128)(2,1)}, u32[]{:S(2)}, u32[]{:S(2)}) collective-permute-start(bf16[256,1024]{1,0:T(8,128)(2,1)} %get-tuple-element.275), channel_id=1, source_target_pairs={{0,1},{2,0},{4,2},{6,4},{7,6},{5,7},{3,5},{1,3},{8,10},{10,12},{12... | collective-permute-start | bytes 1572872 | tf_op jit(solution)/shard_map/ppermute | solution.py:554
  271.1 25.4 %collective-permute-start.44 = (bf16[256,1024]{1,0:T(8,128)(2,1)}, bf16[256,1024]{1,0:T(8,128)(2,1)}, u32[]{:S(2)}, u32[]{:S(2)}) collective-permute-start(bf16[256,1024]{1,0:T(8,128)(2,1)} %get-tuple-element.276), channel_id=1, source_target_pairs={{0,2},{2,4},{4,6},{6,7},{7,5},{5,3},{3,1},{1,0},{8,9},{10,8},{12,1... | collective-permute-start | bytes 1572872 | tf_op jit(solution)/shard_map/ppermute | solution.py:554
  298.6 27.7 %collective-permute-start.49 = (bf16[64,4096]{1,0:T(8,128)(2,1)S(1)}, bf16[64,4096]{1,0:T(8,128)(2,1)S(1)}, u32[]{:S(2)}, u32[]{:S(2)}) collective-permute-start(bf16[64,4096]{1,0:T(8,128)(2,1)S(1)} %fusion.23), channel_id=1, source_target_pairs={{0,2},{2,4},{4,6},{6,7},{7,5},{5,3},{3,1},{1,0},{8,9},{10,8},{12,1... | collective-permute-start | bytes 1572872 | tf_op jit(solution)/shard_map/ppermute | solution.py:554
  301.8 24.5 %collective-permute-start.48 = (bf16[256,1024]{1,0:T(8,128)(2,1)S(1)}, bf16[256,1024]{1,0:T(8,128)(2,1)S(1)}, u32[]{:S(2)}, u32[]{:S(2)}) collective-permute-start(bf16[256,1024]{1,0:T(8,128)(2,1)S(1)} %get-tuple-element.273), channel_id=1, source_target_pairs={{0,1},{2,0},{4,2},{6,4},{7,6},{5,7},{3,5},{1,3},{8,10},{10,12},{12... | collective-permute-start | bytes 1572872 | tf_op jit(solution)/shard_map/ppermute | solution.py:554
  303.2 23.1 %collective-permute-start.47 = (bf16[256,1024]{1,0:T(8,128)(2,1)S(1)}, bf16[256,1024]{1,0:T(8,128)(2,1)S(1)}, u32[]{:S(2)}, u32[]{:S(2)}) collective-permute-start(bf16[256,1024]{1,0:T(8,128)(2,1)S(1)} %get-tuple-element.274), channel_id=1, source_target_pairs={{0,2},{2,4},{4,6},{6,7},{7,5},{5,3},{3,1},{1,0},{8,9},{10,8},{12,1... | collective-permute-start | bytes 1572872 | tf_op jit(solution)/shard_map/ppermute | solution.py:554
  338.4 32.6 %collective-permute-start.54 = (bf16[8,64,2560]{2,1,0:T(8,128)(2,1)}, bf16[8,64,2560]{2,1,0:T(8,128)(2,1)}, u32[]{:S(2)}, u32[]{:S(2)}) collective-permute-start(bf16[8,64,2560]{2,1,0:T(8,128)(2,1)} %dynamic-slice_bitcast_fusion.2), channel_id=1, source_target_pairs={{0,8},{1,9},{2,10},{3,11},{4,12},{5,13},{6,14},{7,15},{8,0},{9,1},... | collective-permute-start | bytes 7864328 | tf_op jit(solution)/shard_map/ppermute | solution.py:561
  341.6 29.4 %collective-permute-start.53 = (bf16[64,4096]{1,0:T(8,128)(2,1)}, bf16[64,4096]{1,0:T(8,128)(2,1)}, u32[]{:S(2)}, u32[]{:S(2)}) collective-permute-start(bf16[64,4096]{1,0:T(8,128)(2,1)} %get-tuple-element.269), channel_id=1, source_target_pairs={{0,1},{2,0},{4,2},{6,4},{7,6},{5,7},{3,5},{1,3},{8,10},{10,12},{12... | collective-permute-start | bytes 1572872 | tf_op jit(solution)/shard_map/ppermute | solution.py:554
  342.9 28.1 %collective-permute-start.52 = (bf16[64,4096]{1,0:T(8,128)(2,1)}, bf16[64,4096]{1,0:T(8,128)(2,1)}, u32[]{:S(2)}, u32[]{:S(2)}) collective-permute-start(bf16[64,4096]{1,0:T(8,128)(2,1)} %get-tuple-element.270), channel_id=1, source_target_pairs={{0,2},{2,4},{4,6},{6,7},{7,5},{5,3},{3,1},{1,0},{8,9},{10,8},{12,1... | collective-permute-start | bytes 1572872 | tf_op jit(solution)/shard_map/ppermute | solution.py:554
  347.0 24.0 %collective-permute-start.51 = (bf16[256,1024]{1,0:T(8,128)(2,1)}, bf16[256,1024]{1,0:T(8,128)(2,1)}, u32[]{:S(2)}, u32[]{:S(2)}) collective-permute-start(bf16[256,1024]{1,0:T(8,128)(2,1)} %get-tuple-element.271), channel_id=1, source_target_pairs={{0,1},{2,0},{4,2},{6,4},{7,6},{5,7},{3,5},{1,3},{8,10},{10,12},{12... | collective-permute-start | bytes 1572872 | tf_op jit(solution)/shard_map/ppermute | solution.py:554
  348.4 22.7 %collective-permute-start.50 = (bf16[256,1024]{1,0:T(8,128)(2,1)}, bf16[256,1024]{1,0:T(8,128)(2,1)}, u32[]{:S(2)}, u32[]{:S(2)}) collective-permute-start(bf16[256,1024]{1,0:T(8,128)(2,1)} %get-tuple-element.272), channel_id=1, source_target_pairs={{0,2},{2,4},{4,6},{6,7},{7,5},{5,3},{3,1},{1,0},{8,9},{10,8},{12,1... | collective-permute-start | bytes 1572872 | tf_op jit(solution)/shard_map/ppermute | solution.py:554
  374.5 18.3 %collective-permute-start.57 = (bf16[64,4096]{1,0:T(8,128)(2,1)}, bf16[64,4096]{1,0:T(8,128)(2,1)S(1)}, u32[]{:S(2)}, u32[]{:S(2)}) collective-permute-start(bf16[64,4096]{1,0:T(8,128)(2,1)} %get-tuple-element.267), channel_id=1, source_target_pairs={{0,1},{2,0},{4,2},{6,4},{7,6},{5,7},{3,5},{1,3},{8,10},{10,12},{12... | collective-permute-start | bytes 1572872 | tf_op jit(solution)/shard_map/ppermute | solution.py:554
  375.8 17.0 %collective-permute-start.56 = (bf16[64,4096]{1,0:T(8,128)(2,1)}, bf16[64,4096]{1,0:T(8,128)(2,1)}, u32[]{:S(2)}, u32[]{:S(2)}) collective-permute-start(bf16[64,4096]{1,0:T(8,128)(2,1)} %get-tuple-element.268), channel_id=1, source_target_pairs={{0,2},{2,4},{4,6},{6,7},{7,5},{5,3},{3,1},{1,0},{8,9},{10,8},{12,1... | collective-permute-start | bytes 1572872 | tf_op jit(solution)/shard_map/ppermute | solution.py:554
  395.0 27.1 %collective-permute-start.59 = (bf16[256,1024]{1,0:T(8,128)(2,1)}, bf16[256,1024]{1,0:T(8,128)(2,1)}, u32[]{:S(2)}, u32[]{:S(2)}) collective-permute-start(bf16[256,1024]{1,0:T(8,128)(2,1)} %add_convert_fusion.3), channel_id=1, source_target_pairs={{0,8},{1,9},{2,10},{3,11},{4,12},{5,13},{6,14},{7,15},{8,0},{9,1},... | collective-permute-start | bytes 1572872 | tf_op jit(solution)/shard_map/ppermute | solution.py:561
  398.0 24.2 %collective-permute-start.64 = (bf16[8,80,1536]{2,1,0:T(8,128)(2,1)}, bf16[8,80,1536]{2,1,0:T(8,128)(2,1)}, u32[]{:S(2)}, u32[]{:S(2)}) collective-permute-start(bf16[8,80,1536]{2,1,0:T(8,128)(2,1)} %dynamic-slice_bitcast_fusion.3), channel_id=1, source_target_pairs={{0,8},{1,9},{2,10},{3,11},{4,12},{5,13},{6,14},{7,15},{8,0},{9,1},... | collective-permute-start | bytes 5898248 | tf_op jit(solution)/shard_map/ppermute | solution.py:561
  404.7 17.5 %collective-permute-start.61 = (bf16[64,4096]{1,0:T(8,128)(2,1)}, bf16[64,4096]{1,0:T(8,128)(2,1)}, u32[]{:S(2)}, u32[]{:S(2)}) collective-permute-start(bf16[64,4096]{1,0:T(8,128)(2,1)} %get-tuple-element.265), channel_id=1, source_target_pairs={{0,1},{2,0},{4,2},{6,4},{7,6},{5,7},{3,5},{1,3},{8,10},{10,12},{12... | collective-permute-start | bytes 1572872 | tf_op jit(solution)/shard_map/ppermute | solution.py:554
  406.0 16.1 %collective-permute-start.60 = (bf16[64,4096]{1,0:T(8,128)(2,1)}, bf16[64,4096]{1,0:T(8,128)(2,1)}, u32[]{:S(2)}, u32[]{:S(2)}) collective-permute-start(bf16[64,4096]{1,0:T(8,128)(2,1)} %get-tuple-element.266), channel_id=1, source_target_pairs={{0,2},{2,4},{4,6},{6,7},{7,5},{5,3},{3,1},{1,0},{8,9},{10,8},{12,1... | collective-permute-start | bytes 1572872 | tf_op jit(solution)/shard_map/ppermute | solution.py:554
  423.2 18.8 %collective-permute-start.68 = (bf16[80,1536]{1,0:T(8,128)(2,1)S(1)}, bf16[80,1536]{1,0:T(8,128)(2,1)S(1)}, u32[]{:S(2)}, u32[]{:S(2)}) collective-permute-start(bf16[80,1536]{1,0:T(8,128)(2,1)S(1)} %fusion.62), channel_id=1, source_target_pairs={{0,2},{2,4},{4,6},{6,7},{7,5},{5,3},{3,1},{1,0},{8,9},{10,8},{12,1... | collective-permute-start | bytes 737288 | tf_op jit(solution)/shard_map/ppermute | solution.py:554
  449.0 17.6 %collective-permute-start.81 = (bf16[64,4096]{1,0:T(8,128)(2,1)S(1)}, bf16[64,4096]{1,0:T(8,128)(2,1)S(1)}, u32[]{:S(2)}, u32[]{:S(2)}) collective-permute-start(bf16[64,4096]{1,0:T(8,128)(2,1)S(1)} %add_convert_fusion.2), channel_id=1, source_target_pairs={{0,8},{1,9},{2,10},{3,11},{4,12},{5,13},{6,14},{7,15},{8,0},{9,1},... | collective-permute-start | bytes 1572872 | tf_op jit(solution)/shard_map/ppermute | solution.py:561
  (133 other events, 1212.0 us)
Sparse Core Ops, SparseCore 0:
  14.6 88.6 all-gather.2
  106.8 80.3 all-gather.4

commit v3 on v2

--- a/solution.py
+++ b/solution.py
@@ -395,30 +395,69 @@
     out_ref[...] = project(left_ref[...], right_ref[...]).astype(LOW)
 
 
-def product_extra_kernel(size, left_ref, right_ref, small_ref, out_ref):
-    found = project(left_ref[...], right_ref[...]).astype(LOW)
-    body = found.shape[0] // size // 2
-    for shard in range(size):
-        extra = jnp.broadcast_to(small_ref[shard : shard + 1, :], (EXTRA, found.shape[1])).astype(LOW)
-        for core in range(2):
-            half = 2 * shard + core
-            at = half * (body + EXTRA)
-            out_ref[at : at + body, :] = found[half * body : (half + 1) * body]
-            out_ref[at + body : at + body + EXTRA, :] = extra
-
-
-def product(left, right, small=None, size=1):
+def product(left, right):
     height, depth = left.shape
-    rows = height if small is None else height + 2 * EXTRA * size
-    return pl.pallas_call(
-        product_kernel if small is None else functools.partial(product_extra_kernel, size),
+    return pl.pallas_call(
+        product_kernel,
         grid=(right.shape[1] // COLUMNS,),
-        in_specs=[kept((height, depth)), columns_of(depth)] + ([] if small is None else [columns_of(size)]),
-        out_specs=columns_of(rows),
-        out_shape=jax.ShapeDtypeStruct((rows, right.shape[1]), LOW),
+        in_specs=[kept((height, depth)), columns_of(depth)],
+        out_specs=columns_of(height),
+        out_shape=jax.ShapeDtypeStruct((height, right.shape[1]), LOW),
         compiler_params=LIMIT,
         name="product",
-    )(left, right, *([] if small is None else [small]))
+    )(left, right)
+
+
+def split_kernel(size, steps, tailed, core_ref, left_ref, right_ref, more_ref, mine_ref, other_ref, found_ref):
+    step = pl.program_id(0)
+    body = found_ref.shape[0] // size // 2
+
+    @pl.when(step < steps)
+    def _():
+        found_ref[...] = project(left_ref[...], right_ref[...]).astype(LOW)
+
+    if tailed:
+
+        @pl.when(step >= steps)
+        def _():
+            found_ref[...] = more_ref[...]
+
+    extra = 0 if tailed else EXTRA
+    for shard in range(size):
+        at = shard * (body + extra)
+        for out_ref, half in ((mine_ref, core_ref[0]), (other_ref, 1 - core_ref[0])):
+            start = pl.multiple_of((2 * shard + half) * body, body)
+            out_ref[at : at + body, :] = found_ref[pl.ds(start, body), :]
+            if extra:
+                row = jnp.broadcast_to(more_ref[shard : shard + 1, :], (EXTRA, more_ref.shape[1]))
+                out_ref[at + body : at + body + EXTRA, :] = row.astype(LOW)
+
+
+def split_product(core, left, right, size, tail=None, small=None):
+    height, depth = left.shape
+    steps = right.shape[1] // COLUMNS
+    width = right.shape[1] + (0 if tail is None else tail.shape[1])
+    rows = height // 2 + (EXTRA * size if tail is None else 0)
+    last = lambda i: (0, jnp.minimum(i, steps - 1))
+    if tail is None:
+        more, more_spec = small, pl.BlockSpec((size, COLUMNS), last)
+    else:
+        more, more_spec = tail, pl.BlockSpec((height, COLUMNS), lambda i: (0, jnp.maximum(i - steps, 0)))
+    return pl.pallas_call(
+        functools.partial(split_kernel, size, steps, tail is not None),
+        grid=(width // COLUMNS,),
+        in_specs=[
+            pl.BlockSpec(memory_space=pltpu.SMEM),
+            kept((height, depth)),
+            pl.BlockSpec((depth, COLUMNS), last),
+            more_spec,
+        ],
+        out_specs=[columns_of(rows), columns_of(rows)],
+        out_shape=[jax.ShapeDtypeStruct((rows, width), LOW)] * 2,
+        scratch_shapes=[pltpu.VMEM((height, COLUMNS), LOW)],
+        compiler_params=LIMIT,
+        name="split_product",
+    )(core.reshape(1).astype(jnp.int32), left, right, more)
 
 
 def assemble_kernel(moves, align, place_ref, *refs):
@@ -635,17 +674,24 @@
         if self.direct:
             own = lax.psum_scatter(values, "shard", scatter_dimension=0, tiled=True)
             return lax.psum(own, ("cross", "core")).astype(FULL)
-        width = values.shape[1]
-        half = values.shape[0] // self.size // 2
-        split = values.reshape(self.size, 2, half, width)
-        other = self.swap(lax.dynamic_index_in_dim(split, 1 - self.core, axis=1, keepdims=False), 1)
-        (other,) = yield [other]
+        if isinstance(values, tuple):
+            kept_rows, other = (part.reshape(self.size, -1, part.shape[1]) for part in values)
+            _, half, width = other.shape
+        else:
+            width = values.shape[1]
+            half = values.shape[0] // self.size // 2
+            split = values.reshape(self.size, 2, half, width)
+            other = lax.dynamic_index_in_dim(split, 1 - self.core, axis=1, keepdims=False)
+        (other,) = yield [self.swap(other, 1)]
 
         def piece(step):
             owner = self.owner(step)
-            own = lax.dynamic_slice(split, (owner, self.core, 0, 0), (1, 1, half, width))
+            if isinstance(values, tuple):
+                own = lax.dynamic_slice(kept_rows, (owner, 0, 0), (1, half, width))[0]
+            else:
+                own = lax.dynamic_slice(split, (owner, self.core, 0, 0), (1, 1, half, width))[0, 0]
             pair = lax.dynamic_slice(other, (owner, 0, 0), (1, half, width))
-            return own[0, 0].astype(FULL) + pair[0].astype(FULL)
+            return own.astype(FULL) + pair[0].astype(FULL)
 
         ahead = piece(self.far).astype(LOW)
         back = piece(-self.near).astype(LOW)
@@ -800,16 +846,19 @@
             spans += [[(i, row, 0, D)] for i, row in ((0, 2), (0, 0), (0, 1), (1, 2), (1, 0), (1, 1))]
             spans += [[(2, 0, 0, size * hidden)]]
             small = pack(arrays, spans, size)
-        if ride and g == GROUPS - 1:
+        if ride and g == 0:
+            halves = split_product(links.core, tokens_turned, d_group, size, tail=grad_out)
+            *halves, d_attended = tie(*halves, d_attended)
+            grad_group = tuple(halves)
+        elif ride:
             small = jnp.pad(small, ((0, 0), (0, 3 * WIDE - used)))
-            grad_group = product(tokens_turned, d_group, small, size)
+            halves = split_product(links.core, tokens_turned, d_group, size, small=small)
+            *halves, d_group = flow.advance(*halves, d_group)
+            grad_group = tuple(halves)
         else:
             grad_group = product(tokens_turned, d_group)
-        if g == 0:
-            grad_group = jnp.concatenate([grad_group, grad_out], axis=1)
-            grad_group, d_attended = tie(grad_group, d_attended)
-        else:
-            grad_group, d_group = flow.advance(grad_group, d_group)
+            if g == 0:
+                grad_group = jnp.concatenate([grad_group, grad_out], axis=1)
         flow.start(f"back{g}", links.reduce(grad_group))
         d_groups.append(d_group)
     d_tokens = flow.advance(tokens_back(d_inner, d_groups[0], whole_groups[0], FULL))

time: 500 us -> 491 us (0.982)
  local copies, waits for them, and re-layouts: 55.7 us -> 44.5 us
  starting transfers between devices: 70.9 us -> 77.8 us
  waiting for transfers between devices: 73.4 us -> 67.7 us
    squeeze x4 -> x2, local copies, waits for them, and re-layouts: 11 us -> 4.65 us  [reduce(): lax.dynamic_index_in_dim(split, 1 - self.core, axis=1, keepdims=False)]
    ppermute x49, waiting for transfers between devices: 66.8 us -> 61.1 us  [hop(): return lax.ppermute(values, AXES, pairs)]
    ppermute x49, starting transfers between devices: 58.4 us -> 63.7 us  [hop(): return lax.ppermute(values, AXES, pairs)]
    unnamed x162 -> x158, local copies, waits for them, and re-layouts: 38.5 us -> 33.6 us
  transfers between devices with their start and end apart: 84 -> 84, of which waited for: 21 -> 20; matrix products, arithmetic and copies ran while one was open for 13% -> 13% of each run, Pallas kernels for 32% -> 33%
where the time goes in v3:
time: 491 us; the launch traced here: 483 us
  Pallas kernels  189 us (38%)
  starting transfers between devices  77.8 us (16%)
  waiting for transfers between devices  67.7 us (14%)
  other arithmetic  54.4 us (11%)
  local copies, waits for them, and re-layouts  44.5 us (9%)
  matrix products  34.4 us (7%)
  between operations  15.8 us (3%)
    ppermute x49, starting transfers between devices, hop(): return lax.ppermute(values, AXES, pairs)  63.7 us
    ppermute x49, waiting for transfers between devices, hop(): return lax.ppermute(values, AXES, pairs)  61.1 us
    pallas_call x2, Pallas kernels, attend_back(): pl.pallas_call(attend_back_kernel, grid=(count // SEQ, PAIRS), in_specs=t...  36.2 us
    unnamed x158, local copies, waits for them, and re-layouts  33.6 us
    dot_general x3, matrix products, gram(): lax.dot_general(left, right, (((0,), (0,)), ((), ())), preferred_element_...  26 us
    pallas_call x1, Pallas kernels, inner_back(): pl.pallas_call(inner_back_kernel, grid=(hidden // D,), in_specs=[pl.Block...  22.8 us
    pallas_call x2, Pallas kernels, attend(): pl.pallas_call(attend_kernel, grid=(seqs, PAIRS), in_specs=triple() + [pl...  22.6 us
    pallas_call x1, Pallas kernels, inner_gelu(): pl.pallas_call(inner_kernel, grid=(hidden // COLUMNS,), in_specs=[kept((c...  18.9 us
  transfers between devices with their start and end apart: 84, of which 20 were waited for; matrix products, arithmetic and copies ran while one was open for 13% of the time, Pallas kernels for 33%

profile of v3, /device:TPU:0, one launch (start us, length us, event | category | flops | bytes accessed | tf_op | source)
XLA Modules:
  0.0 483.5 jit_solution(7949523369113958357)
XLA Ops:
  19.4 6.2 %collective-permute-done.refs_1_ = bf16[80,1536]{1,0:T(8,128)(2,1)S(1)} collective-permute-done((bf16[80,1536]{1,0:T(8,128)(2,1)S(1)}, bf16[80,1536]{1,0:T(8,128)(2,1)S(1)}, u32[]{:S(2)}, u32[]{:S(2)}) %collective-permute-start) | collective-permute-done | bytes 245792 | tf_op jit(solution)/shard_map/ppermute | solution.py:593
  28.6 7.7 %collective-permute-done.2.refs_5_.refs_3_ = bf16[80,1536]{1,0:T(8,128)(2,1)S(1)} collective-permute-done((bf16[80,1536]{1,0:T(8,128)(2,1)S(1)}, bf16[80,1536]{1,0:T(8,128)(2,1)S(1)}, u32[]{:S(2)}, u32[]{:S(2)}) %collective-permute-start.2) | collective-permute-done | bytes 245792 | tf_op jit(solution)/shard_map/ppermute | solution.py:593
  46.9 10.8 %collective-permute-done.11.refs_2_ = bf16[64,1536]{1,0:T(8,128)(2,1)} collective-permute-done((bf16[64,1536]{1,0:T(8,128)(2,1)S(1)}, bf16[64,1536]{1,0:T(8,128)(2,1)}, u32[]{:S(2)}, u32[]{:S(2)}) %collective-permute-start.11) | collective-permute-done | bytes 196640 | tf_op jit(solution)/shard_map/ppermute | solution.py:593
  76.9 10.4 %collective-permute-start.26 = (bf16[64,1024]{1,0:T(8,128)(2,1)}, bf16[64,1024]{1,0:T(8,128)(2,1)}, u32[]{:S(2)}, u32[]{:S(2)}) collective-permute-start(bf16[64,1024]{1,0:T(8,128)(2,1)} %collective-permute-done.19.refs_1_), channel_id=1, source_target_pairs={{0,2},{2,4},{4,6},{6,7},{7,5},{5,3},{3,1},{1,0},{8,9},{10,8},{12,1... | collective-permute-start | bytes 393224 | tf_op jit(solution)/shard_map/ppermute | solution.py:593
  90.0 3.8 collective-permute-start.22
  96.8 5.2 %assemble.3.w_ref = bf16[1024,1536]{1,0:T(8,128)(2,1)S(1)} custom-call(s32[15]{0:T(128)S(1)} %stack.122.place_ref, bf16[128,1536]{1,0:T(8,128)(2,1)S(1)} %pad_maximum_fusion.3.refs_0_, bf16[80,1536]{1,0:T(8,128)(2,1)S(1)} %collective-permute-done.refs_1_, bf16[80,1536]{1,0:T(8,128)(2,1)S(1)} %collective-permute-done.1.refs_2_, ...), custom_call_target="tpu_custom_call" | custom-call | tf_op jit(solution)/shard_map/assemble/pallas_call | solution.py:478
  104.3 3.6 fusion.query_ref.key_ref.value_ref
  116.5 11.3 %attend.2 = (bf16[1024,1024]{1,0:T(8,128)(2,1)S(1)}, f32[8,2,512]{2,1,0:T(2,128)S(1)}) custom-call(bf16[1024,1536]{1,0:T(8,128)(2,1)S(1)} %fusion.query_ref.key_ref.value_ref, bf16[1024,1536]{1,0:T(8,128)(2,1)S(1)} %fusion.query_ref.key_ref.value_ref, bf16[1024,1536]{1,0:T(8,128)(2,1)S(1)} %fusion.query_ref.key_ref.value_ref), custom_call_target="tpu_custom_call" | custom-call | tf_op jit(solution)/shard_map/attend/pallas_call | solution.py:119
  129.9 3.4 assemble.4.w_ref
  133.4 4.8 fusion.1.query_ref.key_ref.value_ref
  143.1 11.3 %attend.3 = (bf16[1024,1024]{1,0:T(8,128)(2,1)S(1)}, f32[8,2,512]{2,1,0:T(2,128)S(1)}) custom-call(bf16[1024,1536]{1,0:T(8,128)(2,1)S(1)} %copy-done.2, bf16[1024,1536]{1,0:T(8,128)(2,1)S(1)} %copy-done.2, bf16[1024,1536]{1,0:T(8,128)(2,1)S(1)} %copy-done.2, bf16[1024,1024]{1,0:T(8,128)(2,1)S(1)} %copy-done.14), custom_call_target="tpu_custom_call", output_to_operand_aliasing={{0}: (3, {})} | custom-call | tf_op jit(solution)/shard_map/attend/pallas_call | solution.py:119
  160.6 6.7 %out_norm.1 = (f32[1024,1024]{1,0:T(8,128)}, f32[1024,128]{1,0:T(8,128)S(1)}, bf16[1024,1024]{1,0:T(8,128)(2,1)S(1)}) custom-call(bf16[1024,1024]{1,0:T(8,128)(2,1)S(1)} %copy-done.16, bf16[1024,1024]{1,0:T(8,128)(2,1)} %copy-done.6, bf16[1024,1024]{1,0:T(8,128)(2,1)} %tokens_ref.1, f32[8,1024]{1,0:T(8,128)S(1)} %copy-done.33), custom_call_target="tpu_custom_call" | custom-call | tf_op jit(solution)/shard_map/out_norm/pallas_call | solution.py:205
  171.1 18.9 %inner_gelu.1 = (bf16[1024,4096]{1,0:T(8,128)(2,1)}, bf16[1024,4096]{1,0:T(8,128)(2,1)}) custom-call(bf16[1024,1024]{1,0:T(8,128)(2,1)S(1)} %copy-done.21, bf16[1024,4096]{1,0:T(8,128)(2,1)} %all-gather.3.cloned.1.call-done.w_ref, f32[1,4096]{1,0:T(1,128)S(1)} %get-tuple-element.199.bias_ref), custom_call_target="tpu_custom_call" | custom-call | tf_op jit(solution)/shard_map/inner_gelu/pallas_call | solution.py:230
  191.6 18.6 %outer_norms.1 = (bf16[1024,1024]{1,0:T(8,128)(2,1)}, f32[1024,1024]{1,0:T(8,128)}, bf16[1024,1024]{1,0:T(8,128)(2,1)S(1)}, f32[8,1024]{1,0:T(8,128)S(1)}) custom-call(bf16[1024,4096]{1,0:T(8,128)(2,1)} %get-tuple-element.200.active_ref, bf16[4096,1024]{1,0:T(8,128)(2,1)} %all-gather.5.cloned.1.call-done.w_ref, f32[1024,1024]{1,0:T(8,128)} %get-tuple-element.202.unit_ref, ...), custom_call_target="tpu_custom_call" | custom-call | tf_op jit(solution)/shard_map/outer_norms/pallas_call | solution.py:259
  210.2 12.1 %convolution_convert_fusion.1 = bf16[4096,1024]{1,0:T(8,128)(2,1)S(1)} fusion(bf16[1024,4096]{1,0:T(8,128)(2,1)} %get-tuple-element.200.active_ref, bf16[1024,1024]{1,0:T(8,128)(2,1)S(1)} %get-tuple-element.205.d_ref), kind=kOutput, calls=%fused_computation.1 | convolution fusion | flops 8594128896 | bytes 18874368 | tf_op jit(solution)/shard_map/dot_general | solution.py:29
  222.3 3.4 copy-done.66
  230.2 15.5 %outer_back.1 = (bf16[1024,4096]{1,0:T(8,128)(2,1)}, f32[1,4096]{1,0:T(1,128)S(1)}) custom-call(bf16[1024,1024]{1,0:T(8,128)(2,1)S(1)} %copy-done.24, bf16[4096,1024]{1,0:T(8,128)(2,1)} %all-gather.5.cloned.1.call-done.w_ref, bf16[1024,4096]{1,0:T(8,128)(2,1)} %get-tuple-element.206.slope_ref), custom_call_target="tpu_custom_call" | custom-call | tf_op jit(solution)/shard_map/outer_back/pallas_call | solution.py:285
  247.7 11.4 %convolution_convert_fusion = bf16[1024,4096]{1,0:T(8,128)(2,1)S(1)} fusion(bf16[1024,1024]{1,0:T(8,128)(2,1)S(1)} %copy-done.22, bf16[1024,4096]{1,0:T(8,128)(2,1)} %get-tuple-element.211.d_pre_ref), kind=kOutput, calls=%fused_computation | convolution fusion | flops 8594128896 | bytes 18874368 | tf_op jit(solution)/shard_map/dot_general | solution.py:29
  271.2 22.8 %inner_back.1 = (f32[1024,1024]{1,0:T(8,128)}, bf16[1024,1024]{1,0:T(8,128)(2,1)S(1)}, bf16[1024,1024]{1,0:T(8,128)(2,1)S(1)}, f32[8,1024]{1,0:T(8,128)S(1)}) custom-call(bf16[1024,4096]{1,0:T(8,128)(2,1)} %get-tuple-element.211.d_pre_ref, bf16[1024,4096]{1,0:T(8,128)(2,1)} %all-gather.3.cloned.1.call-done.w_ref, f32[1024,1024]{1,0:T(8,128)} %get-tuple-element.212.d_ref, ...), custom_call_target="tpu_custom_call" | custom-call | tf_op jit(solution)/shard_map/inner_back/pallas_call | solution.py:331
  304.1 18.2 %attend_back.2 = (bf16[1024,1536]{1,0:T(8,128)(2,1)S(1)}, f32[8,1536]{1,0:T(8,128)S(1)}) custom-call(bf16[1024,1536]{1,0:T(8,128)(2,1)S(1)} %fusion.query_ref.key_ref.value_ref, bf16[1024,1536]{1,0:T(8,128)(2,1)S(1)} %fusion.query_ref.key_ref.value_ref, bf16[1024,1536]{1,0:T(8,128)(2,1)S(1)} %fusion.query_ref.key_ref.value_ref, ...), custom_call_target="tpu_custom_call" | custom-call | tf_op jit(solution)/shard_map/attend_back/pallas_call | solution.py:136
  324.0 8.3 %split_product.2 = (bf16[512,2560]{1,0:T(8,128)(2,1)}, bf16[512,2560]{1,0:T(8,128)(2,1)}) custom-call(s32[1]{0:T(128)} %bitcast.51.core_ref, bf16[1024,1024]{1,0:T(8,128)(2,1)S(1)} %copy-done.4, bf16[1024,1536]{1,0:T(8,128)(2,1)} %copy-done.8, bf16[1024,1024]{1,0:T(8,128)(2,1)S(1)} %convolution_convert_fusion.2.more_ref), custom_call_target="tpu_custom_call" | custom-call | tf_op jit(solution)/shard_map/split_product/pallas_call | solution.py:446
  332.4 3.6 fusion.17
  344.5 18.0 %attend_back.3 = (bf16[1024,1536]{1,0:T(8,128)(2,1)S(1)}, f32[8,1536]{1,0:T(8,128)S(1)}) custom-call(bf16[1024,1536]{1,0:T(8,128)(2,1)S(1)} %copy-done.3, bf16[1024,1536]{1,0:T(8,128)(2,1)S(1)} %copy-done.3, bf16[1024,1536]{1,0:T(8,128)(2,1)S(1)} %copy-done.3, bf16[1024,1024]{1,0:T(8,128)(2,1)S(1)} %copy-done.19, f32[8,2,512]{2,1,0:T(2,128)S(1)} %get-tuple-element.235.lse_ref), custom_call_target="tpu_custom_call" | custom-call | tf_op jit(solution)/shard_map/attend_back/pallas_call | solution.py:136
  366.9 3.3 fusion.10
  378.9 6.3 %split_product.3 = (bf16[640,1536]{1,0:T(8,128)(2,1)S(1)}, bf16[640,1536]{1,0:T(8,128)(2,1)}) custom-call(s32[1]{0:T(128)} %bitcast.51.core_ref, bf16[1024,1024]{1,0:T(8,128)(2,1)S(1)} %copy-done.5, bf16[1024,1536]{1,0:T(8,128)(2,1)} %copy-done.11, f32[8,1536]{1,0:T(8,128)S(1)} %copy-done.40), custom_call_target="tpu_custom_call" | custom-call | tf_op jit(solution)/shard_map/split_product/pallas_call | solution.py:446
  385.2 6.2 %collective-permute-done.58 = bf16[64,2560]{1,0:T(8,128)(2,1)} collective-permute-done((bf16[64,2560]{1,0:T(8,128)(2,1)}, bf16[64,2560]{1,0:T(8,128)(2,1)}, u32[]{:S(2)}, u32[]{:S(2)}) %collective-permute-start.58) | collective-permute-done | bytes 327712 | tf_op jit(solution)/shard_map/ppermute | solution.py:593
  394.7 3.5 fusion.6
  403.1 7.9 %tokens_back.2.base_ref = f32[1024,1024]{1,0:T(8,128)} custom-call(f32[1024,1024]{1,0:T(8,128)} %get-tuple-element.214.base_ref, bf16[1024,1536]{1,0:T(8,128)(2,1)S(1)} %copy-done.9, bf16[1024,1536]{1,0:T(8,128)(2,1)} %copy-done.7), custom_call_target="tpu_custom_call" | custom-call | tf_op jit(solution)/shard_map/tokens_back/pallas_call | solution.py:363
  411.0 5.3 %collective-permute-done.62 = bf16[64,2560]{1,0:T(8,128)(2,1)} collective-permute-done((bf16[64,2560]{1,0:T(8,128)(2,1)}, bf16[64,2560]{1,0:T(8,128)(2,1)}, u32[]{:S(2)}, u32[]{:S(2)}) %collective-permute-start.62) | collective-permute-done | bytes 327712 | tf_op jit(solution)/shard_map/ppermute | solution.py:593
  427.1 7.2 %tokens_back.3 = bf16[1024,1024]{1,0:T(8,128)(2,1)} custom-call(f32[1024,1024]{1,0:T(8,128)} %tokens_back.2.base_ref, bf16[1024,1536]{1,0:T(8,128)(2,1)S(1)} %copy-done.12, bf16[1024,1536]{1,0:T(8,128)(2,1)} %copy-done.10), custom_call_target="tpu_custom_call" | custom-call | tf_op jit(solution)/shard_map/tokens_back/pallas_call | solution.py:363
  441.7 4.0 collective-permute-done.73
  465.7 5.2 %collective-permute-done.79 = bf16[80,1536]{1,0:T(8,128)(2,1)S(1)} collective-permute-done((bf16[80,1536]{1,0:T(8,128)(2,1)S(1)}, bf16[80,1536]{1,0:T(8,128)(2,1)S(1)}, u32[]{:S(2)}, u32[]{:S(2)}) %collective-permute-start.79) | collective-permute-done | bytes 245792 | tf_op jit(solution)/shard_map/ppermute | solution.py:600
  (379 shorter events, 183.0 us)
Async XLA Ops:
  7.2 162.2 %all-gather.3.cloned.1.call-start = ((), (), s32[]{:S(2)}) async-start(), calls=%async_computation | async-start | bytes 8650752 | tf_op jit(solution)/shard_map/all_gather | solution.py:663
  14.5 175.5 %all-gather.5.cloned.1.call-start = ((), (), s32[]{:S(2)}) async-start(), calls=%async_computation.1 | async-start | bytes 8650752 | tf_op jit(solution)/shard_map/all_gather | solution.py:663
  38.9 18.9 %collective-permute-start.6 = (bf16[80,1536]{1,0:T(8,128)(2,1)S(1)}, bf16[80,1536]{1,0:T(8,128)(2,1)S(1)}, u32[]{:S(2)}, u32[]{:S(2)}) collective-permute-start(bf16[80,1536]{1,0:T(8,128)(2,1)S(1)} %collective-permute-done.2.refs_5_.refs_3_), channel_id=1, source_target_pairs={{0,2},{2,4},{4,6},{6,7},{7,5},{5,3},{3,1},{1,0},{8,9},{10,8},{12,1... | collective-permute-start | bytes 737288 | tf_op jit(solution)/shard_map/ppermute | solution.py:593
  41.2 16.6 %collective-permute-start.7 = (bf16[80,1536]{1,0:T(8,128)(2,1)S(1)}, bf16[80,1536]{1,0:T(8,128)(2,1)S(1)}, u32[]{:S(2)}, u32[]{:S(2)}) collective-permute-start(bf16[80,1536]{1,0:T(8,128)(2,1)S(1)} %collective-permute-done.3.refs_6_.refs_4_), channel_id=1, source_target_pairs={{0,1},{2,0},{4,2},{6,4},{7,6},{5,7},{3,5},{1,3},{8,10},{10,12},{12... | collective-permute-start | bytes 737288 | tf_op jit(solution)/shard_map/ppermute | solution.py:593
  41.2 16.6 %collective-permute-start.8 = (bf16[80,1536]{1,0:T(8,128)(2,1)S(1)}, bf16[80,1536]{1,0:T(8,128)(2,1)S(1)}, u32[]{:S(2)}, u32[]{:S(2)}) collective-permute-start(bf16[80,1536]{1,0:T(8,128)(2,1)S(1)} %collective-permute-done.2.refs_5_.refs_3_), channel_id=1, source_target_pairs={{0,8},{1,9},{2,10},{3,11},{4,12},{5,13},{6,14},{7,15},{8,0},{9,1},... | collective-permute-start | bytes 737288 | tf_op jit(solution)/shard_map/ppermute | solution.py:600
  76.9 25.1 %collective-permute-start.26 = (bf16[64,1024]{1,0:T(8,128)(2,1)}, bf16[64,1024]{1,0:T(8,128)(2,1)}, u32[]{:S(2)}, u32[]{:S(2)}) collective-permute-start(bf16[64,1024]{1,0:T(8,128)(2,1)} %collective-permute-done.19.refs_1_), channel_id=1, source_target_pairs={{0,2},{2,4},{4,6},{6,7},{7,5},{5,3},{3,1},{1,0},{8,9},{10,8},{12,1... | collective-permute-start | bytes 393224 | tf_op jit(solution)/shard_map/ppermute | solution.py:593
  87.3 16.9 %collective-permute-start.28 = (bf16[64,1024]{1,0:T(8,128)(2,1)}, bf16[64,1024]{1,0:T(8,128)(2,1)}, u32[]{:S(2)}, u32[]{:S(2)}) collective-permute-start(bf16[64,1024]{1,0:T(8,128)(2,1)} %collective-permute-done.19.refs_1_), channel_id=1, source_target_pairs={{0,8},{1,9},{2,10},{3,11},{4,12},{5,13},{6,14},{7,15},{8,0},{9,1},... | collective-permute-start | bytes 393224 | tf_op jit(solution)/shard_map/ppermute | solution.py:600
  90.0 18.7 %collective-permute-start.22 = (bf16[64,1536]{1,0:T(8,128)(2,1)}, bf16[64,1536]{1,0:T(8,128)(2,1)S(1)}, u32[]{:S(2)}, u32[]{:S(2)}) collective-permute-start(bf16[64,1536]{1,0:T(8,128)(2,1)} %collective-permute-done.15.refs_5_), channel_id=1, source_target_pairs={{0,2},{2,4},{4,6},{6,7},{7,5},{5,3},{3,1},{1,0},{8,9},{10,8},{12,1... | collective-permute-start | bytes 589832 | tf_op jit(solution)/shard_map/ppermute | solution.py:593
  110.8 17.1 %collective-permute-start.30 = (bf16[64,1536]{1,0:T(8,128)(2,1)S(1)}, bf16[64,1536]{1,0:T(8,128)(2,1)S(1)}, u32[]{:S(2)}, u32[]{:S(2)}) collective-permute-start(bf16[64,1536]{1,0:T(8,128)(2,1)S(1)} %collective-permute-done.22.refs_9_), channel_id=1, source_target_pairs={{0,2},{2,4},{4,6},{6,7},{7,5},{5,3},{3,1},{1,0},{8,9},{10,8},{12,1... | collective-permute-start | bytes 589832 | tf_op jit(solution)/shard_map/ppermute | solution.py:593
  228.1 17.5 %collective-permute-start.42 = (bf16[8,256,1024]{2,1,0:T(8,128)(2,1)}, bf16[8,256,1024]{2,1,0:T(8,128)(2,1)}, u32[]{:S(2)}, u32[]{:S(2)}) collective-permute-start(bf16[8,256,1024]{2,1,0:T(8,128)(2,1)} %dynamic-slice_bitcast_fusion.1), channel_id=1, source_target_pairs={{0,8},{1,9},{2,10},{3,11},{4,12},{5,13},{6,14},{7,15},{8,0},{9,1},... | collective-permute-start | bytes 12582920 | tf_op jit(solution)/shard_map/ppermute | solution.py:600
  264.6 29.4 %collective-permute-start.46 = (bf16[8,64,4096]{2,1,0:T(8,128)(2,1)}, bf16[8,64,4096]{2,1,0:T(8,128)(2,1)}, u32[]{:S(2)}, u32[]{:S(2)}) collective-permute-start(bf16[8,64,4096]{2,1,0:T(8,128)(2,1)} %dynamic-slice_bitcast_fusion), channel_id=1, source_target_pairs={{0,8},{1,9},{2,10},{3,11},{4,12},{5,13},{6,14},{7,15},{8,0},{9,1},... | collective-permute-start | bytes 12582920 | tf_op jit(solution)/shard_map/ppermute | solution.py:600
  268.2 25.8 %collective-permute-start.44 = (bf16[256,1024]{1,0:T(8,128)(2,1)}, bf16[256,1024]{1,0:T(8,128)(2,1)}, u32[]{:S(2)}, u32[]{:S(2)}) collective-permute-start(bf16[256,1024]{1,0:T(8,128)(2,1)} %get-tuple-element.288), channel_id=1, source_target_pairs={{0,2},{2,4},{4,6},{6,7},{7,5},{5,3},{3,1},{1,0},{8,9},{10,8},{12,1... | collective-permute-start | bytes 1572872 | tf_op jit(solution)/shard_map/ppermute | solution.py:593
  268.9 25.0 %collective-permute-start.45 = (bf16[256,1024]{1,0:T(8,128)(2,1)}, bf16[256,1024]{1,0:T(8,128)(2,1)}, u32[]{:S(2)}, u32[]{:S(2)}) collective-permute-start(bf16[256,1024]{1,0:T(8,128)(2,1)} %get-tuple-element.287), channel_id=1, source_target_pairs={{0,1},{2,0},{4,2},{6,4},{7,6},{5,7},{3,5},{1,3},{8,10},{10,12},{12... | collective-permute-start | bytes 1572872 | tf_op jit(solution)/shard_map/ppermute | solution.py:593
  297.3 26.6 %collective-permute-start.47 = (bf16[256,1024]{1,0:T(8,128)(2,1)S(1)}, bf16[256,1024]{1,0:T(8,128)(2,1)S(1)}, u32[]{:S(2)}, u32[]{:S(2)}) collective-permute-start(bf16[256,1024]{1,0:T(8,128)(2,1)S(1)} %get-tuple-element.286), channel_id=1, source_target_pairs={{0,2},{2,4},{4,6},{6,7},{7,5},{5,3},{3,1},{1,0},{8,9},{10,8},{12,1... | collective-permute-start | bytes 1572872 | tf_op jit(solution)/shard_map/ppermute | solution.py:593
  298.1 25.8 %collective-permute-start.48 = (bf16[256,1024]{1,0:T(8,128)(2,1)S(1)}, bf16[256,1024]{1,0:T(8,128)(2,1)S(1)}, u32[]{:S(2)}, u32[]{:S(2)}) collective-permute-start(bf16[256,1024]{1,0:T(8,128)(2,1)S(1)} %get-tuple-element.285), channel_id=1, source_target_pairs={{0,1},{2,0},{4,2},{6,4},{7,6},{5,7},{3,5},{1,3},{8,10},{10,12},{12... | collective-permute-start | bytes 1572872 | tf_op jit(solution)/shard_map/ppermute | solution.py:593
  300.7 23.3 %collective-permute-start.49 = (bf16[64,4096]{1,0:T(8,128)(2,1)S(1)}, bf16[64,4096]{1,0:T(8,128)(2,1)S(1)}, u32[]{:S(2)}, u32[]{:S(2)}) collective-permute-start(bf16[64,4096]{1,0:T(8,128)(2,1)S(1)} %fusion.23), channel_id=1, source_target_pairs={{0,2},{2,4},{4,6},{6,7},{7,5},{5,3},{3,1},{1,0},{8,9},{10,8},{12,1... | collective-permute-start | bytes 1572872 | tf_op jit(solution)/shard_map/ppermute | solution.py:593
  332.3 30.3 %collective-permute-start.54 = (bf16[8,64,2560]{2,1,0:T(8,128)(2,1)}, bf16[8,64,2560]{2,1,0:T(8,128)(2,1)}, u32[]{:S(2)}, u32[]{:S(2)}) collective-permute-start(bf16[8,64,2560]{2,1,0:T(8,128)(2,1)} %bitcast.260), channel_id=1, source_target_pairs={{0,8},{1,9},{2,10},{3,11},{4,12},{5,13},{6,14},{7,15},{8,0},{9,1},... | collective-permute-start | bytes 7864328 | tf_op jit(solution)/shard_map/ppermute | solution.py:600
  336.0 26.5 %collective-permute-start.50 = (bf16[256,1024]{1,0:T(8,128)(2,1)}, bf16[256,1024]{1,0:T(8,128)(2,1)}, u32[]{:S(2)}, u32[]{:S(2)}) collective-permute-start(bf16[256,1024]{1,0:T(8,128)(2,1)} %get-tuple-element.284), channel_id=1, source_target_pairs={{0,2},{2,4},{4,6},{6,7},{7,5},{5,3},{3,1},{1,0},{8,9},{10,8},{12,1... | collective-permute-start | bytes 1572872 | tf_op jit(solution)/shard_map/ppermute | solution.py:593
  337.0 25.5 %collective-permute-start.51 = (bf16[256,1024]{1,0:T(8,128)(2,1)}, bf16[256,1024]{1,0:T(8,128)(2,1)}, u32[]{:S(2)}, u32[]{:S(2)}) collective-permute-start(bf16[256,1024]{1,0:T(8,128)(2,1)} %get-tuple-element.283), channel_id=1, source_target_pairs={{0,1},{2,0},{4,2},{6,4},{7,6},{5,7},{3,5},{1,3},{8,10},{10,12},{12... | collective-permute-start | bytes 1572872 | tf_op jit(solution)/shard_map/ppermute | solution.py:593
  340.9 21.7 %collective-permute-start.52 = (bf16[64,4096]{1,0:T(8,128)(2,1)}, bf16[64,4096]{1,0:T(8,128)(2,1)}, u32[]{:S(2)}, u32[]{:S(2)}) collective-permute-start(bf16[64,4096]{1,0:T(8,128)(2,1)} %get-tuple-element.282), channel_id=1, source_target_pairs={{0,2},{2,4},{4,6},{6,7},{7,5},{5,3},{3,1},{1,0},{8,9},{10,8},{12,1... | collective-permute-start | bytes 1572872 | tf_op jit(solution)/shard_map/ppermute | solution.py:593
  341.8 20.7 %collective-permute-start.53 = (bf16[64,4096]{1,0:T(8,128)(2,1)}, bf16[64,4096]{1,0:T(8,128)(2,1)}, u32[]{:S(2)}, u32[]{:S(2)}) collective-permute-start(bf16[64,4096]{1,0:T(8,128)(2,1)} %get-tuple-element.281), channel_id=1, source_target_pairs={{0,1},{2,0},{4,2},{6,4},{7,6},{5,7},{3,5},{1,3},{8,10},{10,12},{12... | collective-permute-start | bytes 1572872 | tf_op jit(solution)/shard_map/ppermute | solution.py:593
  365.5 25.9 %collective-permute-start.55 = (bf16[256,1024]{1,0:T(8,128)(2,1)S(1)}, bf16[256,1024]{1,0:T(8,128)(2,1)}, u32[]{:S(2)}, u32[]{:S(2)}) collective-permute-start(bf16[256,1024]{1,0:T(8,128)(2,1)S(1)} %fusion.22), channel_id=1, source_target_pairs={{0,16},{1,17},{2,18},{3,19},{4,20},{5,21},{6,22},{7,23},{8,24},{9,... | collective-permute-start | bytes 1572872 | tf_op jit(solution)/shard_map/ppermute | solution.py:600
  370.2 21.2 %collective-permute-start.56 = (bf16[64,4096]{1,0:T(8,128)(2,1)}, bf16[64,4096]{1,0:T(8,128)(2,1)S(1)}, u32[]{:S(2)}, u32[]{:S(2)}) collective-permute-start(bf16[64,4096]{1,0:T(8,128)(2,1)} %get-tuple-element.280), channel_id=1, source_target_pairs={{0,2},{2,4},{4,6},{6,7},{7,5},{5,3},{3,1},{1,0},{8,9},{10,8},{12,1... | collective-permute-start | bytes 1572872 | tf_op jit(solution)/shard_map/ppermute | solution.py:593
  371.3 20.1 %collective-permute-start.57 = (bf16[64,4096]{1,0:T(8,128)(2,1)}, bf16[64,4096]{1,0:T(8,128)(2,1)}, u32[]{:S(2)}, u32[]{:S(2)}) collective-permute-start(bf16[64,4096]{1,0:T(8,128)(2,1)} %get-tuple-element.279), channel_id=1, source_target_pairs={{0,1},{2,0},{4,2},{6,4},{7,6},{5,7},{3,5},{1,3},{8,10},{10,12},{12... | collective-permute-start | bytes 1572872 | tf_op jit(solution)/shard_map/ppermute | solution.py:593
  374.5 16.8 %collective-permute-start.58 = (bf16[64,2560]{1,0:T(8,128)(2,1)}, bf16[64,2560]{1,0:T(8,128)(2,1)}, u32[]{:S(2)}, u32[]{:S(2)}) collective-permute-start(bf16[64,2560]{1,0:T(8,128)(2,1)} %get-tuple-element.294), channel_id=1, source_target_pairs={{0,2},{2,4},{4,6},{6,7},{7,5},{5,3},{3,1},{1,0},{8,9},{10,8},{12,1... | collective-permute-start | bytes 983048 | tf_op jit(solution)/shard_map/ppermute | solution.py:593
  375.6 26.8 %collective-permute-start.63 = (bf16[64,2560]{1,0:T(8,128)(2,1)}, bf16[64,2560]{1,0:T(8,128)(2,1)S(1)}, u32[]{:S(2)}, u32[]{:S(2)}) collective-permute-start(bf16[64,2560]{1,0:T(8,128)(2,1)} %get-tuple-element.293), channel_id=1, source_target_pairs={{0,1},{2,0},{4,2},{6,4},{7,6},{5,7},{3,5},{1,3},{8,10},{10,12},{12... | collective-permute-start | bytes 983048 | tf_op jit(solution)/shard_map/ppermute | solution.py:593
  394.2 22.1 %collective-permute-start.59 = (bf16[256,1024]{1,0:T(8,128)(2,1)}, bf16[256,1024]{1,0:T(8,128)(2,1)}, u32[]{:S(2)}, u32[]{:S(2)}) collective-permute-start(bf16[256,1024]{1,0:T(8,128)(2,1)} %add_convert_fusion.3), channel_id=1, source_target_pairs={{0,8},{1,9},{2,10},{3,11},{4,12},{5,13},{6,14},{7,15},{8,0},{9,1},... | collective-permute-start | bytes 1572872 | tf_op jit(solution)/shard_map/ppermute | solution.py:600
  394.2 22.1 %collective-permute-start.64 = (bf16[8,80,1536]{2,1,0:T(8,128)(2,1)}, bf16[8,80,1536]{2,1,0:T(8,128)(2,1)}, u32[]{:S(2)}, u32[]{:S(2)}) collective-permute-start(bf16[8,80,1536]{2,1,0:T(8,128)(2,1)} %bitcast.73), channel_id=1, source_target_pairs={{0,8},{1,9},{2,10},{3,11},{4,12},{5,13},{6,14},{7,15},{8,0},{9,1},... | collective-permute-start | bytes 5898248 | tf_op jit(solution)/shard_map/ppermute | solution.py:600
  398.3 18.0 %collective-permute-start.60 = (bf16[64,4096]{1,0:T(8,128)(2,1)}, bf16[64,4096]{1,0:T(8,128)(2,1)}, u32[]{:S(2)}, u32[]{:S(2)}) collective-permute-start(bf16[64,4096]{1,0:T(8,128)(2,1)} %get-tuple-element.278), channel_id=1, source_target_pairs={{0,2},{2,4},{4,6},{6,7},{7,5},{5,3},{3,1},{1,0},{8,9},{10,8},{12,1... | collective-permute-start | bytes 1572872 | tf_op jit(solution)/shard_map/ppermute | solution.py:593
  399.1 17.2 %collective-permute-start.61 = (bf16[64,4096]{1,0:T(8,128)(2,1)}, bf16[64,4096]{1,0:T(8,128)(2,1)}, u32[]{:S(2)}, u32[]{:S(2)}) collective-permute-start(bf16[64,4096]{1,0:T(8,128)(2,1)} %get-tuple-element.277), channel_id=1, source_target_pairs={{0,1},{2,0},{4,2},{6,4},{7,6},{5,7},{3,5},{1,3},{8,10},{10,12},{12... | collective-permute-start | bytes 1572872 | tf_op jit(solution)/shard_map/ppermute | solution.py:593
  418.1 17.7 %collective-permute-start.65 = (bf16[64,4096]{1,0:T(8,128)(2,1)S(1)}, bf16[64,4096]{1,0:T(8,128)(2,1)S(1)}, u32[]{:S(2)}, u32[]{:S(2)}) collective-permute-start(bf16[64,4096]{1,0:T(8,128)(2,1)S(1)} %fusion.4), channel_id=1, source_target_pairs={{0,16},{1,17},{2,18},{3,19},{4,20},{5,21},{6,22},{7,23},{8,24},{9,... | collective-permute-start | bytes 1572872 | tf_op jit(solution)/shard_map/ppermute | solution.py:600
  424.9 16.8 %collective-permute-start.76 = (bf16[80,1536]{1,0:T(8,128)(2,1)S(1)}, bf16[80,1536]{1,0:T(8,128)(2,1)S(1)}, u32[]{:S(2)}, u32[]{:S(2)}) collective-permute-start(bf16[80,1536]{1,0:T(8,128)(2,1)S(1)} %get-tuple-element.299), channel_id=1, source_target_pairs={{0,1},{2,0},{4,2},{6,4},{7,6},{5,7},{3,5},{1,3},{8,10},{10,12},{12... | collective-permute-start | bytes 737288 | tf_op jit(solution)/shard_map/ppermute | solution.py:593
  (131 other events, 1160.9 us)
Sparse Core Ops, SparseCore 0:
  14.6 86.7 all-gather.2
  104.8 80.5 all-gather.4
